TPU v7x, 32 devices: a whole 2x2x4 slice. The times are simulated.
32 devices in a mesh: fsdp: 32 (over z, y, x, core).
Axes of the slice: x: 2, y: 2, z: 4, core: 2. Of those that a mesh axis runs over, the one named last changes fastest.
Arguments:
- tokens: bfloat16 [4096, 1536], P('fsdp'), may hold values from -6 to 6
- segment: int32 [4096], P('fsdp'), may hold values from -1 to 3, as said below
- position: int32 [4096], P('fsdp'), may hold values from 0 to 127, as said below
- first_gain: bfloat16 [1536], P('fsdp'), may hold values from 0.25 to 1.75
- query_weight: bfloat16 [1536, 1536], P('fsdp'), may hold values from -0.15625 to 0.15625
- query_bias: bfloat16 [1536], P('fsdp'), may hold values from -3 to 3
- key_weight: bfloat16 [1536, 256], P('fsdp'), may hold values from -0.15625 to 0.15625
- key_bias: bfloat16 [256], P('fsdp'), may hold values from -3 to 3
- value_weight: bfloat16 [1536, 256], P('fsdp'), may hold values from -0.15625 to 0.15625
- value_bias: bfloat16 [256], P('fsdp'), may hold values from -3 to 3
- out_weight: bfloat16 [1536, 1536], P('fsdp'), may hold values from -1.25 to 1.25
- second_gain: bfloat16 [1536], P('fsdp'), may hold values from 0.25 to 1.75
- gate_weight: bfloat16 [1536, 8960], P('fsdp'), may hold values from -0.15625 to 0.15625
- up_weight: bfloat16 [1536, 8960], P('fsdp'), may hold values from -0.15625 to 0.15625
- down_weight: bfloat16 [1536, 8960], P('fsdp'), may hold values from -0.0625 to 0.0625
- cotangent: bfloat16 [4096, 1536], P('fsdp'), may hold values from -6 to 6
Outputs:
- block_output: bfloat16 [4096, 1536], P('fsdp')
- input_gradient: bfloat16 [4096, 1536], P('fsdp')
- first_gain_gradient: float32 [1536], P('fsdp')
- query_weight_gradient: float32 [1536, 1536], P('fsdp')
- query_bias_gradient: float32 [1536], P('fsdp')
- key_weight_gradient: float32 [1536, 256], P('fsdp')
- key_bias_gradient: float32 [256], replicated
- value_weight_gradient: float32 [1536, 256], P('fsdp')
- value_bias_gradient: float32 [256], P('fsdp')
- out_weight_gradient: float32 [1536, 1536], P('fsdp')
- second_gain_gradient: float32 [1536], P('fsdp')
- gate_weight_gradient: float32 [1536, 8960], P('fsdp')
- up_weight_gradient: float32 [1536, 8960], P('fsdp')
- down_weight_gradient: float32 [1536, 8960], P('fsdp')
Inputs may be any that keep to these rules, and one draw needn't show every extreme that they name: `segment`: within a block of 128 slots the live tokens come first: each of at most 4 sequences stands in one run of slots and carries one number, numbers never fall along a block, and -1 marks the padding after the last live token; in every draw some block holds a single sequence of 128 tokens. `position`: A live token's offset within its sequence, counted from 0; a padding slot's offset counted from 0 at the block's first padding slot.
All inputs are finite; a program needn't handle non-finite values.
Results may differ from a plain program's by a relative error of at most 0.025.
Values may be sent and summed in bfloat16 or wider, within the bound.
A program may use at most 640 MiB of HBM per device.

v0:
```python
import math

import jax
import jax.numpy as jnp
from jax import lax
from jax.sharding import PartitionSpec as P

H = 12
KV = 2
HD = 128


EPSILON = 1e-06
ROPE_BASE = 1000000.0


def tables(position):
    freq_index = jnp.arange(HD // 2).astype(jnp.float32)
    frequency = jnp.exp(freq_index * (-2.0 * math.log(ROPE_BASE) / HD))
    angles = position.astype(jnp.float32)[:, None] * frequency[None, :]
    angles = jnp.concatenate([angles, angles], axis=-1)
    return (jnp.cos(angles)[:, None, :], jnp.sin(angles)[:, None, :])


def rotary(values, cosine_table, sine_table):
    middle = values.shape[-1] // 2
    turned = jnp.concatenate([-values[..., middle:], values[..., :middle]], axis=-1)
    return values * cosine_table + turned * sine_table


def rotary_back(gradient, cosine_table, sine_table):
    middle = gradient.shape[-1] // 2
    weighted = gradient * sine_table
    return gradient * cosine_table + jnp.concatenate(
        [weighted[..., middle:], -weighted[..., :middle]], axis=-1
    )


def norm_back(gradient, values, row_scale, gain_vector):
    weighted = gradient * gain_vector.astype(jnp.float32)
    return row_scale * weighted - values * row_scale**3 * jnp.mean(
        weighted * values, axis=-1, keepdims=True
    )


def masked_scores(queries, key_rows, visible, factor):
    scores = (
        jnp.einsum("qkgd,skd->kgqs", queries, key_rows, preferred_element_type=jnp.float32) * factor
    )
    return jnp.where(visible, scores, -jnp.inf)


def fold_owner(received, count):
    return jnp.sum(
        received.reshape((count, received.shape[0] // count) + received.shape[1:]), axis=0
    )


def reduce_feed(term):
    received = lax.all_to_all(term, "fsdp", split_axis=0, concat_axis=0, tiled=True)
    return fold_owner(received, lax.axis_size("fsdp"))


def body(
    tokens,
    segment,
    position,
    first_gain,
    query_weight,
    query_bias,
    key_weight,
    key_bias,
    value_weight,
    value_bias,
    out_weight,
    second_gain,
    gate_weight,
    up_weight,
    down_weight,
    cotangent,
):
    attention_full = (
        lax.all_gather(first_gain, "fsdp", axis=0, tiled=True),
        lax.all_gather(query_weight, "fsdp", axis=0, tiled=True),
        lax.all_gather(query_bias, "fsdp", axis=0, tiled=True),
        lax.all_gather(key_weight, "fsdp", axis=0, tiled=True),
        lax.all_gather(key_bias, "fsdp", axis=0, tiled=True),
        lax.all_gather(value_weight, "fsdp", axis=0, tiled=True),
        lax.all_gather(value_bias, "fsdp", axis=0, tiled=True),
        lax.all_gather(out_weight, "fsdp", axis=0, tiled=True),
    )
    (
        gain_one,
        weight_query,
        bias_query,
        weight_key,
        bias_key,
        weight_value,
        bias_value,
        weight_out,
    ) = attention_full
    length = tokens.shape[0]
    groups = H // KV
    factor = 1.0 / math.sqrt(HD)
    live_rows = (segment >= 0).astype(jnp.float32)[:, None]
    slot_order = jnp.arange(length)
    visible = (segment[:, None] == segment[None, :]) & (slot_order[None, :] <= slot_order[:, None])
    cosine_table, sine_table = tables(position)
    token_float = tokens.astype(jnp.float32)
    scale_one = lax.rsqrt(jnp.mean(token_float * token_float, axis=-1, keepdims=True) + EPSILON)
    normed_one = (token_float * scale_one * gain_one.astype(jnp.float32)).astype(jnp.bfloat16)
    query_pre = jnp.dot(
        normed_one, weight_query, preferred_element_type=jnp.float32
    ) + bias_query.astype(jnp.float32)
    key_pre = jnp.dot(normed_one, weight_key, preferred_element_type=jnp.float32) + bias_key.astype(
        jnp.float32
    )
    value_pre = jnp.dot(
        normed_one, weight_value, preferred_element_type=jnp.float32
    ) + bias_value.astype(jnp.float32)
    queries = rotary(query_pre.reshape(length, H, HD), cosine_table, sine_table).astype(
        jnp.bfloat16
    )
    queries = queries.reshape(length, KV, groups, HD)
    key_rows = rotary(key_pre.reshape(length, KV, HD), cosine_table, sine_table).astype(
        jnp.bfloat16
    )
    value_rows = value_pre.astype(jnp.bfloat16).reshape(length, KV, HD)
    scores = masked_scores(queries, key_rows, visible, factor)
    row_peak = jnp.max(scores, axis=-1, keepdims=True)
    row_total = jnp.sum(jnp.exp(scores - row_peak), axis=-1, keepdims=True)
    log_total = row_peak + jnp.log(row_total)
    attention = jnp.exp(scores - log_total).astype(jnp.bfloat16)
    mixed_heads = jnp.einsum(
        "kgqs,skd->qkgd", attention, value_rows, preferred_element_type=jnp.float32
    )
    mixed_heads = mixed_heads.reshape(length, H * HD).astype(jnp.bfloat16)
    branch = jnp.einsum("td,ed->te", mixed_heads, weight_out, preferred_element_type=jnp.float32)
    hidden_state = token_float + branch
    feed_full = (
        lax.all_gather(second_gain, "fsdp", axis=0, tiled=True),
        lax.all_gather(gate_weight, "fsdp", axis=0, tiled=True),
        lax.all_gather(up_weight, "fsdp", axis=0, tiled=True),
        lax.all_gather(down_weight, "fsdp", axis=0, tiled=True),
    )
    gain_two, weight_gate, weight_up, weight_down = feed_full
    scale_two = lax.rsqrt(jnp.mean(hidden_state * hidden_state, axis=-1, keepdims=True) + EPSILON)
    normed_two = (hidden_state * scale_two * gain_two.astype(jnp.float32)).astype(jnp.bfloat16)
    gate_value = jnp.dot(normed_two, weight_gate, preferred_element_type=jnp.float32)
    up_value = jnp.dot(normed_two, weight_up, preferred_element_type=jnp.float32)
    activated = (jax.nn.silu(gate_value) * up_value).astype(jnp.bfloat16)
    feed_out = jnp.einsum("tf,ef->te", activated, weight_down, preferred_element_type=jnp.float32)
    block_output = (live_rows * (hidden_state + feed_out)).astype(jnp.bfloat16)
    feed_back = (
        lax.all_gather(second_gain, "fsdp", axis=0, tiled=True),
        lax.all_gather(gate_weight, "fsdp", axis=0, tiled=True),
        lax.all_gather(up_weight, "fsdp", axis=0, tiled=True),
        lax.all_gather(down_weight, "fsdp", axis=0, tiled=True),
    )
    attention_back = (
        lax.all_gather(first_gain, "fsdp", axis=0, tiled=True),
        lax.all_gather(query_weight, "fsdp", axis=0, tiled=True),
        lax.all_gather(query_bias, "fsdp", axis=0, tiled=True),
        lax.all_gather(key_weight, "fsdp", axis=0, tiled=True),
        lax.all_gather(key_bias, "fsdp", axis=0, tiled=True),
        lax.all_gather(value_weight, "fsdp", axis=0, tiled=True),
        lax.all_gather(value_bias, "fsdp", axis=0, tiled=True),
        lax.all_gather(out_weight, "fsdp", axis=0, tiled=True),
    )
    gain_two_back, gate_back, up_back, down_back = feed_back
    gain_one_back, query_back, unused_qb, key_back, unused_kb, value_back, unused_vb, out_back = (
        attention_back
    )
    upstream = cotangent.astype(jnp.float32) * live_rows
    upstream_low = upstream.astype(jnp.bfloat16)
    down_sum = reduce_feed(
        jnp.einsum("te,tf->ef", upstream_low, activated, preferred_element_type=jnp.float32)
    )
    act_grad = jnp.dot(upstream_low, down_back, preferred_element_type=jnp.float32)
    sigmoid_gate = jax.nn.sigmoid(gate_value)
    gate_grad = (
        act_grad * up_value * sigmoid_gate * (1.0 + gate_value * (1.0 - sigmoid_gate))
    ).astype(jnp.bfloat16)
    up_grad = (act_grad * gate_value * sigmoid_gate).astype(jnp.bfloat16)
    gate_sum = reduce_feed(
        jnp.einsum("td,tf->df", normed_two, gate_grad, preferred_element_type=jnp.float32)
    )
    up_sum = reduce_feed(
        jnp.einsum("td,tf->df", normed_two, up_grad, preferred_element_type=jnp.float32)
    )
    normed_two_grad = jnp.einsum(
        "tf,df->td", gate_grad, gate_back, preferred_element_type=jnp.float32
    ) + jnp.einsum("tf,df->td", up_grad, up_back, preferred_element_type=jnp.float32)
    gain_two_term = jnp.sum(normed_two_grad * hidden_state * scale_two, axis=0)
    hidden_grad = upstream + norm_back(normed_two_grad, hidden_state, scale_two, gain_two_back)
    branch_grad = hidden_grad.astype(jnp.bfloat16)
    out_term = jnp.einsum("te,td->ed", branch_grad, mixed_heads, preferred_element_type=jnp.float32)
    mixed_grad = jnp.dot(branch_grad, out_back, preferred_element_type=jnp.float32).astype(
        jnp.bfloat16
    )
    mixed_grad = mixed_grad.reshape(length, KV, groups, HD)
    probs_again = jnp.exp(masked_scores(queries, key_rows, visible, factor) - log_total)
    prob_grad = jnp.einsum(
        "qkgd,skd->kgqs", mixed_grad, value_rows, preferred_element_type=jnp.float32
    )
    value_grad = jnp.einsum(
        "kgqs,qkgd->skd",
        probs_again.astype(jnp.bfloat16),
        mixed_grad,
        preferred_element_type=jnp.float32,
    )
    score_grad = probs_again * (
        prob_grad - jnp.sum(probs_again * prob_grad, axis=-1, keepdims=True)
    )
    score_grad = score_grad.astype(jnp.bfloat16)
    query_grad = (
        jnp.einsum("kgqs,skd->qkgd", score_grad, key_rows, preferred_element_type=jnp.float32)
        * factor
    )
    key_grad = (
        jnp.einsum("kgqs,qkgd->skd", score_grad, queries, preferred_element_type=jnp.float32)
        * factor
    )
    query_low = rotary_back(query_grad.reshape(length, H, HD), cosine_table, sine_table)
    query_low = query_low.reshape(length, H * HD).astype(jnp.bfloat16)
    key_low = (
        rotary_back(key_grad, cosine_table, sine_table)
        .reshape(length, KV * HD)
        .astype(jnp.bfloat16)
    )
    value_low = value_grad.reshape(length, KV * HD).astype(jnp.bfloat16)
    query_term = jnp.einsum("td,te->de", normed_one, query_low, preferred_element_type=jnp.float32)
    key_term = jnp.einsum("td,te->de", normed_one, key_low, preferred_element_type=jnp.float32)
    value_term = jnp.einsum("td,te->de", normed_one, value_low, preferred_element_type=jnp.float32)
    query_bias_term = jnp.sum(query_low, axis=0, dtype=jnp.float32)
    key_bias_term = jnp.sum(key_low, axis=0, dtype=jnp.float32)
    value_bias_term = jnp.sum(value_low, axis=0, dtype=jnp.float32)
    normed_one_grad = (
        jnp.einsum("te,de->td", query_low, query_back, preferred_element_type=jnp.float32)
        + jnp.einsum("te,de->td", key_low, key_back, preferred_element_type=jnp.float32)
        + jnp.einsum("te,de->td", value_low, value_back, preferred_element_type=jnp.float32)
    )
    gain_one_term = jnp.sum(normed_one_grad * token_float * scale_one, axis=0)
    token_grad = hidden_grad + norm_back(normed_one_grad, token_float, scale_one, gain_one_back)
    count = lax.axis_size("fsdp")
    key_bias_every = jnp.tile(key_bias_term, count)
    received = (
        lax.all_to_all(gain_one_term, "fsdp", split_axis=0, concat_axis=0, tiled=True),
        lax.all_to_all(query_term, "fsdp", split_axis=0, concat_axis=0, tiled=True),
        lax.all_to_all(query_bias_term, "fsdp", split_axis=0, concat_axis=0, tiled=True),
        lax.all_to_all(key_term, "fsdp", split_axis=0, concat_axis=0, tiled=True),
        lax.all_to_all(key_bias_every, "fsdp", split_axis=0, concat_axis=0, tiled=True),
        lax.all_to_all(value_term, "fsdp", split_axis=0, concat_axis=0, tiled=True),
        lax.all_to_all(value_bias_term, "fsdp", split_axis=0, concat_axis=0, tiled=True),
        lax.all_to_all(out_term, "fsdp", split_axis=0, concat_axis=0, tiled=True),
        lax.all_to_all(gain_two_term, "fsdp", split_axis=0, concat_axis=0, tiled=True),
    )
    attention_sums = [fold_owner(member, count) for member in received]
    return (
        block_output,
        token_grad.astype(jnp.bfloat16),
        attention_sums[0],
        attention_sums[1],
        attention_sums[2],
        attention_sums[3],
        attention_sums[4],
        attention_sums[5],
        attention_sums[6],
        attention_sums[7],
        attention_sums[8],
        gate_sum,
        up_sum,
        down_sum,
    )


def solution(mesh):
    return jax.shard_map(
        body,
        mesh=mesh,
        in_specs=(
            P("fsdp", None),
            P("fsdp"),
            P("fsdp"),
            P("fsdp"),
            P("fsdp", None),
            P("fsdp"),
            P("fsdp", None),
            P("fsdp"),
            P("fsdp", None),
            P("fsdp"),
            P("fsdp", None),
            P("fsdp"),
            P("fsdp", None),
            P("fsdp", None),
            P("fsdp", None),
            P("fsdp", None),
        ),
        out_specs=(
            P("fsdp", None),
            P("fsdp", None),
            P("fsdp"),
            P("fsdp", None),
            P("fsdp"),
            P("fsdp", None),
            P(),
            P("fsdp", None),
            P("fsdp"),
            P("fsdp", None),
            P("fsdp"),
            P("fsdp", None),
            P("fsdp", None),
            P("fsdp", None),
        ),
        check_vma=False,
    )
```

profile of v0, /device:TPU:0, one launch (start us, length us, event | category | flops | bytes accessed | tf_op | source)
XLA Modules:
  0.0 5013.7 jit_solution(3570101253077445984)
XLA Ops:
  15.5 42.3 all-reduce.5
  59.5 43.2 all_gather.48
  105.1 41.2 all_gather.46
  158.1 158.0 %all-gather.12.cloned.1.call-done = bf16[1536,8960]{1,0:T(8,128)(2,1)} async-done(((bf16[48,8960]{1,0:T(8,128)(2,1)}), bf16[1536,8960]{1,0:T(8,128)(2,1)}) %all-gather.12.cloned.1.call-update) | async-done | bytes 27525136 | tf_op jit(solution)/shard_map/all_gather | solution.py:143
  316.2 14.9 fusion.49
  331.0 152.0 %all-gather.10.cloned.1.call-done = bf16[1536,8960]{1,0:T(8,128)(2,1)} async-done(((bf16[48,8960]{1,0:T(8,128)(2,1)}), bf16[1536,8960]{1,0:T(8,128)(2,1)}) %all-gather.10.cloned.1.call-update) | async-done | bytes 27525136 | tf_op jit(solution)/shard_map/all_gather | solution.py:142
  483.1 14.8 fusion.48
  497.8 152.1 %all-gather.14.cloned.1.call-done = bf16[1536,8960]{1,0:T(8,128)(2,1)} async-done(((bf16[48,8960]{1,0:T(8,128)(2,1)}), bf16[1536,8960]{1,0:T(8,128)(2,1)}) %all-gather.14.cloned.1.call-update) | async-done | bytes 27525136 | tf_op jit(solution)/shard_map/all_gather | solution.py:144
  650.0 17.5 multiply_convert_fusion
  667.5 14.6 fusion.50
  682.1 16.0 multiply_reduce_fusion
  720.4 5.8 all-to-all-start.8
  736.9 6.4 all-to-all-done.2
  757.7 5.7 all-to-all-done.4
  767.6 36.3 all-to-all-done.5
  807.6 5.0 fusion.52
  812.7 32.7 all-to-all-done.3
  849.5 5.0 fusion.55
  854.5 203.9 %all-to-all-done.1 = f32[32,48,1536]{2,1,0:T(8,128)} async-done(((f32[32,48,1536]{2,1,0:T(8,128)}), f32[32,48,1536]{2,1,0:T(8,128)}, u32[]{:S(2)}, u32[]{:S(2)}) %all-to-all-start.1) | async-done | bytes 9437216 | tf_op jit(solution)/shard_map/all_to_all | solution.py:249
  1062.1 21.2 fusion.25
  1083.3 188.0 %all-to-all-done.7 = f32[32,48,1536]{2,1,0:T(8,128)} async-done(((f32[32,48,1536]{2,1,0:T(8,128)}), f32[32,48,1536]{2,1,0:T(8,128)}, u32[]{:S(2)}, u32[]{:S(2)}) %all-to-all-start.7) | async-done | bytes 9437216 | tf_op jit(solution)/shard_map/all_to_all | solution.py:255
  1271.4 5.1 all-to-all-start.11
  1276.5 21.2 fusion.57
  1297.6 1212.7 %all-to-all-done.11 = f32[32,48,8960]{2,1,0:T(8,128)} async-done(((f32[32,48,8960]{2,1,0:T(8,128)}), f32[32,48,8960]{2,1,0:T(8,128)}, u32[]{:S(2)}, u32[]{:S(2)}) %all-to-all-start.11) | async-done | bytes 55050272 | tf_op jit(solution)/shard_map/all_to_all | solution.py:60
  2515.3 21.2 fusion.56
  2536.4 1212.8 %all-to-all-done.10 = f32[32,48,8960]{2,1,0:T(8,128)} async-done(((f32[32,48,8960]{2,1,0:T(8,128)}), f32[32,48,8960]{2,1,0:T(8,128)}, u32[]{:S(2)}, u32[]{:S(2)}) %all-to-all-start.10) | async-done | bytes 55050272 | tf_op jit(solution)/shard_map/all_to_all | solution.py:60
  3749.2 5.3 all-to-all-start.9
  3754.5 14.7 fusion.1
  3787.0 18.6 reduce_sum.229
  3805.6 18.6 reduce_sum.228
  3824.1 1164.2 %all-to-all-done.9 = f32[32,48,8960]{2,1,0:T(8,128)} async-done(((f32[32,48,8960]{2,1,0:T(8,128)}), f32[32,48,8960]{2,1,0:T(8,128)}, u32[]{:S(2)}, u32[]{:S(2)}) %all-to-all-start.9) | async-done | bytes 55050272 | tf_op jit(solution)/shard_map/all_to_all | solution.py:60
  4988.4 18.6 reduce_sum.227
  (206 shorter events, 109.4 us)
Async XLA Ops:
  7.2 139.9 %copy-start.6 = (bf16[128,1536]{1,0:T(8,128)(2,1)S(1)}, bf16[128,1536]{1,0:T(8,128)(2,1)}, u32[]{:S(2)}) copy-start(bf16[128,1536]{1,0:T(8,128)(2,1)} %param.16) | copy-start | bytes 1179652
  7.2 97.9 %copy-start.38 = (bf16[48,256]{1,0:T(8,128)(2,1)S(1)}, bf16[48,256]{1,0:T(8,128)(2,1)}, u32[]{:S(2)}) copy-start(bf16[48,256]{1,0:T(8,128)(2,1)} %param.24) | copy-start | bytes 73732
  7.2 141.3 %copy-start.46 = (s32[128]{0:T(128)S(1)}, s32[128]{0:T(128)}, u32[]{:S(2)}) copy-start(s32[128]{0:T(128)} %param.17) | copy-start | bytes 1540
  7.2 141.5 %all-gather.6.cloned.1.call-start = ((), (), s32[]{:S(2)}) async-start(), calls=%async_computation.12 | async-start | bytes 4866048 | tf_op jit(solution)/shard_map/all_gather | solution.py:84
  7.9 145.3 %all-gather.8.cloned.1.call-start = ((), (), s32[]{:S(2)}) async-start(), calls=%async_computation.13 | async-start | bytes 4866048 | tf_op jit(solution)/shard_map/all_gather | solution.py:90
  8.7 307.5 %all-gather.12.cloned.1.call-start = ((), (), s32[]{:S(2)}) async-start(), calls=%async_computation.15 | async-start | bytes 28385280 | tf_op jit(solution)/shard_map/all_gather | solution.py:143
  9.4 473.6 %all-gather.10.cloned.1.call-start = ((), (), s32[]{:S(2)}) async-start(), calls=%async_computation.14 | async-start | bytes 28385280 | tf_op jit(solution)/shard_map/all_gather | solution.py:142
  10.0 640.0 %all-gather.14.cloned.1.call-start = ((), (), s32[]{:S(2)}) async-start(), calls=%async_computation.16 | async-start | bytes 28385280 | tf_op jit(solution)/shard_map/all_gather | solution.py:144
  57.8 100.2 %copy-start.27 = (f32[1536]{0:T(1024)}, f32[1536]{0:T(1024)S(1)}, u32[]{:S(2)}) copy-start(f32[1536]{0:T(1024)S(1)} %convert_element_type.161) | copy-start | bytes 18436
  59.5 92.4 %copy-start.42 = (f32[128]{0:T(128)}, f32[128]{0:T(128)S(1)}, u32[]{:S(2)}) copy-start(f32[128]{0:T(128)S(1)} %get-tuple-element.47) | copy-start | bytes 1540
  148.5 501.4 %copy-start.39 = (f32[128]{0:T(128)}, f32[128]{0:T(128)S(1)}, u32[]{:S(2)}) copy-start(f32[128]{0:T(128)S(1)} %compare_convert_fusion) | copy-start | bytes 1540
  157.4 540.7 %copy-start = (f32[128,1536]{1,0:T(8,128)}, f32[128,1536]{1,0:T(8,128)S(1)}, u32[]{:S(2)}) copy-start(f32[128,1536]{1,0:T(8,128)S(1)} %get-tuple-element.53) | copy-start | bytes 2359300
  158.0 158.1 %copy-start.44 = (f32[128]{0:T(128)}, f32[128]{0:T(128)S(1)}, u32[]{:S(2)}) copy-start(f32[128]{0:T(128)S(1)} %get-tuple-element.49) | copy-start | bytes 1540
  331.0 318.9 %copy-start.16 = (bf16[128,1536]{1,0:T(8,128)(2,1)S(1)}, bf16[128,1536]{1,0:T(8,128)(2,1)}, u32[]{:S(2)}) copy-start(bf16[128,1536]{1,0:T(8,128)(2,1)} %param.31) | copy-start | bytes 1179652
  707.8 12.6 all-to-all-start.6
  720.4 12.8 all-to-all-start.8
  733.2 10.1 all-to-all-start.2
  743.3 9.6 all-to-all-start
  752.9 51.0 %copy-start.35 = (f32[32,48,1]{1,2,0:T(1,128)}, f32[32,48,1]{1,2,0:T(1,128)S(1)}, u32[]{:S(2)}) copy-start(f32[32,48,1]{1,2,0:T(1,128)S(1)} %all-to-all-done) | copy-start | bytes 18436
  753.6 9.8 all-to-all-start.4
  757.7 50.0 copy-start.18
  763.4 49.3 copy-start.29
  763.4 40.5 all-to-all-start.5
  803.9 41.4 all-to-all-start.3
  845.3 213.1 %all-to-all-start.1 = ((f32[32,48,1536]{2,1,0:T(8,128)}), f32[32,48,1536]{2,1,0:T(8,128)}, u32[]{:S(2)}, u32[]{:S(2)}) async-start(f32[32,48,1536]{2,1,0:T(8,128)} %fusion.52), calls=%async_computation.1 | async-start | bytes 18874368 | tf_op jit(solution)/shard_map/all_to_all | solution.py:249
  854.5 207.6 %copy-start.3 = (bf16[128,8960]{1,0:T(8,128)(2,1)S(1)}, bf16[128,8960]{1,0:T(8,128)(2,1)}, u32[]{:S(2)}) copy-start(bf16[128,8960]{1,0:T(8,128)(2,1)} %get-tuple-element.29) | copy-start | bytes 6881284
  854.5 207.6 %copy-start.17 = (bf16[128,1536]{1,0:T(8,128)(2,1)S(1)}, bf16[128,1536]{1,0:T(8,128)(2,1)}, u32[]{:S(2)}) copy-start(bf16[128,1536]{1,0:T(8,128)(2,1)} %param.31) | copy-start | bytes 1179652
  854.5 207.6 %copy-start.41 = (f32[128]{0:T(128)S(1)}, f32[128]{0:T(128)}, u32[]{:S(2)}) copy-start(f32[128]{0:T(128)} %copy-done.39) | copy-start | bytes 1540
  1058.4 213.0 %all-to-all-start.7 = ((f32[32,48,1536]{2,1,0:T(8,128)}), f32[32,48,1536]{2,1,0:T(8,128)}, u32[]{:S(2)}, u32[]{:S(2)}) async-start(f32[32,48,1536]{2,1,0:T(8,128)} %fusion.55), calls=%async_computation.7 | async-start | bytes 18874368 | tf_op jit(solution)/shard_map/all_to_all | solution.py:255
  1271.4 1239.0 %all-to-all-start.11 = ((f32[32,48,8960]{2,1,0:T(8,128)}), f32[32,48,8960]{2,1,0:T(8,128)}, u32[]{:S(2)}, u32[]{:S(2)}) async-start(f32[32,48,8960]{2,1,0:T(8,128)} %bitcast.129), calls=%async_computation.11 | async-start | bytes 110100480 | tf_op jit(solution)/shard_map/all_to_all | solution.py:60
  2510.3 1238.8 %all-to-all-start.10 = ((f32[32,48,8960]{2,1,0:T(8,128)}), f32[32,48,8960]{2,1,0:T(8,128)}, u32[]{:S(2)}, u32[]{:S(2)}) async-start(f32[32,48,8960]{2,1,0:T(8,128)} %bitcast.128), calls=%async_computation.10 | async-start | bytes 110100480 | tf_op jit(solution)/shard_map/all_to_all | solution.py:60
  3749.2 1239.2 %all-to-all-start.9 = ((f32[32,48,8960]{2,1,0:T(8,128)}), f32[32,48,8960]{2,1,0:T(8,128)}, u32[]{:S(2)}, u32[]{:S(2)}) async-start(f32[32,48,8960]{2,1,0:T(8,128)} %bitcast.127), calls=%async_computation.9 | async-start | bytes 110100480 | tf_op jit(solution)/shard_map/all_to_all | solution.py:60
  (36 other events, 394.9 us)
Sparse Core Ops, SparseCore 0:
  10.9 68.7 all-gather.5
  82.6 64.7 all-gather.7
  150.3 165.8 all-gather.11
  318.9 164.0 all-gather.9
  485.8 164.0 all-gather.13
where the time goes:
time: 5020 us; the launch traced here: 5010 us
  waiting for transfers between devices  4540 us (90%)
  matrix products  190 us (4%)
  blocking collectives  127 us (3%)
  other arithmetic  86.8 us (2%)
    all_to_all x3, waiting for transfers between devices, reduce_feed(): lax.all_to_all(term, 'fsdp', split_axis=0, concat_axis=0, tiled=True)  3590 us
    all_to_all x1, waiting for transfers between devices, body(): lax.all_to_all(query_term, 'fsdp', split_axis=0, concat_axis=0, tiled=True)  204 us
    all_to_all x1, waiting for transfers between devices, body(): lax.all_to_all(out_term, 'fsdp', split_axis=0, concat_axis=0, tiled=True)  188 us
    all_gather x1, waiting for transfers between devices, body(): lax.all_gather(up_weight, 'fsdp', axis=0, tiled=True)  158 us
    all_gather x1, waiting for transfers between devices, body(): lax.all_gather(down_weight, 'fsdp', axis=0, tiled=True)  152 us
    all_gather x1, waiting for transfers between devices, body(): lax.all_gather(gate_weight, 'fsdp', axis=0, tiled=True)  152 us
  transfers between devices with their start and end apart: 17, of which 14 were waited for; matrix products, arithmetic and copies ran while one was open for 4% of the time, Pallas kernels for 0%

commit v1 on v0

v1 whole, which is shorter than its diff:
```python
import math

import jax
import jax.numpy as jnp
from jax import lax
from jax.sharding import PartitionSpec as P

H = 12
KV = 2
HD = 128
GROUP = 8

EPSILON = 1e-06
ROPE_BASE = 1000000.0
AXIS = "fsdp"
F32 = jnp.float32
BF16 = jnp.bfloat16


def tables(position):
    freq_index = jnp.arange(HD // 2).astype(F32)
    frequency = jnp.exp(freq_index * (-2.0 * math.log(ROPE_BASE) / HD))
    angles = position.astype(F32)[:, None] * frequency[None, :]
    angles = jnp.concatenate([angles, angles], axis=-1)
    return (jnp.cos(angles)[:, None, :], jnp.sin(angles)[:, None, :])


def rotary(values, cosine_table, sine_table):
    middle = values.shape[-1] // 2
    turned = jnp.concatenate([-values[..., middle:], values[..., :middle]], axis=-1)
    return values * cosine_table + turned * sine_table


def rotary_back(gradient, cosine_table, sine_table):
    middle = gradient.shape[-1] // 2
    weighted = gradient * sine_table
    return gradient * cosine_table + jnp.concatenate(
        [weighted[..., middle:], -weighted[..., :middle]], axis=-1
    )


def norm_back(weighted, values, row_scale):
    return row_scale * weighted - values * row_scale**3 * jnp.mean(
        weighted * values, axis=-1, keepdims=True
    )


def dot(left, right, dims):
    return lax.dot_general(left, right, ((dims[:1], dims[1:]), ((), ())), preferred_element_type=F32)


def groups_of(count):
    plane = count // GROUP
    lines = GROUP // 2
    token = [[(z * plane + p) * 2 + c for z in range(lines) for c in range(2)] for p in range(plane)]
    other = [[(z * plane + p) * 2 + c for p in range(plane)] for z in range(lines) for c in range(2)]
    return token, other


def array_body(
    tokens,
    segment,
    position,
    first_gain,
    query_weight,
    query_bias,
    key_weight,
    key_bias,
    value_weight,
    value_bias,
    out_weight,
    second_gain,
    gate_weight,
    up_weight,
    down_weight,
    cotangent,
):
    count = lax.axis_size(AXIS)
    me = lax.axis_index(AXIS)
    token_groups, plane_groups = groups_of(count)
    plane = count // GROUP
    lines = GROUP // 2
    rows, width = query_weight.shape
    hidden = gate_weight.shape[1]
    shard = hidden // GROUP
    key_width = key_weight.shape[1]
    length = tokens.shape[0]
    heads_per_key = H // KV
    factor = 1.0 / math.sqrt(HD)

    gain_one = first_gain.astype(F32)[:, None]
    gain_two = second_gain.astype(F32)[:, None]

    def scaled(weight, gain):
        return (weight.astype(F32) * gain).astype(BF16)

    attention_own = jnp.concatenate(
        [scaled(query_weight, gain_one), scaled(key_weight, gain_one), scaled(value_weight, gain_one), out_weight], axis=1
    )
    attention_all = lax.all_gather(attention_own, AXIS, axis=0, tiled=True)
    input_width = width + 2 * key_width
    weight_input = attention_all[:, :input_width]
    weight_out = attention_all[:, input_width:]
    biases = lax.all_gather(jnp.concatenate([query_bias, key_bias, value_bias]), AXIS, axis=0, tiled=False).astype(F32)
    cut = (rows, rows + key_bias.shape[0])
    bias_input = jnp.concatenate(
        [biases[:, : cut[0]].reshape(-1), biases[:, cut[0] : cut[1]].reshape(-1), biases[:, cut[1] :].reshape(-1)]
    )

    def spread(weight):
        pieces = weight.reshape(rows, GROUP, shard).transpose(1, 0, 2)
        got = lax.all_to_all(pieces, AXIS, split_axis=0, concat_axis=0, tiled=True, axis_index_groups=token_groups)
        full = lax.all_gather(got, AXIS, axis=0, tiled=False, axis_index_groups=plane_groups)
        full = full.reshape(plane, lines, 2, rows, shard).transpose(1, 0, 2, 3, 4)
        return full.reshape(count * rows, shard)

    weight_gate = spread(scaled(gate_weight, gain_two))
    weight_up = spread(scaled(up_weight, gain_two))
    weight_down = spread(down_weight)

    live_rows = (segment >= 0).astype(F32)[:, None]
    slot_order = jnp.arange(length)
    visible = (segment[:, None] == segment[None, :]) & (slot_order[None, :] <= slot_order[:, None])
    cosine_table, sine_table = tables(position)
    token_float = tokens.astype(F32)
    scale_one = lax.rsqrt(jnp.mean(token_float * token_float, axis=-1, keepdims=True) + EPSILON)
    normed_one = (token_float * scale_one).astype(BF16)
    projected = dot(normed_one, weight_input, (1, 0)) + bias_input
    queries = rotary(projected[:, :width].reshape(length, H, HD), cosine_table, sine_table).astype(BF16)
    queries = queries.reshape(length, KV, heads_per_key, HD)
    key_rows = rotary(
        projected[:, width : width + key_width].reshape(length, KV, HD), cosine_table, sine_table
    ).astype(BF16)
    value_rows = projected[:, width + key_width :].astype(BF16).reshape(length, KV, HD)
    scores = jnp.einsum("qkgd,skd->kgqs", queries, key_rows, preferred_element_type=F32) * factor
    probs = jax.nn.softmax(jnp.where(visible, scores, -jnp.inf), axis=-1)
    probs_low = probs.astype(BF16)
    mixed_heads = jnp.einsum("kgqs,skd->qkgd", probs_low, value_rows, preferred_element_type=F32)
    mixed_heads = mixed_heads.reshape(length, H * HD).astype(BF16)
    hidden_state = token_float + dot(mixed_heads, weight_out, (1, 1))
    scale_two = lax.rsqrt(jnp.mean(hidden_state * hidden_state, axis=-1, keepdims=True) + EPSILON)
    normed_two = (hidden_state * scale_two).astype(BF16)
    upstream = cotangent.astype(F32) * live_rows
    group_tokens = lax.all_gather(normed_two, AXIS, axis=0, tiled=True, axis_index_groups=token_groups)
    group_upstream = lax.all_gather(
        upstream.astype(BF16), AXIS, axis=0, tiled=True, axis_index_groups=token_groups
    )

    gate_value = dot(group_tokens, weight_gate, (1, 0))
    up_value = dot(group_tokens, weight_up, (1, 0))
    sigmoid_gate = jax.nn.sigmoid(gate_value)
    activated = (gate_value * sigmoid_gate * up_value).astype(BF16)
    act_grad = dot(group_upstream, weight_down, (1, 0))
    gate_grad = (act_grad * up_value * sigmoid_gate * (1.0 + gate_value * (1.0 - sigmoid_gate))).astype(BF16)
    up_grad = (act_grad * gate_value * sigmoid_gate).astype(BF16)

    def fold_tokens(term):
        return lax.psum_scatter(
            term.astype(BF16), AXIS, scatter_dimension=0, tiled=True, axis_index_groups=token_groups
        ).astype(F32)

    weighted_two = fold_tokens(dot(gate_grad, weight_gate, (1, 1)) + dot(up_grad, weight_up, (1, 1)))
    feed_out = fold_tokens(dot(activated, weight_down, (1, 1)))
    block_output = (live_rows * (hidden_state + feed_out)).astype(BF16)

    def fold_feed(term):
        pieces = term.astype(BF16).reshape(lines, plane, 2, rows, shard).transpose(1, 0, 2, 3, 4)
        pieces = lax.all_to_all(
            pieces.reshape(plane, GROUP * rows, shard), AXIS, split_axis=0, concat_axis=0, tiled=True,
            axis_index_groups=plane_groups,
        )
        mine = jnp.sum(pieces.astype(F32), axis=0).astype(BF16).reshape(GROUP, rows, shard)
        mine = lax.all_to_all(mine, AXIS, split_axis=0, concat_axis=0, tiled=True, axis_index_groups=token_groups)
        return mine.transpose(1, 0, 2).reshape(rows, hidden).astype(F32)

    down_sum = fold_feed(dot(group_upstream, activated, (0, 0)))
    gate_raw = fold_feed(dot(group_tokens, gate_grad, (0, 0)))
    up_raw = fold_feed(dot(group_tokens, up_grad, (0, 0)))
    gain_two_sum = jnp.sum(gate_raw * gate_weight.astype(F32) + up_raw * up_weight.astype(F32), axis=1)

    hidden_grad = upstream + norm_back(weighted_two, hidden_state, scale_two)
    branch_grad = hidden_grad.astype(BF16)
    mixed_grad = dot(branch_grad, weight_out, (1, 0)).astype(BF16).reshape(length, KV, heads_per_key, HD)
    prob_grad = jnp.einsum("qkgd,skd->kgqs", mixed_grad, value_rows, preferred_element_type=F32)
    value_grad = jnp.einsum("kgqs,qkgd->skd", probs_low, mixed_grad, preferred_element_type=F32)
    score_grad = probs * (prob_grad - jnp.sum(probs * prob_grad, axis=-1, keepdims=True))
    score_grad = score_grad.astype(BF16)
    query_grad = jnp.einsum("kgqs,skd->qkgd", score_grad, key_rows, preferred_element_type=F32) * factor
    key_grad = jnp.einsum("kgqs,qkgd->skd", score_grad, queries, preferred_element_type=F32) * factor
    query_low = rotary_back(query_grad.reshape(length, H, HD), cosine_table, sine_table)
    key_low = rotary_back(key_grad, cosine_table, sine_table)
    input_low = jnp.concatenate(
        [query_low.reshape(length, width), key_low.reshape(length, key_width), value_grad.reshape(length, key_width)],
        axis=1,
    ).astype(BF16)
    attention_term = jnp.concatenate(
        [dot(normed_one, input_low, (0, 0)), dot(branch_grad, mixed_heads, (0, 0))], axis=1
    ).astype(BF16)
    attention_sum = lax.psum_scatter(attention_term, AXIS, scatter_dimension=0, tiled=True).astype(F32)
    bias_sum = lax.psum(jnp.sum(input_low, axis=0, dtype=F32), AXIS)
    input_raw = attention_sum[:, :input_width]
    out_sum = attention_sum[:, input_width:]
    input_sum = input_raw * gain_one
    own_weight = jnp.concatenate([query_weight, key_weight, value_weight], axis=1).astype(F32)
    gain_one_sum = jnp.sum(input_raw * own_weight, axis=1)
    weighted_one = dot(input_low, weight_input, (1, 1))
    token_grad = hidden_grad + norm_back(weighted_one, token_float, scale_one)
    query_bias_sum = lax.dynamic_slice(bias_sum, (me * rows,), (rows,))
    value_bias_sum = lax.dynamic_slice(
        bias_sum, (width + key_width + me * value_bias.shape[0],), (value_bias.shape[0],)
    )
    return (
        block_output,
        token_grad.astype(BF16),
        gain_one_sum,
        input_sum[:, :width],
        query_bias_sum,
        input_sum[:, width : width + key_width],
        bias_sum[width : width + key_width],
        input_sum[:, width + key_width :],
        value_bias_sum,
        out_sum,
        gain_two_sum,
        gate_raw * gain_two,
        up_raw * gain_two,
        down_sum,
    )


def solution(mesh):
    split = P(AXIS)
    split_rows = P(AXIS, None)
    return jax.shard_map(
        array_body,
        mesh=mesh,
        in_specs=(
            split_rows, split, split, split, split_rows, split, split_rows, split,
            split_rows, split, split_rows, split, split_rows, split_rows, split_rows, split_rows,
        ),
        out_specs=(
            split_rows, split_rows, split, split_rows, split, split_rows, P(),
            split_rows, split, split_rows, split, split_rows, split_rows, split_rows,
        ),
        check_vma=False,
    )
```

time: 5020 us -> 832 us (0.17)
  waiting for transfers between devices: 4540 us -> 366 us
  matrix products: 190 us -> 90 us
  blocking collectives: 127 us -> 192 us
  local copies, waits for them, and re-layouts: 11.7 us -> 76.3 us
    all_to_all x12 -> x6, waiting for transfers between devices: 4070 us -> 159 us  [the longest x3 97.7 us: fold_feed(): lax.all_to_all(pieces.reshape(plane, GROUP * rows, shard), AXIS, split_ax...]
    all_gather x5 -> x6, waiting for transfers between devices: 462 us -> 146 us  [the longest x3 85.4 us: spread(): lax.all_gather(got, AXIS, axis=0, tiled=False, axis_index_groups=plane_gr...]
    all_to_all x0 -> x3, blocking collectives: none -> 116 us  [spread(): lax.all_to_all(pieces, AXIS, split_axis=0, concat_axis=0, tiled=True, axi...]
    dot_general x27 -> x20, matrix products: 190 us -> 89.5 us  [the longest x15 87.5 us: dot(): lax.dot_general(left, right, ((dims[:1], dims[1:]), ((), ())), preferred_...]
    all_gather x2 -> x0, blocking collectives: 84.4 us -> none  [the longest x1 43.2 us: body(): lax.all_gather(key_weight, 'fsdp', axis=0, tiled=True)]
    reduce_sum x16 -> x6, other arithmetic: 76.2 us -> 10.5 us  [the longest x3 8.98 us: fold_feed(): jnp.sum(pieces.astype(F32), axis=0).astype(BF16).reshape(GROUP, rows, shard)]
    reduce_scatter x0 -> x3, waiting for transfers between devices: none -> 61.1 us  [the longest x2 61.1 us: fold_tokens(): lax.psum_scatter(term.astype(BF16), AXIS, scatter_dimension=0, tiled=True...]
  transfers between devices with their start and end apart: 17 -> 15, of which waited for: 14 -> 12; matrix products, arithmetic and copies ran while one was open for 4% -> 19% of each run, Pallas kernels for 0% -> 0%
where the time goes in v1:
time: 832 us; the launch traced here: 821 us
  waiting for transfers between devices  366 us (44%)
  blocking collectives  192 us (23%)
  matrix products  90 us (11%)
  local copies, waits for them, and re-layouts  76.3 us (9%)
  other arithmetic  41.3 us (5%)
  starting transfers between devices  40.6 us (5%)
  between operations  15.1 us (2%)
    all_to_all x3, blocking collectives, spread(): lax.all_to_all(pieces, AXIS, split_axis=0, concat_axis=0, tiled=True, axi...  116 us
    all_to_all x3, waiting for transfers between devices, fold_feed(): lax.all_to_all(pieces.reshape(plane, GROUP * rows, shard), AXIS, split_ax...  97.7 us
    dot_general x15, matrix products, dot(): lax.dot_general(left, right, ((dims[:1], dims[1:]), ((), ())), preferred_...  87.5 us
    all_gather x3, waiting for transfers between devices, spread(): lax.all_gather(got, AXIS, axis=0, tiled=False, axis_index_groups=plane_gr...  85.4 us
    reduce_scatter x2, waiting for transfers between devices, fold_tokens(): lax.psum_scatter(term.astype(BF16), AXIS, scatter_dimension=0, tiled=True...  61.1 us
    all_to_all x3, waiting for transfers between devices, fold_feed(): lax.all_to_all(mine, AXIS, split_axis=0, concat_axis=0, tiled=True, axis_...  61 us
    unnamed x1, blocking collectives  38.5 us
    psum x1, blocking collectives, array_body(): bias_sum = lax.psum(jnp.sum(input_low, axis=0, dtype=F32), AXIS)  37 us
  transfers between devices with their start and end apart: 15, of which 12 were waited for; matrix products, arithmetic and copies ran while one was open for 19% of the time, Pallas kernels for 0%

profile of v1, /device:TPU:0, one launch (start us, length us, event | category | flops | bytes accessed | tf_op | source)
XLA Modules:
  0.0 821.4 jit_solution(724760652699481390)
XLA Ops:
  15.6 36.7 %all_to_all.45 = bf16[8,48,1120]{2,1,0:T(8,128)(2,1)} all-to-all(bf16[8,48,1120]{2,1,0:T(8,128)(2,1)S(1)} %copy.171), channel_id=1, replica_groups={{0,1,8,9,16,17,24,25},{2,3,10,11,18,19,26,27},{4,5,12,13,20,21,28,29},{..., dimensions={0} | all-to-all | bytes 1720320 | tf_op jit(solution)/shard_map/all_to_all | solution.py:112
  54.0 36.9 %all_to_all.46 = bf16[8,48,1120]{2,1,0:T(8,128)(2,1)} all-to-all(bf16[8,48,1120]{2,1,0:T(8,128)(2,1)S(1)} %copy.173), channel_id=1, replica_groups={{0,1,8,9,16,17,24,25},{2,3,10,11,18,19,26,27},{4,5,12,13,20,21,28,29},{..., dimensions={0} | all-to-all | bytes 1720320 | tf_op jit(solution)/shard_map/all_to_all | solution.py:112
  92.6 42.7 %all_to_all.47 = bf16[8,48,1120]{2,1,0:T(8,128)(2,1)} all-to-all(bf16[8,48,1120]{2,1,0:T(8,128)(2,1)S(1)} %copy.175), channel_id=1, replica_groups={{0,1,8,9,16,17,24,25},{2,3,10,11,18,19,26,27},{4,5,12,13,20,21,28,29},{..., dimensions={0} | all-to-all | bytes 1720320 | tf_op jit(solution)/shard_map/all_to_all | solution.py:112
  135.7 38.5 %all-reduce = bf16[2048]{0:T(1024)(128)(2,1)S(1)} all-reduce(bf16[2048]{0:T(1024)(128)(2,1)S(1)} %dynamic-update-slice), channel_id=2, replica_groups=mesh['fsdp'=32] {'fsdp'}, use_global_device_ids=true, to_apply=%add | all-reduce | flops 2048 | bytes 8192
  194.1 40.6 %all-gather.19.cloned.1.call-done = bf16[32,48,1120]{2,1,0:T(8,128)(2,1)} async-done(((bf16[8,48,1120]{2,1,0:T(8,128)(2,1)}), bf16[32,48,1120]{2,1,0:T(8,128)(2,1)}) %all-gather.19.cloned.1.call-update) | async-done | bytes 3440656 | tf_op jit(solution)/shard_map/all_gather | solution.py:113
  238.9 44.8 %all-gather.21.cloned.1.call-done = bf16[32,48,1120]{2,1,0:T(8,128)(2,1)} async-done(((bf16[8,48,1120]{2,1,0:T(8,128)(2,1)}), bf16[32,48,1120]{2,1,0:T(8,128)(2,1)}) %all-gather.21.cloned.1.call-update) | async-done | bytes 3440656 | tf_op jit(solution)/shard_map/all_gather | solution.py:113
  287.9 36.2 %all-gather.13.cloned.1.call-done = bf16[1024,1536]{1,0:T(8,128)(2,1)} async-done(((bf16[128,1536]{1,0:T(8,128)(2,1)}), bf16[1024,1536]{1,0:T(8,128)(2,1)}) %all-gather.13.cloned.1.call-update) | async-done | bytes 3145744 | tf_op jit(solution)/shard_map/all_gather | solution.py:144
  324.1 9.0 %fusion.65 = f32[1024,1120]{0,1:T(8,128)} fusion(bf16[1024,1536]{1,0:T(8,128)(2,1)} %all-gather.13.cloned.1.call-done, bf16[1536,1120]{1,0:T(8,128)(2,1)} %bitcast.151), kind=kOutput, calls=%fused_computation.132 | convolution fusion | flops 3523215360 | bytes 11173888 | tf_op jit(solution)/shard_map/dot_general | solution.py:49
  333.1 5.4 fusion.66
  338.5 24.9 %all-gather.15.cloned.1.call-done = bf16[1024,1536]{1,0:T(8,128)(2,1)} async-done(((bf16[128,1536]{1,0:T(8,128)(2,1)}), bf16[1024,1536]{1,0:T(8,128)(2,1)}) %all-gather.15.cloned.1.call-update) | async-done | bytes 3145744 | tf_op jit(solution)/shard_map/all_gather | solution.py:145
  363.3 11.6 %multiply_convert_fusion = (bf16[1024,1120]{0,1:T(8,128)(2,1)S(1)}, bf16[1024,1120]{0,1:T(8,128)(2,1)S(1)}, bf16[1024,1120]{0,1:T(8,128)(2,1)}) fusion(f32[1024,1120]{0,1:T(8,128)} %fusion.65, f32[1024,1120]{0,1:T(8,128)} %fusion.66, bf16[1024,1536]{1,0:T(8,128)(2,1)} %all-gather.15.cloned.1.call-done, bf16[1536,1120]{1,0:T(8,128)(2,1)} %bitcast.149), kind=kOutput, calls=%fused_computation.12 | convolution fusion | flops 3541565440 | bytes 22642688 | tf_op jit(solution)/shard_map/dot_general | solution.py:49
  379.3 5.9 add_convert_fusion
  385.2 9.5 %reduce-scatter.4.cloned.1.call-start = ((), (), s32[]{:S(2)}) async-start(), calls=%async_computation.14 | async-start | bytes 3538944 | tf_op jit(solution)/shard_map/reduce_scatter | solution.py:158
  394.7 8.8 %convolution_convert_fusion.5 = bf16[1024,1536]{1,0:T(8,128)(2,1)} fusion(bf16[1024,1120]{0,1:T(8,128)(2,1)} %get-tuple-element.16, bf16[1536,1120]{1,0:T(8,128)(2,1)} %bitcast.150), kind=kOutput, calls=%fused_computation.20 | convolution fusion | flops 3524788224 | bytes 8880128 | tf_op jit(solution)/shard_map/dot_general | solution.py:49
  403.5 21.0 %reduce-scatter.6.cloned.1.call-done = bf16[128,1536]{1,0:T(8,128)(2,1)} async-done(((bf16[1024,1536]{1,0:T(8,128)(2,1)}), bf16[128,1536]{1,0:T(8,128)(2,1)}) %reduce-scatter.6.cloned.1.call-update) | async-done | bytes 393232 | tf_op jit(solution)/shard_map/reduce_scatter | solution.py:158
  426.2 40.1 %reduce-scatter.4.cloned.1.call-done = bf16[128,1536]{1,0:T(8,128)(2,1)} async-done(((bf16[1024,1536]{1,0:T(8,128)(2,1)}), bf16[128,1536]{1,0:T(8,128)(2,1)}) %reduce-scatter.4.cloned.1.call-update) | async-done | bytes 393232 | tf_op jit(solution)/shard_map/reduce_scatter | solution.py:158
  486.9 6.9 convolution_convert_fusion.2
  500.4 5.9 copy.186
  506.3 5.2 all-to-all-start.3
  511.6 7.1 convolution_convert_fusion.1
  525.2 5.8 copy.191
  531.0 27.4 %all-to-all-done.3 = bf16[4,384,1120]{1,2,0:T(8,128)(2,1)} async-done(((bf16[4,384,1120]{1,2,0:T(8,128)(2,1)}), bf16[4,384,1120]{1,2,0:T(8,128)(2,1)}, u32[]{:S(2)}, u32[]{:S(2)}) %all-to-all-start.3) | async-done | bytes 3440672 | tf_op jit(solution)/shard_map/all_to_all | solution.py:168
  563.2 6.9 convolution_convert_fusion
  576.7 5.8 copy.196
  582.5 27.8 %all-to-all-done.5 = bf16[4,384,1120]{1,2,0:T(8,128)(2,1)} async-done(((bf16[4,384,1120]{1,2,0:T(8,128)(2,1)}), bf16[4,384,1120]{1,2,0:T(8,128)(2,1)}, u32[]{:S(2)}, u32[]{:S(2)}) %all-to-all-start.5) | async-done | bytes 3440672 | tf_op jit(solution)/shard_map/all_to_all | solution.py:168
  619.9 42.6 %all-to-all-done.7 = bf16[4,384,1120]{1,2,0:T(8,128)(2,1)S(1)} async-done(((bf16[4,384,1120]{1,2,0:T(8,128)(2,1)}), bf16[4,384,1120]{1,2,0:T(8,128)(2,1)S(1)}, u32[]{:S(2)}, u32[]{:S(2)}) %all-to-all-start.7) | async-done | bytes 3440672 | tf_op jit(solution)/shard_map/all_to_all | solution.py:168
  662.4 8.1 all-to-all-start.4
  676.4 24.7 %all-to-all-done.4 = bf16[8,48,1120]{2,1,0:T(8,128)(2,1)} async-done(((bf16[8,48,1120]{2,1,0:T(8,128)(2,1)}), bf16[8,48,1120]{2,1,0:T(8,128)(2,1)}, u32[]{:S(2)}, u32[]{:S(2)}) %all-to-all-start.4) | async-done | bytes 860192 | tf_op jit(solution)/shard_map/all_to_all | solution.py:173
  709.2 19.2 %all-to-all-done.6 = bf16[8,48,1120]{2,1,0:T(8,128)(2,1)} async-done(((bf16[8,48,1120]{2,1,0:T(8,128)(2,1)}), bf16[8,48,1120]{2,1,0:T(8,128)(2,1)}, u32[]{:S(2)}, u32[]{:S(2)}) %all-to-all-start.6) | async-done | bytes 860192 | tf_op jit(solution)/shard_map/all_to_all | solution.py:173
  738.9 17.1 %all-to-all-done.8 = bf16[8,48,1120]{2,1,0:T(8,128)(2,1)} async-done(((bf16[8,48,1120]{2,1,0:T(8,128)(2,1)}), bf16[8,48,1120]{2,1,0:T(8,128)(2,1)}, u32[]{:S(2)}, u32[]{:S(2)}) %all-to-all-start.8) | async-done | bytes 860192 | tf_op jit(solution)/shard_map/all_to_all | solution.py:173
  764.7 37.0 %psum.7 = f32[2048]{0:T(1024)S(1)} all-reduce(f32[2048]{0:T(1024)S(1)} %convert_reduce_fusion), channel_id=1, replica_groups=mesh['fsdp'=32] {'fsdp'}, use_global_device_ids=true, to_apply=%region_12.13 | all-reduce | flops 2048 | bytes 16384 | tf_op jit(solution)/shard_map/psum | solution.py:200
  803.4 5.1 fusion.36
  (211 shorter events, 141.5 us)
Async XLA Ops:
  7.2 168.6 %all-gather.11.cloned.1.call-start = ((), (), s32[]{:S(2)}) async-start(), calls=%async_computation.12 | async-start | bytes 11354112 | tf_op jit(solution)/shard_map/all_gather | solution.py:100
  11.4 178.6 %all-gather.17.cloned.1.call-start = ((), (), s32[]{:S(2)}) async-start(), calls=%async_computation.18 | async-start | bytes 4423680 | tf_op jit(solution)/shard_map/all_gather | solution.py:113
  52.3 38.7 %copy-start.10 = (bf16[48,8960]{1,0:T(8,128)(2,1)S(1)}, bf16[48,8960]{1,0:T(8,128)(2,1)}, u32[]{:S(2)}) copy-start(bf16[48,8960]{1,0:T(8,128)(2,1)} %param.30) | copy-start | bytes 2580484
  52.3 182.4 %all-gather.19.cloned.1.call-start = ((), (), s32[]{:S(2)}) async-start(), calls=%async_computation.19 | async-start | bytes 4423680 | tf_op jit(solution)/shard_map/all_gather | solution.py:113
  90.9 44.5 %copy-start.30 = (bf16[8]{0:T(256)(128)(2,1)S(1)}, bf16[8]{0:T(256)(128)(2,1)}, u32[]{:S(2)}) copy-start(bf16[8]{0:T(256)(128)(2,1)} %param.25) | copy-start | bytes 52
  90.9 44.5 %copy-start.31 = (bf16[8]{0:T(256)(128)(2,1)S(1)}, bf16[8]{0:T(256)(128)(2,1)}, u32[]{:S(2)}) copy-start(bf16[8]{0:T(256)(128)(2,1)} %param.23) | copy-start | bytes 52
  90.9 44.5 %copy-start.32 = (bf16[48]{0:T(256)(128)(2,1)S(1)}, bf16[48]{0:T(256)(128)(2,1)}, u32[]{:S(2)}) copy-start(bf16[48]{0:T(256)(128)(2,1)} %param.21) | copy-start | bytes 292
  90.9 83.7 %copy-start.37 = (s32[128]{0:T(128)S(1)}, s32[128]{0:T(128)}, u32[]{:S(2)}) copy-start(s32[128]{0:T(128)} %param.18) | copy-start | bytes 1540
  90.9 84.1 %copy-start.2 = (bf16[128,1536]{1,0:T(8,128)(2,1)S(1)}, bf16[128,1536]{1,0:T(8,128)(2,1)}, u32[]{:S(2)}) copy-start(bf16[128,1536]{1,0:T(8,128)(2,1)} %param.16) | copy-start | bytes 1179652
  90.9 84.8 %copy-start.26 = (s32[128]{0:T(128)S(1)}, s32[128]{0:T(128)}, u32[]{:S(2)}) copy-start(s32[128]{0:T(128)} %param.17) | copy-start | bytes 1540
  90.9 192.8 %all-gather.21.cloned.1.call-start = ((), (), s32[]{:S(2)}) async-start(), calls=%async_computation.20 | async-start | bytes 4423680 | tf_op jit(solution)/shard_map/all_gather | solution.py:113
  135.3 188.8 %all-gather.13.cloned.1.call-start = ((), (), s32[]{:S(2)}) async-start(), calls=%async_computation.13 | async-start | bytes 3538944 | tf_op jit(solution)/shard_map/all_gather | solution.py:144
  181.5 7.3 copy-start.9
  187.6 175.8 %all-gather.15.cloned.1.call-start = ((), (), s32[]{:S(2)}) async-start(), calls=%async_computation.15 | async-start | bytes 3538944 | tf_op jit(solution)/shard_map/all_gather | solution.py:145
  189.7 234.9 %reduce-scatter.6.cloned.1.call-start = ((), (), s32[]{:S(2)}) async-start(), calls=%async_computation.16 | async-start | bytes 3538944 | tf_op jit(solution)/shard_map/reduce_scatter | solution.py:158
  324.1 9.0 %copy-start.7 = (bf16[4,4,2,48,1120]{4,3,2,1,0:T(8,128)(2,1)S(1)}, bf16[4,4,2,48,1120]{4,3,2,1,0:T(8,128)(2,1)}, u32[]{:S(2)}) copy-start(bf16[4,4,2,48,1120]{4,3,2,1,0:T(8,128)(2,1)} %copy.174) | copy-start | bytes 10321924
  324.1 9.0 %copy-start.34 = (bf16[1024,1536]{1,0:T(8,128)(2,1)S(1)}, bf16[1024,1536]{1,0:T(8,128)(2,1)}, u32[]{:S(2)}) copy-start(bf16[1024,1536]{1,0:T(8,128)(2,1)} %all-gather.13.cloned.1.call-done) | copy-start | bytes 9437188
  363.3 11.6 %copy-start.6 = (bf16[4,4,2,48,1120]{4,3,2,1,0:T(8,128)(2,1)S(1)}, bf16[4,4,2,48,1120]{4,3,2,1,0:T(8,128)(2,1)}, u32[]{:S(2)}) copy-start(bf16[4,4,2,48,1120]{4,3,2,1,0:T(8,128)(2,1)} %copy.172) | copy-start | bytes 10321924
  385.2 81.1 %reduce-scatter.4.cloned.1.call-start = ((), (), s32[]{:S(2)}) async-start(), calls=%async_computation.14 | async-start | bytes 3538944 | tf_op jit(solution)/shard_map/reduce_scatter | solution.py:158
  403.5 406.2 %reduce-scatter.8.cloned.1.call-start = ((), (), s32[]{:S(2)}) async-start(), calls=%async_computation.17 | async-start | bytes 11354112 | tf_op jit(solution)/shard_map/reduce_scatter | solution.py:199
  506.3 52.0 %all-to-all-start.3 = ((bf16[4,384,1120]{1,2,0:T(8,128)(2,1)}), bf16[4,384,1120]{1,2,0:T(8,128)(2,1)}, u32[]{:S(2)}, u32[]{:S(2)}) async-start(bf16[4,384,1120]{1,2,0:T(8,128)(2,1)} %copy.186), calls=%async_computation.6 | async-start | bytes 6881280 | tf_op jit(solution)/shard_map/all_to_all | solution.py:168
  531.0 32.2 %copy-start.33 = (bf16[1024,1536]{1,0:T(8,128)(2,1)S(1)}, bf16[1024,1536]{1,0:T(8,128)(2,1)}, u32[]{:S(2)}) copy-start(bf16[1024,1536]{1,0:T(8,128)(2,1)} %all-gather.15.cloned.1.call-done) | copy-start | bytes 9437188
  558.4 51.9 %all-to-all-start.5 = ((bf16[4,384,1120]{1,2,0:T(8,128)(2,1)}), bf16[4,384,1120]{1,2,0:T(8,128)(2,1)}, u32[]{:S(2)}, u32[]{:S(2)}) async-start(bf16[4,384,1120]{1,2,0:T(8,128)(2,1)} %copy.191), calls=%async_computation.8 | async-start | bytes 6881280 | tf_op jit(solution)/shard_map/all_to_all | solution.py:168
  610.2 52.2 %all-to-all-start.7 = ((bf16[4,384,1120]{1,2,0:T(8,128)(2,1)}), bf16[4,384,1120]{1,2,0:T(8,128)(2,1)S(1)}, u32[]{:S(2)}, u32[]{:S(2)}) async-start(bf16[4,384,1120]{1,2,0:T(8,128)(2,1)} %copy.196), calls=%async_computation.10 | async-start | bytes 6881280 | tf_op jit(solution)/shard_map/all_to_all | solution.py:168
  662.4 38.6 %all-to-all-start.4 = ((bf16[8,48,1120]{2,1,0:T(8,128)(2,1)}), bf16[8,48,1120]{2,1,0:T(8,128)(2,1)}, u32[]{:S(2)}, u32[]{:S(2)}) async-start(bf16[8,48,1120]{2,1,0:T(8,128)(2,1)} %bitcast.156), calls=%async_computation.7 | async-start | bytes 1769472 | tf_op jit(solution)/shard_map/all_to_all | solution.py:173
  701.1 27.3 %all-to-all-start.6 = ((bf16[8,48,1120]{2,1,0:T(8,128)(2,1)}), bf16[8,48,1120]{2,1,0:T(8,128)(2,1)}, u32[]{:S(2)}, u32[]{:S(2)}) async-start(bf16[8,48,1120]{2,1,0:T(8,128)(2,1)} %bitcast.155), calls=%async_computation.9 | async-start | bytes 1769472 | tf_op jit(solution)/shard_map/all_to_all | solution.py:173
  728.4 27.6 %all-to-all-start.8 = ((bf16[8,48,1120]{2,1,0:T(8,128)(2,1)}), bf16[8,48,1120]{2,1,0:T(8,128)(2,1)}, u32[]{:S(2)}, u32[]{:S(2)}) async-start(bf16[8,48,1120]{2,1,0:T(8,128)(2,1)} %bitcast.54), calls=%async_computation.11 | async-start | bytes 1769472 | tf_op jit(solution)/shard_map/all_to_all | solution.py:173
  759.6 43.8 %copy-start.3 = (bf16[128,1536]{1,0:T(8,128)(2,1)S(1)}, bf16[128,1536]{1,0:T(8,128)(2,1)}, u32[]{:S(2)}) copy-start(bf16[128,1536]{1,0:T(8,128)(2,1)} %param.16) | copy-start | bytes 1179652
  803.4 7.3 copy-start.13
  803.4 7.3 copy-start.16
  803.4 7.3 copy-start.17
  803.4 7.3 copy-start.21
  (25 other events, 73.6 us)
Sparse Core Ops, SparseCore 0:
  11.5 125.1 all-gather.10
  138.6 46.9 all-gather.16
  187.4 47.2 all-gather.18
  236.4 47.2 all-gather.20
  285.8 38.2 all-gather.12
  326.1 37.1 all-gather.14
  385.3 39.2 reduce-scatter.5
  426.9 39.4 reduce-scatter.3
  485.2 206.6 reduce-scatter.7

commit v2 on v1

--- a/solution.py
+++ b/solution.py
@@ -1,14 +1,18 @@
+import functools
 import math
 
 import jax
 import jax.numpy as jnp
 from jax import lax
+from jax.experimental import pallas as pl
+from jax.experimental.pallas import tpu as pltpu
 from jax.sharding import PartitionSpec as P
 
 H = 12
 KV = 2
 HD = 128
 GROUP = 8
+LINES = GROUP // 2
 
 EPSILON = 1e-06
 ROPE_BASE = 1000000.0
@@ -227,11 +231,734 @@
     )
 
 
+def mega(rows, plane, *refs):
+    (
+        x_in, cot_in, aux_in, bias_in, wq_in, wk_in, wv_in, wo_in, wg_in, wu_in, wd_in,
+        o1, o2, o3, o4, o5, fo_out, bg_out, tg_out, h_out,
+        xs, xh, aux, sa, wgs, wus, w1, w2, w3, w4, w5, g5,
+        r1, r2, r3, r4, hn, gb, gt, up, act, pb, rb, rt,
+        zb, zr, dh, dz, ob, qr, kr, vr, pr, dob, dq, cos, sin, msk, ba, bp, bgp, bsum,
+        lsem, a_s, a_r, p_s, p_r, r_s, r_r, o_s, o_r, t_s, t_r, d_s, d_r, b_s, b_r, e_s, e_r, credit, pair_credit,
+    ) = refs
+    weights = (w1, w2, w3, w4, w5)
+    grads = (w1, w2, w3, w4, g5)
+    landing = (r1, r2, r3, r4, r4)
+    outs = (o1, o2, o3, o4, o5)
+    block, width = x_in.shape
+    shard = w3.shape[1]
+    half = w2.shape[1]
+    heads = half // HD
+    strip = width // LINES
+    hidden = wg_in.shape[1]
+    short = GROUP * shard - hidden
+    factor = 1.0 / math.sqrt(HD)
+
+    me = lax.axis_index(AXIS)
+    c = lax.rem(me, 2)
+    p = lax.rem(lax.div(me, 2), plane)
+    z = lax.div(me, 2 * plane)
+    f = z * 2 + c
+    xbit, ybit = lax.rem(p, 2), lax.div(p, 2)
+    px = p + 1 - 2 * xbit
+    py = p + 2 - 4 * ybit
+    pd = px + 2 - 4 * ybit
+    zlow, zhigh = lax.rem(z, 2), lax.div(z, 2)
+
+    def flip(bit, on):
+        return bit + on - 2 * bit * on
+
+    def zf(high, low):
+        return flip(zhigh, high) * 2 + flip(zlow, low)
+
+    def zj(j):
+        if isinstance(j, int):
+            return zf(j // 2, j % 2)
+        return zf(lax.div(j, 2), lax.rem(j, 2))
+
+    def dev(zz, pp, cc):
+        return (zz * plane + pp) * 2 + cc
+
+    sib, xnb, ynb = dev(z, p, 1 - c), dev(z, px, c), dev(z, py, c)
+
+    def unit(zz, pp):
+        return pl.ds(pl.multiple_of((zz * plane + pp) * 2 * rows, 16), 2 * rows)
+
+    def piece(zz, pp, cc):
+        return pl.ds(pl.multiple_of(((zz * plane + pp) * 2 + cc) * rows, 16), rows)
+
+    def slot(s):
+        return pl.ds(pl.multiple_of(s * 2 * rows, 16), 2 * rows)
+
+    def tokens_of(zz, cc):
+        return pl.ds(pl.multiple_of((zz * 2 + cc) * block, block), block)
+
+    def chunk_of(zz):
+        return pl.ds(pl.multiple_of(zz * 2 * block, 2 * block), 2 * block)
+
+    def remote(src, dst, send, recv, target):
+        return pltpu.make_async_remote_copy(
+            src_ref=src, dst_ref=dst, send_sem=send, recv_sem=recv,
+            device_id=(target,), device_id_type=pl.DeviceIdType.MESH,
+        )
+
+    def dot_nn(a, b):
+        return lax.dot_general(a, b, (((1,), (0,)), ((), ())), preferred_element_type=F32)
+
+    def dot_nt(a, b):
+        return lax.dot_general(a, b, (((1,), (1,)), ((), ())), preferred_element_type=F32)
+
+    def dot_tn(a, b):
+        return lax.dot_general(a, b, (((0,), (0,)), ((), ())), preferred_element_type=F32)
+
+    def local(n, src, dst):
+        return pltpu.make_async_copy(src, dst, lsem.at[n])
+
+    loads = [local(0, aux_in, aux.at[c]), local(1, x_in, xs.at[c])]
+    for side in range(2):
+        loads.append(local(2 + side, wq_in.at[:, pl.ds(side * half, half)], sa.at[side, :, pl.ds(0, half)]))
+        loads.append(local(4 + side, wk_in.at[:, pl.ds(side * HD, HD)], sa.at[side, :, pl.ds(half, HD)]))
+        loads.append(local(6 + side, wv_in.at[:, pl.ds(side * HD, HD)], sa.at[side, :, pl.ds(half + HD, HD)]))
+    late = [local(8, wg_in, wgs), local(9, wu_in, wus), local(10, cot_in, gb.at[tokens_of(z, c)])]
+    for copy in loads + late:
+        copy.start()
+
+    barrier = pltpu.get_barrier_semaphore()
+    friends = [dev(zj(j // 2), p, flip(c, j % 2)) for j in range(1, GROUP)] + [xnb, ynb, dev(z, pd, c)]
+    for friend in friends:
+        pl.semaphore_signal(barrier, inc=1, device_id=(friend,), device_id_type=pl.DeviceIdType.MESH)
+
+    for copy in loads:
+        copy.wait()
+    row_id = lax.broadcasted_iota(jnp.int32, (block, block), 0)
+    lane_id = lax.broadcasted_iota(jnp.int32, (block, block), 1)
+
+    def column(row):
+        return jnp.sum(jnp.where(row_id == lane_id, row, 0.0), axis=1, keepdims=True)
+
+    own_aux = aux[c]
+    gain_one = column(own_aux[2:3])[:rows]
+    gain_two = column(own_aux[3:4])[:rows]
+    for side in range(2):
+        sa[side] = (sa[side].astype(F32) * gain_one).astype(BF16)
+    pl.semaphore_wait(barrier, len(friends))
+
+    def source(k, ff, cc):
+        if k == 0:
+            return sa.at[cc]
+        if k == 1:
+            return wo_in.at[:, pl.ds(pl.multiple_of(cc * half, 128), half)]
+        start = pl.multiple_of((ff * (shard // 128) - lax.div(ff, GROUP - 1) * (short // 128)) * 128, 128)
+        return (wgs, wus, wd_in)[k - 2].at[:, pl.ds(start, shard)]
+
+    def a_copy(k, j):
+        zz, cc = zj(j // 2), flip(c, j % 2)
+        return remote(
+            source(k, zz * 2 + cc, cc), weights[k].at[piece(z, p, c)], a_s.at[k, j], a_r.at[k, j], dev(zz, p, cc)
+        )
+
+    def a_own(k):
+        return local(11 + k, source(k, f, c), weights[k].at[piece(z, p, c)])
+
+    def a_send(k):
+        a_own(k).start()
+        for j in range(1, GROUP):
+            a_copy(k, j).start()
+
+    def a_wait(k, jz):
+        if jz == 0:
+            a_own(k).wait()
+        else:
+            a_copy(k, 2 * jz).wait_recv()
+        a_copy(k, 2 * jz + 1).wait_recv()
+
+    def ag_copy(k, s):
+        j = s % 4
+        if s < 4:
+            part, target = unit(zj(j), p), xnb
+        elif s < 8:
+            part, target = unit(zj(j), p), ynb
+        elif j < 2:
+            part, target = unit(zj(j), px), ynb
+        else:
+            part, target = unit(zj(j), py), xnb
+        return remote(weights[k].at[part], weights[k].at[part], p_s.at[k, s], p_r.at[k, s], target)
+
+    def ag_send(k):
+        for j in range(LINES):
+            a_wait(k, j)
+            ag_copy(k, j).start()
+            ag_copy(k, 4 + j).start()
+
+    def ag_relay(k):
+        for j in range(4):
+            ag_copy(k, j if j < 2 else 4 + j).wait_recv()
+            ag_copy(k, 8 + j).start()
+
+    def ag_finish(k):
+        for s in (2, 3, 4, 5, 8, 9, 10, 11):
+            ag_copy(k, s).wait_recv()
+
+    def ag_sent(k):
+        for s in range(12):
+            ag_copy(k, s).wait_send()
+
+    def tok_copy(which, s):
+        buf = (hn, gb)[which]
+        if s < 3:
+            part, target = tokens_of(z, c), dev(zj(s + 1), p, c)
+        elif s == 3:
+            part, target = tokens_of(z, c), sib
+        else:
+            part, target = tokens_of(zj(s - 3), c), sib
+        return remote(buf.at[part], buf.at[part], t_s.at[which, s], t_r.at[which, s], target)
+
+    def tok_send(which):
+        for s in range(4):
+            tok_copy(which, s).start()
+
+    def tok_forward(which):
+        for s in range(3):
+            tok_copy(which, s).wait_recv()
+            tok_copy(which, 4 + s).start()
+
+    def tok_finish(which):
+        for s in range(3, 7):
+            tok_copy(which, s).wait_recv()
+
+    def e_copy(n, src, dst):
+        return remote(src, dst, e_s.at[n], e_r.at[n], sib)
+
+    send_aux = e_copy(0, aux.at[c], aux.at[c])
+    send_x = e_copy(1, xs.at[c], xs.at[c])
+    send_z = e_copy(2, zb.at[1 - c], zr)
+    send_dz = e_copy(3, dz.at[pl.ds(pl.multiple_of(c * block, block), block)], dz.at[pl.ds(pl.multiple_of(c * block, block), block)])
+    send_u = e_copy(4, zb.at[1 - c], zr)
+
+    def bias_copy(s):
+        zz, cc = zj(s // 2), flip(c, s % 2)
+        return remote(bias_in.at[cc], ba.at[f], b_s.at[s], b_r.at[s], dev(zz, p, cc))
+
+    def plane_copy(base, n, buf):
+        target = dev(z, (px, py, pd)[n], c)
+        return remote(buf.at[p], buf.at[p], b_s.at[base + n], b_r.at[base + n], target)
+
+    def bias_out(s):
+        zz, cc = zj(s // 2), flip(c, s % 2)
+        return remote(bsum, bg_out.at[f], b_s.at[16 + s], b_r.at[16 + s], dev(zz, p, cc))
+
+    send_aux.start()
+    send_x.start()
+    a_send(0)
+    bias_own = local(16, bias_in.at[c], ba.at[f])
+    bias_own.start()
+    for s in range(1, GROUP):
+        bias_copy(s).start()
+    a_send(1)
+
+    late[0].wait()
+    late[1].wait()
+    late[2].wait()
+    for ref in (wgs, wus):
+        for n in range(0, hidden, 1792):
+            cols = pl.ds(n, min(1792, hidden - n))
+            ref[:, cols] = (ref[:, cols].astype(F32) * gain_two).astype(BF16)
+    live = jnp.where(column(own_aux[1:2]) >= 0.0, 1.0, 0.0)
+    gb[tokens_of(z, c)] = (gb[tokens_of(z, c)].astype(F32) * live).astype(BF16)
+
+    ag_send(0)
+    a_send(2)
+
+    send_x.wait_recv()
+    send_aux.wait_recv()
+    lanes = lax.broadcasted_iota(jnp.int32, (1, HD), 1)
+    freq_index = jnp.where(lanes < HD // 2, lanes, lanes - HD // 2).astype(F32)
+    frequency = jnp.exp(freq_index * (-2.0 * math.log(ROPE_BASE) / HD))
+    for b in range(2):
+        values = xs[b].astype(F32)
+        scale = lax.rsqrt(jnp.mean(values * values, axis=1, keepdims=True) + EPSILON)
+        xh[pl.ds(b * block, block)] = (values * scale).astype(BF16)
+        info = aux[b]
+        angles = column(info[0:1]) * frequency
+        cos[b] = jnp.cos(angles)
+        sine = jnp.sin(angles)
+        sin[b] = jnp.where(lane_id < HD // 2, -sine, sine)
+        same = column(info[1:2]) == info[1:2]
+        msk[b] = jnp.where(same & (lane_id <= row_id), 1.0, 0.0)
+
+    ag_relay(0)
+    for s in range(1, GROUP):
+        bias_copy(s).wait_recv()
+    bias_own.wait()
+    total = ba[0]
+    for s in range(1, GROUP):
+        total = total + ba[s]
+    bp[p] = total
+    for n in range(3):
+        plane_copy(8, n, bp).start()
+    ag_send(1)
+    a_send(3)
+
+    for n in range(3):
+        plane_copy(8, n, bp).wait_recv()
+    bias_row = (bp[0] + bp[1]) + (bp[2] + bp[3])
+    ag_finish(0)
+
+    def rope(v, b):
+        return v * cos[b] + pltpu.roll(v, HD // 2, 1) * sin[b]
+
+    def rope_back(v, b):
+        return v * cos[b] + pltpu.roll(v * sin[b], HD // 2, 1)
+
+    for n in range(heads // 2 + 1):
+        cols = pl.ds(n * 2 * HD, 2 * HD)
+        out = dot_nn(xh[...], w1[:, cols]) + bias_row[:, n * 2 * HD : (n + 1) * 2 * HD]
+        for b in range(2):
+            part = out[b * block : (b + 1) * block]
+            if n < heads // 2:
+                for i in range(2):
+                    qr[b, pl.ds((2 * n + i) * block, block)] = rope(part[:, i * HD : (i + 1) * HD], b).astype(BF16)
+            else:
+                kr[b] = rope(part[:, :HD], b).astype(BF16)
+                vr[b] = part[:, HD:].astype(BF16)
+
+    ag_relay(1)
+    ag_send(2)
+    a_send(4)
+
+    for b in range(2):
+        scores = dot_nt(qr[b], kr[b]) * factor
+        scores = jnp.where(msk[b][None] > 0.0, scores.reshape(heads, block, block), -jnp.inf)
+        weight = jnp.exp(scores - jnp.max(scores, axis=-1, keepdims=True))
+        weight = weight / jnp.sum(weight, axis=-1, keepdims=True)
+        weight = weight.reshape(heads * block, block)
+        pr[b] = weight
+        mixed = dot_nn(weight.astype(BF16), vr[b]).astype(BF16)
+        for i in range(heads):
+            ob[pl.ds(b * block, block), pl.ds(i * HD, HD)] = mixed[i * block : (i + 1) * block]
+
+    ag_finish(1)
+    for n in range(0, width, 512):
+        part = dot_nt(ob[...], w2[pl.ds(n, 512), :])
+        zb[0, :, pl.ds(n, 512)] = part[:block]
+        zb[1, :, pl.ds(n, 512)] = part[block:]
+    send_z.start()
+    ag_relay(2)
+    send_z.wait_recv()
+    state = xs[c].astype(F32) + zb[c] + zr[...]
+    h_out[...] = state
+    scale_two = lax.rsqrt(jnp.mean(state * state, axis=1, keepdims=True) + EPSILON)
+    hn[tokens_of(z, c)] = (state * scale_two).astype(BF16)
+    tok_send(0)
+    ag_send(3)
+    tok_send(1)
+    tok_forward(0)
+    ag_relay(3)
+    tok_finish(0)
+    ag_finish(2)
+    ag_finish(3)
+
+    tile = 3 * HD
+    last = lax.div(f, GROUP - 1)
+    tile_lane = lax.broadcasted_iota(jnp.int32, (1, tile), 1)
+    keep = jnp.where(tile_lane < last * short, 0.0, 1.0)
+
+    @pl.loop(0, LINES)
+    def forward_chunk(i):
+        rows_here = chunk_of(i)
+        left = hn[rows_here]
+        for n in range(0, shard, tile):
+            cols = pl.ds(n, tile)
+            gate = dot_nn(left, w3[:, cols])
+            lift = dot_nn(left, w4[:, cols])
+            if n == 0:
+                gate = gate * keep
+                lift = lift * keep
+            gt[rows_here, cols] = gate.astype(BF16)
+            up[rows_here, cols] = lift.astype(BF16)
+            act[rows_here, cols] = (gate * jax.nn.sigmoid(gate) * lift).astype(BF16)
+
+    tok_forward(1)
+    ag_send(4)
+    tok_finish(1)
+
+    def rs_copy(k, s, h):
+        ref = grads[k]
+        high = (0, 1, 1, 0, 0, 1)[s]
+        zz = zf(high, h)
+        part = unit(zz, (pd, pd, px, py, px, py)[s])
+        place = (0, 2, 6, 8, 4, 10)[s] + h
+        target = (ynb, xnb, xnb, ynb, xnb, ynb)[s]
+        return remote(ref.at[part], landing[k].at[slot(place)], r_s.at[k, place], r_r.at[k, place], target)
+
+    def rs_start(k, left_ref, right_ref):
+        @pl.loop(0, 2)
+        def both(h):
+            for high in range(2):
+                zz = zf(high, h)
+                at = pl.multiple_of(zz * strip, 128)
+                left = left_ref[:, pl.ds(at, strip)]
+                grads[k][pl.ds(at, strip), :] = dot_tn(left, right_ref[...]).astype(BF16)
+                for s in ((0, 3), (1, 2))[high]:
+                    rs_copy(k, s, h).start()
+
+    def rs_middle(k):
+        @pl.loop(0, 2)
+        def both(h):
+            for high in range(2):
+                rs_copy(k, high, h).wait_recv()
+                part = unit(zf(high, h), (px, py)[high])
+                got = landing[k][slot(2 * high + h)]
+                grads[k][part] = (grads[k][part].astype(F32) + got.astype(F32)).astype(BF16)
+                rs_copy(k, 4 + high, h).start()
+
+    def out_copy(k, j, other):
+        zz, cc = zj(j), flip(c, other)
+        return remote(
+            grads[k].at[piece(zz, p, cc)], outs[k].at[f], o_s.at[k, 2 * j + other], o_r.at[k, 2 * j + other], dev(zz, p, cc)
+        )
+
+    def out_own(k):
+        return local(17 + k, grads[k].at[piece(z, p, c)], outs[k].at[f])
+
+    def rs_finish(k):
+        for j in (3, 2, 1, 0):
+            h, high = j % 2, j // 2
+            rs_copy(k, (4, 2)[high], h).wait_recv()
+            rs_copy(k, (3, 5)[high], h).wait_recv()
+            part = unit(zj(j), p)
+            got = landing[k][slot(4 + j)].astype(F32) + landing[k][slot(8 + j)].astype(F32)
+            grads[k][part] = (grads[k][part].astype(F32) + got).astype(BF16)
+            out_copy(k, j, 1).start()
+            if j == 0:
+                out_own(k).start()
+            else:
+                out_copy(k, j, 0).start()
+
+    rs_start(4, gb, act)
+    ag_relay(4)
+    ag_finish(4)
+
+    def pair_copy(which, j):
+        return remote(
+            pb.at[tokens_of(zj(j), 1 - c)], rb.at[pl.ds(pl.multiple_of(j * block, block), block)],
+            d_s.at[which, j], d_r.at[which, j], sib,
+        )
+
+    def line_copy(which, j):
+        dst = (rt, fo_out)[which]
+        return remote(
+            pb.at[tokens_of(zj(j), c)], dst.at[j], d_s.at[which, 4 + j], d_r.at[which, 4 + j], dev(zj(j), p, c)
+        )
+
+    def pair_add(which, j):
+        pair_copy(which, j).wait_recv()
+        part = tokens_of(zj(j), c)
+        got = rb[pl.ds(pl.multiple_of(j * block, block), block)].astype(F32)
+        pb[part] = (pb[part].astype(F32) + got).astype(BF16)
+
+    @pl.loop(0, LINES)
+    def backward_chunk(i):
+        j = LINES - 1 - i
+        rows_here = chunk_of(zj(j))
+        left = gb[rows_here]
+        for n in range(0, shard, tile):
+            cols = pl.ds(n, tile)
+            d_act = dot_nn(left, w5[:, cols])
+            gate = gt[rows_here, cols].astype(F32)
+            lift = up[rows_here, cols].astype(F32)
+            sig = jax.nn.sigmoid(gate)
+            gt[rows_here, cols] = (d_act * lift * sig * (1.0 + gate * (1.0 - sig))).astype(BF16)
+            up[rows_here, cols] = (d_act * gate * sig).astype(BF16)
+        for n in range(0, width, 512):
+            part = pl.ds(n, 512)
+            back = dot_nt(gt[rows_here], w3[part, :]) + dot_nt(up[rows_here], w4[part, :])
+            pb[rows_here, part] = back.astype(BF16)
+        pair_copy(0, j).start()
+
+        @pl.when(i > 0)
+        def _():
+            pair_add(0, j + 1)
+            line_copy(0, j + 1).start()
+
+    pair_add(0, 0)
+    pl.semaphore_signal(pair_credit, inc=1, device_id=(sib,), device_id_type=pl.DeviceIdType.MESH)
+
+    rs_middle(4)
+    ag_sent(2)
+    rs_start(2, hn, gt)
+    rs_finish(4)
+    for target in (xnb, ynb):
+        pl.semaphore_signal(credit, inc=1, device_id=(target,), device_id_type=pl.DeviceIdType.MESH)
+    ag_sent(3)
+    pl.semaphore_wait(credit, 2)
+    rs_start(3, hn, up)
+    rs_middle(2)
+
+    for j in range(1, LINES):
+        line_copy(0, j).wait_recv()
+    weighted = pb[tokens_of(z, c)].astype(F32)
+    for j in range(1, LINES):
+        weighted = weighted + rt[j].astype(F32)
+    state = h_out[...]
+    scale_two = lax.rsqrt(jnp.mean(state * state, axis=1, keepdims=True) + EPSILON)
+    spread = jnp.mean(weighted * state, axis=1, keepdims=True)
+    grad = gb[tokens_of(z, c)].astype(F32) + scale_two * weighted - state * (scale_two * scale_two * scale_two) * spread
+    dh[...] = grad
+    dz[pl.ds(pl.multiple_of(c * block, block), block)] = grad.astype(BF16)
+    send_dz.start()
+
+    for j in range(LINES):
+        pair_copy(0, j).wait_send()
+    for j in range(1, LINES):
+        line_copy(0, j).wait_send()
+    pl.semaphore_wait(pair_credit, 1)
+
+    @pl.loop(0, LINES)
+    def output_chunk(i):
+        j = LINES - 1 - i
+        rows_here = chunk_of(zj(j))
+        for n in range(0, width, 512):
+            part = pl.ds(n, 512)
+            pb[rows_here, part] = dot_nt(act[rows_here], w5[part, :]).astype(BF16)
+        pair_copy(1, j).start()
+
+        @pl.when(i > 0)
+        def _():
+            pair_add(1, j + 1)
+            line_copy(1, j + 1).start()
+
+    pair_add(1, 0)
+    fo_own = local(22, pb.at[tokens_of(z, c)], fo_out.at[0])
+    fo_own.start()
+    rs_middle(3)
+    rs_finish(2)
+
+    send_dz.wait_recv()
+    for n in range(0, heads, 2):
+        part = dot_nn(dz[...], w2[:, pl.ds(n * HD, 2 * HD)]).astype(BF16)
+        for b in range(2):
+            for i in range(2):
+                dob[b, pl.ds((n + i) * block, block)] = part[b * block : (b + 1) * block, i * HD : (i + 1) * HD]
+    ag_sent(1)
+    rs_start(1, dz, ob)
+    for b in range(2):
+        weight = pr[b]
+        d_weight = dot_nt(dob[b], vr[b])
+        d_score = weight * (d_weight - jnp.sum(weight * d_weight, axis=-1, keepdims=True))
+        d_score = d_score.astype(BF16)
+        d_query = dot_nn(d_score, kr[b]) * factor
+        here = pl.ds(b * block, block)
+        for i in range(heads):
+            dq[here, pl.ds(i * HD, HD)] = rope_back(d_query[i * block : (i + 1) * block], b).astype(BF16)
+        dq[here, pl.ds(half, HD)] = rope_back(dot_tn(d_score, qr[b]) * factor, b).astype(BF16)
+        dq[here, pl.ds(half + HD, HD)] = dot_tn(weight.astype(BF16), dob[b]).astype(BF16)
+
+    rs_middle(1)
+    send_z.wait_send()
+    for n in range(0, width, 512):
+        part = dot_nt(dq[...], w1[pl.ds(n, 512), :])
+        zb[0, :, pl.ds(n, 512)] = part[:block]
+        zb[1, :, pl.ds(n, 512)] = part[block:]
+    send_u.start()
+    ag_sent(0)
+    rs_start(0, xh, dq)
+    bgp[p] = jnp.sum(dq[...].astype(F32), axis=0, keepdims=True)
+    for n in range(3):
+        plane_copy(11, n, bgp).start()
+
+    send_u.wait_recv()
+    weighted = zb[c] + zr[...]
+    values = xs[c].astype(F32)
+    scale = lax.rsqrt(jnp.mean(values * values, axis=1, keepdims=True) + EPSILON)
+    spread = jnp.mean(weighted * values, axis=1, keepdims=True)
+    tg_out[...] = (dh[...] + scale * weighted - values * (scale * scale * scale) * spread).astype(BF16)
+
+    for n in range(3):
+        plane_copy(11, n, bgp).wait_recv()
+    bsum[...] = (bgp[0] + bgp[1]) + (bgp[2] + bgp[3])
+    bg_own = local(23, bsum, bg_out.at[f])
+    bg_own.start()
+    for s in range(1, GROUP):
+        bias_out(s).start()
+    rs_finish(3)
+    rs_finish(1)
+    rs_middle(0)
+    rs_finish(0)
+
+    for s in range(1, GROUP):
+        bias_out(s).wait()
+        bias_copy(s).wait_send()
+    for n in range(3):
+        plane_copy(8, n, bp).wait_send()
+        plane_copy(11, n, bgp).wait_send()
+    bg_own.wait()
+    fo_own.wait()
+    for j in range(LINES):
+        pair_copy(1, j).wait_send()
+    for j in range(1, LINES):
+        line_copy(1, j).wait()
+    for copy in (send_aux, send_x, send_dz, send_u):
+        copy.wait_send()
+    for which in range(2):
+        for s in range(7):
+            tok_copy(which, s).wait_send()
+    ag_sent(4)
+    for k in range(5):
+        out_own(k).wait()
+        for j in range(1, GROUP):
+            a_copy(k, j).wait_send()
+            out_copy(k, j // 2, j % 2).wait()
+        for h in range(2):
+            for s in range(6):
+                rs_copy(k, s, h).wait_send()
+
+
+def kernel_call(rows, plane, block, width, hidden, aux, bias, tokens, cotangent, *weights):
+    half = width // 2
+    blocks = hidden // 128
+    shard = -(-blocks // GROUP) * 128
+    inner = half + 2 * HD
+    heads = half // HD
+    columns = (inner, half, shard, shard, shard)
+    dma = pltpu.SemaphoreType.DMA
+    vm = pltpu.VMEM
+    group_tokens = GROUP * block
+    any_space = pl.BlockSpec(memory_space=pl.ANY)
+    vmem_space = pl.BlockSpec(memory_space=pltpu.VMEM)
+    out_shape = [jax.ShapeDtypeStruct((GROUP, rows, n), BF16) for n in columns]
+    out_shape += [
+        jax.ShapeDtypeStruct((LINES, block, width), BF16),
+        jax.ShapeDtypeStruct((GROUP, 1, inner), F32),
+        jax.ShapeDtypeStruct((block, width), BF16),
+        jax.ShapeDtypeStruct((block, width), F32),
+    ]
+    scratch = [
+        vm((2, block, width), BF16), vm((2 * block, width), BF16), vm((2, 8, 128), F32), vm((2, rows, inner), BF16),
+        vm((rows, hidden), BF16), vm((rows, hidden), BF16),
+    ]
+    scratch += [vm((width, n), BF16) for n in columns] + [vm((width, shard), BF16)]
+    scratch += [vm((12 * 2 * rows, n), BF16) for n in columns[:4]]
+    scratch += [vm((group_tokens, width), BF16)] * 2 + [vm((group_tokens, shard), BF16)] * 3
+    scratch += [
+        vm((group_tokens, width), BF16), vm((LINES * block, width), BF16), vm((LINES, block, width), BF16),
+        vm((2, block, width), F32), vm((block, width), F32), vm((block, width), F32), vm((2 * block, width), BF16),
+        vm((2 * block, half), BF16), vm((2, heads * block, HD), BF16), vm((2, block, HD), BF16), vm((2, block, HD), BF16),
+        vm((2, heads * block, block), F32), vm((2, heads * block, HD), BF16), vm((2 * block, inner), BF16),
+        vm((2, block, HD), F32), vm((2, block, HD), F32), vm((2, block, block), F32),
+        vm((GROUP, 1, inner), F32), vm((4, 1, inner), F32), vm((4, 1, inner), F32), vm((1, inner), F32),
+    ]
+    scratch += [dma((24,))]
+    scratch += [dma((5, 8))] * 2 + [dma((5, 12))] * 4 + [dma((5, 8))] * 2 + [dma((2, 8))] * 4 + [dma((24,))] * 2 + [dma((8,))] * 2
+    scratch += [pltpu.SemaphoreType.REGULAR] * 2
+    return pl.pallas_call(
+        functools.partial(mega, rows, plane),
+        out_shape=out_shape,
+        in_specs=[any_space] * 11,
+        out_specs=[any_space] * 7 + [vmem_space] * 2,
+        scratch_shapes=scratch,
+        compiler_params=pltpu.CompilerParams(
+            collective_id=0, has_side_effects=True, vmem_limit_bytes=64 * 2**20 - 2**17
+        ),
+        name="layer",
+    )(tokens, cotangent, aux, bias, *weights)
+
+
+def kernel_body(
+    tokens, segment, position, first_gain, query_weight, query_bias, key_weight, key_bias, value_weight, value_bias,
+    out_weight, second_gain, gate_weight, up_weight, down_weight, cotangent,
+):
+    count = lax.axis_size(AXIS)
+    me = lax.axis_index(AXIS)
+    plane = count // GROUP
+    rows, width = query_weight.shape
+    block = tokens.shape[0]
+    hidden = gate_weight.shape[1]
+    key_width = key_weight.shape[1]
+    half = width // 2
+
+    def wide(v):
+        return jnp.pad(v.astype(F32), (0, 128 - v.shape[0]))
+
+    aux = jnp.stack([wide(position), wide(segment), wide(first_gain), wide(second_gain)] + [jnp.zeros((128,), F32)] * 4)
+
+    def placed(v):
+        full = jnp.zeros((v.shape[0] * count,), F32)
+        return lax.dynamic_update_slice(full, v.astype(F32), (me * v.shape[0],)).reshape(2, -1)
+
+    bias = jnp.concatenate([placed(query_bias), placed(key_bias), placed(value_bias)], axis=1)[:, None, :]
+    pieces_in, pieces_out, gate_raw, up_raw, down_raw, feed, bias_sum, token_grad, state = kernel_call(
+        rows, plane, block, width, hidden, aux, bias, tokens, cotangent,
+        query_weight, key_weight, value_weight, out_weight, gate_weight, up_weight, down_weight,
+    )
+    live_rows = (segment >= 0).astype(F32)[:, None]
+    gain_one = first_gain.astype(F32)[:, None]
+    gain_two = second_gain.astype(F32)[:, None]
+    block_output = (live_rows * (state + jnp.sum(feed.astype(F32), axis=0))).astype(BF16)
+
+    def sides(pieces):
+        total = jnp.sum(pieces.astype(F32).reshape(LINES, 2, rows, -1), axis=0)
+        return total[0], total[1]
+
+    def join(pieces):
+        shard = pieces.shape[2]
+        short = GROUP * shard - hidden
+        parts = [pieces[i] for i in range(GROUP - 1)] + [pieces[GROUP - 1][:, short:]]
+        return jnp.concatenate(parts, axis=1).astype(F32)
+
+    left, right = sides(pieces_in)
+    query_raw = jnp.concatenate([left[:, :half], right[:, :half]], axis=1)
+    key_raw = jnp.concatenate([left[:, half : half + HD], right[:, half : half + HD]], axis=1)
+    value_raw = jnp.concatenate([left[:, half + HD :], right[:, half + HD :]], axis=1)
+    gain_one_sum = (
+        jnp.sum(query_raw * query_weight.astype(F32), axis=1)
+        + jnp.sum(key_raw * key_weight.astype(F32), axis=1)
+        + jnp.sum(value_raw * value_weight.astype(F32), axis=1)
+    )
+    gate_raw, up_raw, down_raw = join(gate_raw), join(up_raw), join(down_raw)
+    gain_two_sum = jnp.sum(gate_raw * gate_weight.astype(F32) + up_raw * up_weight.astype(F32), axis=1)
+    bias_total = jnp.sum(bias_sum.reshape(LINES, 2, -1), axis=0)
+    query_bias_all = bias_total[:, :half].reshape(-1)
+    key_bias_all = bias_total[:, half : half + HD].reshape(-1)
+    value_bias_all = bias_total[:, half + HD :].reshape(-1)
+    return (
+        block_output,
+        token_grad,
+        gain_one_sum,
+        query_raw * gain_one,
+        lax.dynamic_slice(query_bias_all, (me * rows,), (rows,)),
+        key_raw * gain_one,
+        key_bias_all,
+        value_raw * gain_one,
+        lax.dynamic_slice(value_bias_all, (me * value_bias.shape[0],), (value_bias.shape[0],)),
+        jnp.concatenate(sides(pieces_out), axis=1),
+        gain_two_sum,
+        gate_raw * gain_two,
+        up_raw * gain_two,
+        down_raw,
+    )
+
+
+def layer(*args):
+    tokens, query_weight, key_weight, gate_weight = args[0], args[4], args[6], args[12]
+    rows, width = query_weight.shape
+    fits = (
+        lax.axis_size(AXIS) == 4 * GROUP
+        and rows % 16 == 0
+        and rows * lax.axis_size(AXIS) == width
+        and width == H * HD
+        and key_weight.shape[1] == KV * HD
+        and KV == 2
+        and tokens.shape[0] == 128
+        and gate_weight.shape[1] % 128 == 0
+    )
+    return kernel_body(*args) if fits else array_body(*args)
+
+
 def solution(mesh):
     split = P(AXIS)
     split_rows = P(AXIS, None)
     return jax.shard_map(
-        array_body,
+        layer,
         mesh=mesh,
         in_specs=(
             split_rows, split, split, split, split_rows, split, split_rows, split,

time: 832 us -> 407 us (0.49); the launches traced: 821 us -> 406 us
  Pallas kernels: 0 us -> 385 us
  waiting for transfers between devices: 366 us -> 0 us
  blocking collectives: 192 us -> 0 us
  matrix products: 90 us -> 0 us
  local copies, waits for them, and re-layouts: 76.3 us -> 5.45 us
  starting transfers between devices: 40.6 us -> 0 us
  other arithmetic: 41.3 us -> 14.5 us
  between operations: 15.1 us -> 1.02 us
    pallas_call x0 -> x1, Pallas kernels: none -> 385 us  [kernel_call(): pl.pallas_call(functools.partial(mega, rows, plane), out_shape=out_shape,...]
    all_to_all x6 -> x0, waiting for transfers between devices: 159 us -> none  [the longest x3 97.7 us: fold_feed(): lax.all_to_all(pieces.reshape(plane, GROUP * rows, shard), AXIS, split_ax...]
    all_gather x6 -> x0, waiting for transfers between devices: 146 us -> none  [the longest x3 85.4 us: spread(): lax.all_gather(got, AXIS, axis=0, tiled=False, axis_index_groups=plane_gr...]
    all_to_all x3 -> x0, blocking collectives: 116 us -> none  [spread(): lax.all_to_all(pieces, AXIS, split_axis=0, concat_axis=0, tiled=True, axi...]
    dot_general x20 -> x0, matrix products: 89.5 us -> none  [the longest x15 87.5 us: dot(): lax.dot_general(left, right, ((dims[:1], dims[1:]), ((), ())), preferred_...]
    reduce_scatter x3 -> x0, waiting for transfers between devices: 61.1 us -> none  [the longest x2 61.1 us: fold_tokens(): lax.psum_scatter(term.astype(BF16), AXIS, scatter_dimension=0, tiled=True...]
    unnamed x1 -> x0, blocking collectives: 38.5 us -> none
    psum x1 -> x0, blocking collectives: 37 us -> none  [array_body(): bias_sum = lax.psum(jnp.sum(input_low, axis=0, dtype=F32), AXIS)]
  transfers between devices with their start and end apart: 15 -> 0, of which waited for: 12 -> 0; matrix products, arithmetic and copies ran while one was open for 19% -> 0% of each run, Pallas kernels for 0% -> 0%
where the time goes in v2:
time: 407 us; the launch traced here: 406 us
  Pallas kernels  385 us (95%)
  other arithmetic  14.5 us (4%)
  local copies, waits for them, and re-layouts  5.45 us (1%)
    pallas_call x1, Pallas kernels, kernel_call(): pl.pallas_call(functools.partial(mega, rows, plane), out_shape=out_shape,...  385 us

profile of v2, /device:TPU:0, one launch (start us, length us, event | category | flops | bytes accessed | tf_op | source)
XLA Modules:
  0.0 406.3 jit_solution(5503784739563980132)
XLA Ops:
  0.6 0.7 convert_bitcast_fusion
  1.3 0.7 convert_element_type.65
  2.0 0.7 convert_element_type.64
  2.6 0.6 stack.23.refs_2_
  3.3 0.7 convert_dynamic-update-slice_fusion
  4.0 0.7 convert_dynamic-update-slice_fusion.1
  4.7 0.7 convert_dynamic-update-slice_fusion.2
  5.5 0.6 broadcast_in_dim.10.refs_3_
  6.1 385.3 %layer.1 = (bf16[8,48,1024]{2,1,0:T(8,128)(2,1)}, bf16[8,48,768]{2,1,0:T(8,128)(2,1)}, bf16[8,48,1152]{2,1,0:T(8,128)(2,1)}, bf16[8,48,1152]{2,1,0:T(8,128)(2,1)...) custom-call(bf16[128,1536]{1,0:T(8,128)(2,1)} %refs_0_.1, ...), custom_call_target="tpu_custom_call" | custom-call | tf_op jit(solution)/shard_map/layer/pallas_call | solution.py:853
  391.5 0.0 copy-start.13
  391.5 1.8 convert_reduce_fusion
  393.4 0.0 copy-start.10
  393.4 0.0 copy-start.11
  393.4 0.9 multiply_convert_fusion
  394.3 0.1 convert_reduce_fusion.1
  394.5 0.8 fusion.3
  395.4 0.9 fusion.2
  396.3 0.5 add_add_fusion
  396.8 0.1 reduce
  397.0 0.6 dynamic_slice.6
  397.5 0.6 slice_bitcast_fusion.7
  398.1 0.6 dynamic_slice.7
  398.7 0.1 convert_reduce_fusion.2
  398.8 0.7 pad_maximum_fusion.1
  399.6 0.0 copy-start
  399.6 0.0 copy-start.1
  399.8 0.3 copy-done.3
  400.2 0.6 copy-done
  400.8 0.3 copy-done.1
  401.1 3.0 convert_multiply_fusion
  404.2 1.3 convert_element_type.78
  405.6 0.7 copy.57
  (65 shorter events, 0.6 us)
Async XLA Ops:
  391.5 1.9 copy-start.13
  391.5 1.9 copy-start.6
  391.5 2.8 copy-start.5
  393.4 1.1 copy-start.10
  393.4 1.1 copy-start.11
  394.2 1.1 copy-start.7
  394.2 2.5 copy-start.12
  394.3 4.4 %copy-start.8 = (bf16[8,48,768]{2,1,0:T(8,128)(2,1)S(1)}, bf16[8,48,768]{2,1,0:T(8,128)(2,1)}, u32[]{:S(2)}) copy-start(bf16[8,48,768]{2,1,0:T(8,128)(2,1)} %get-tuple-element.28) | copy-start | bytes 1769476
  395.3 4.2 %copy-start.4 = (bf16[8,48,1152]{2,1,0:T(8,128)(2,1)S(1)}, bf16[8,48,1152]{2,1,0:T(8,128)(2,1)}, u32[]{:S(2)}) copy-start(bf16[8,48,1152]{2,1,0:T(8,128)(2,1)} %get-tuple-element.30) | copy-start | bytes 2654212
  398.8 1.3 copy-start.3
  399.6 1.2 copy-start
  399.6 1.5 copy-start.1
  401.1 3.0 copy-start.2
  404.2 1.4 copy-start.9

commit v3 on v1

--- a/solution.py
+++ b/solution.py
@@ -1,14 +1,18 @@
+import functools
 import math
 
 import jax
 import jax.numpy as jnp
 from jax import lax
+from jax.experimental import pallas as pl
+from jax.experimental.pallas import tpu as pltpu
 from jax.sharding import PartitionSpec as P
 
 H = 12
 KV = 2
 HD = 128
 GROUP = 8
+LINES = GROUP // 2
 
 EPSILON = 1e-06
 ROPE_BASE = 1000000.0
@@ -227,11 +231,827 @@
     )
 
 
+def mega(rows, plane, *refs):
+    (
+        x_in, cot_in, aux_in, bias_in, wq_in, wk_in, wv_in, wo_in, wg_in, wu_in, wd_in,
+        o1, o2, o3, o4, o5, fo_out, bg_out, tg_out, h_out,
+        xs, xh, aux, sa, wgs, wus, w1, w2, w3, w4, w5, g5,
+        r1, r2, r3, r4, hn, gb, gt, up, act, pb, rb, rt,
+        zb, zr, dh, dz, ob, qr, kr, vr, pr, dob, dq, cos, sin, msk, ba, bp, bgp, bsum,
+        lsem, a_s, a_r, p_s, p_r, r_s, r_r, o_s, o_r, t_s, t_r, d_s, d_r, b_s, b_r, e_s, e_r, credit, pair_credit, line_credit,
+    ) = refs
+    weights = (w1, w2, w3, w4, w5)
+    grads = (w1, w2, w3, w4, g5)
+    landing = (r1, r2, r3, r4, r4)
+    outs = (o1, o2, o3, o4, o5)
+    block, width = x_in.shape
+    shard = w3.shape[1]
+    half = w2.shape[1]
+    heads = half // HD
+    strip = width // LINES
+    hidden = wg_in.shape[1]
+    short = GROUP * shard - hidden
+    factor = 1.0 / math.sqrt(HD)
+
+    me = lax.axis_index(AXIS)
+    c = lax.rem(me, 2)
+    p = lax.rem(lax.div(me, 2), plane)
+    z = lax.div(me, 2 * plane)
+    f = z * 2 + c
+    xbit, ybit = lax.rem(p, 2), lax.div(p, 2)
+    px = p + 1 - 2 * xbit
+    py = p + 2 - 4 * ybit
+    pd = px + 2 - 4 * ybit
+    zlow, zhigh = lax.rem(z, 2), lax.div(z, 2)
+    inner = zlow + zhigh - 2 * zlow * zhigh
+
+    def flip(bit, on):
+        return bit + on - 2 * bit * on
+
+    def zf(high, low):
+        return flip(zhigh, high) * 2 + flip(zlow, low)
+
+    def zj(j):
+        if isinstance(j, int):
+            return zf(j // 2, j % 2)
+        return zf(lax.div(j, 2), lax.rem(j, 2))
+
+    def dev(zz, pp, cc):
+        return (zz * plane + pp) * 2 + cc
+
+    sib, xnb, ynb = dev(z, p, 1 - c), dev(z, px, c), dev(z, py, c)
+
+    def unit(zz, pp):
+        return pl.ds(pl.multiple_of((zz * plane + pp) * 2 * rows, 16), 2 * rows)
+
+    def piece(zz, pp, cc):
+        return pl.ds(pl.multiple_of(((zz * plane + pp) * 2 + cc) * rows, 16), rows)
+
+    def slot(s):
+        return pl.ds(pl.multiple_of(s * 2 * rows, 16), 2 * rows)
+
+    def tokens_of(zz, cc):
+        return pl.ds(pl.multiple_of((zz * 2 + cc) * block, block), block)
+
+    def chunk_of(zz):
+        return pl.ds(pl.multiple_of(zz * 2 * block, 2 * block), 2 * block)
+
+    def remote(src, dst, send, recv, target):
+        return pltpu.make_async_remote_copy(
+            src_ref=src, dst_ref=dst, send_sem=send, recv_sem=recv,
+            device_id=(target,), device_id_type=pl.DeviceIdType.MESH,
+        )
+
+    def dot_nn(a, b):
+        return lax.dot_general(a, b, (((1,), (0,)), ((), ())), preferred_element_type=F32)
+
+    def dot_nt(a, b):
+        return lax.dot_general(a, b, (((1,), (1,)), ((), ())), preferred_element_type=F32)
+
+    def dot_tn(a, b):
+        return lax.dot_general(a, b, (((0,), (0,)), ((), ())), preferred_element_type=F32)
+
+    pending = {}
+
+    def begin(key, copy, leave=True, arrive=True):
+        copy.start()
+        if leave:
+            pending[key + ("leave",)] = copy.wait_send
+        if arrive:
+            pending[key + ("arrive",)] = copy.wait_recv
+
+    def begin_local(key, copy):
+        copy.start()
+        pending[key] = copy.wait
+
+    def settle(*keys):
+        for key in keys:
+            pending.pop(key)()
+
+    def settle_all(match):
+        settle(*[key for key in pending if match(key)])
+
+    def local(n, src, dst):
+        return pltpu.make_async_copy(src, dst, lsem.at[n])
+
+    def signal(semaphore, target):
+        pl.semaphore_signal(semaphore, inc=1, device_id=(target,), device_id_type=pl.DeviceIdType.MESH)
+
+    def source(k, ff, cc):
+        if k == 0:
+            return sa.at[cc]
+        if k == 1:
+            return wo_in.at[:, pl.ds(pl.multiple_of(cc * half, 128), half)]
+        start = pl.multiple_of((ff * (shard // 128) - lax.div(ff, GROUP - 1) * (short // 128)) * 128, 128)
+        return (wgs, wus, wd_in)[k - 2].at[:, pl.ds(start, shard)]
+
+    def a_copy(k, j):
+        zz, cc = zj(j // 2), flip(c, j % 2)
+        return remote(
+            source(k, zz * 2 + cc, cc), weights[k].at[piece(z, p, c)], a_s.at[k, j], a_r.at[k, j], dev(zz, p, cc)
+        )
+
+    def a_send(k):
+        begin_local(("a_own", k), local(11 + k, source(k, f, c), weights[k].at[piece(z, p, c)]))
+        for j in range(1, GROUP):
+            begin(("a", k, j), a_copy(k, j))
+
+    def a_wait(k, jz):
+        settle(("a_own", k) if jz == 0 else ("a", k, 2 * jz, "arrive"), ("a", k, 2 * jz + 1, "arrive"))
+
+    def ag_copy(k, s):
+        j = s % 4
+        if s < 4:
+            part, target = unit(zj(j), p), xnb
+        elif s < 8:
+            part, target = unit(zj(j), p), ynb
+        elif j < 2:
+            part, target = unit(zj(j), px), ynb
+        else:
+            part, target = unit(zj(j), py), xnb
+        return remote(weights[k].at[part], weights[k].at[part], p_s.at[k, s], p_r.at[k, s], target)
+
+    def ag_send(k):
+        for j in range(LINES):
+            a_wait(k, j)
+            begin(("ag", k, j), ag_copy(k, j))
+            begin(("ag", k, 4 + j), ag_copy(k, 4 + j))
+
+    def ag_relay(k):
+        for j in range(4):
+            settle(("ag", k, j if j < 2 else 4 + j, "arrive"))
+            begin(("ag", k, 8 + j), ag_copy(k, 8 + j))
+
+    def ag_finish(k):
+        for s in (2, 3, 4, 5, 8, 9, 10, 11):
+            settle(("ag", k, s, "arrive"))
+
+    def ag_sent(k):
+        settle_all(lambda key: key[:2] == ("ag", k) and key[-1] == "leave")
+
+    def tok_copy(which, kind, j):
+        buf = (hn, gb)[which]
+        part = tokens_of(zj(0 if kind == "own" else j), c)
+        if kind == "own":
+            send, recv, target = j, j, dev(zj(j), p, c)
+        elif kind == "pair":
+            send, recv, target = 4 + j, 4 + j, sib
+        else:
+            send, recv, target = 6 + j, 5 - j, dev(zj(1), p, c)
+        return remote(buf.at[part], buf.at[part], t_s.at[which, send], t_r.at[which, recv], target)
+
+    def tok_send(which):
+        begin(("tok", which, 1), tok_copy(which, "own", 1))
+        begin(("tok", which, 2), tok_copy(which, "own", 2 + inner))
+        pending["tok", which, 3, "arrive"] = lambda: tok_copy(which, "own", 3 - inner).wait_recv()
+        begin(("pair", which, 0), tok_copy(which, "pair", 0))
+
+    def tok_forward(which):
+        for n, j in ((1, 1), (2, 2 + inner), (3, 3 - inner)):
+            settle(("tok", which, n, "arrive"))
+            if n > 1:
+
+                @pl.when(inner == 1)
+                def _(j=j):
+                    tok_copy(which, "pass", j).start()
+
+            begin(("pair", which, n), tok_copy(which, "pair", j))
+
+        def passed():
+            @pl.when(inner == 1)
+            def _():
+                for j in (2, 3):
+                    tok_copy(which, "pass", j).wait_send()
+
+        pending["pass", which, "leave"] = passed
+
+    def tok_finish(which):
+        for n in range(4):
+            settle(("pair", which, n, "arrive"))
+
+    def e_copy(n, src, dst):
+        return remote(src, dst, e_s.at[n], e_r.at[n], sib)
+
+    own_rows = pl.ds(pl.multiple_of(c * block, block), block)
+
+    def bias_in_copy(s):
+        zz, cc = zj(s // 2), flip(c, s % 2)
+        return remote(bias_in.at[cc], ba.at[f], b_s.at[s], b_r.at[s], dev(zz, p, cc))
+
+    def bias_plane_copy(base, n, buf):
+        target = dev(z, (px, py, pd)[n], c)
+        return remote(buf.at[p], buf.at[p], b_s.at[base + n], b_r.at[base + n], target)
+
+    def bias_out_copy(s):
+        zz, cc = zj(s // 2), flip(c, s % 2)
+        return remote(bsum, bg_out.at[f], b_s.at[16 + s], b_r.at[16 + s], dev(zz, p, cc))
+
+    def rs_copy(k, s, h):
+        ref = grads[k]
+        zz = zf((0, 1, 1, 0, 0, 1)[s], h)
+        part = unit(zz, (pd, pd, px, py, px, py)[s])
+        place = (0, 2, 6, 8, 4, 10)[s] + h
+        target = (ynb, xnb, xnb, ynb, xnb, ynb)[s]
+        return remote(ref.at[part], landing[k].at[slot(place)], r_s.at[k, place], r_r.at[k, place], target)
+
+    def rs_note(k, kinds):
+        for s in kinds:
+            for h in range(2):
+                pending["rs", k, s, h, "leave"] = lambda s=s, h=h: rs_copy(k, s, h).wait_send()
+                pending["rs", k, s, h, "arrive"] = lambda s=s, h=h: rs_copy(k, s, h).wait_recv()
+
+    def rs_start(k, left_ref, right_ref):
+        @pl.loop(0, 2)
+        def both(i):
+            h = 1 - i
+            for high in (1, 0):
+                zz = zf(high, h)
+                at = pl.multiple_of(zz * strip, 128)
+                left = left_ref[:, pl.ds(at, strip)]
+                grads[k][pl.ds(at, strip), :] = dot_tn(left, right_ref[...]).astype(BF16)
+                for s in ((0, 3), (1, 2))[high]:
+                    rs_copy(k, s, h).start()
+
+        rs_note(k, (0, 1, 2, 3))
+
+    def rs_middle(k):
+        @pl.loop(0, 2)
+        def both(i):
+            h = 1 - i
+            for high in (1, 0):
+                rs_copy(k, high, h).wait_recv()
+                part = unit(zf(high, h), (px, py)[high])
+                got = landing[k][slot(2 * high + h)]
+                grads[k][part] = (grads[k][part].astype(F32) + got.astype(F32)).astype(BF16)
+                rs_copy(k, 4 + high, h).start()
+
+        for s in (0, 1):
+            for h in range(2):
+                pending.pop(("rs", k, s, h, "arrive"))
+        rs_note(k, (4, 5))
+
+    def out_copy(k, j, other):
+        zz, cc = zj(j), flip(c, other)
+        return remote(
+            grads[k].at[piece(zz, p, cc)], outs[k].at[f], o_s.at[k, 2 * j + other], o_r.at[k, 2 * j + other], dev(zz, p, cc)
+        )
+
+    def rs_finish(k):
+        for j in (3, 1, 2, 0):
+            h, high = j % 2, j // 2
+            settle(("rs", k, (4, 2)[high], h, "arrive"), ("rs", k, (3, 5)[high], h, "arrive"))
+            part = unit(zj(j), p)
+            got = landing[k][slot(4 + j)].astype(F32) + landing[k][slot(8 + j)].astype(F32)
+            grads[k][part] = (grads[k][part].astype(F32) + got).astype(BF16)
+            begin(("out", k, j, 1), out_copy(k, j, 1))
+            if j == 0:
+                begin_local(("out_own", k), local(17 + k, grads[k].at[piece(z, p, c)], outs[k].at[f]))
+            else:
+                begin(("out", k, j, 0), out_copy(k, j, 0))
+
+    def pair_copy(which, j):
+        return remote(
+            pb.at[tokens_of(zj(j), 1 - c)], rb.at[pl.ds(pl.multiple_of(j * block, block), block)],
+            d_s.at[which, j], d_r.at[which, j], sib,
+        )
+
+    def line_copy(which, j):
+        dst = fo_out.at[1] if which == 1 and isinstance(j, int) and j == 1 else rt.at[j - 1]
+        return remote(
+            pb.at[tokens_of(zj(j), c)], dst, d_s.at[which, 4 + j], d_r.at[which, 4 + j], dev(zj(1), p, c)
+        )
+
+    def far_copy(which, j):
+        dst = fo_out.at[2] if which == 1 else rt.at[3]
+        return remote(pb.at[tokens_of(zj(j), c)], dst, d_s.at[which, 6 + j], d_r.at[which, 4], dev(zj(j), p, c))
+
+    def far_add(which, j):
+        @pl.when(inner == 1)
+        def _():
+            line_copy(which, 5 - j).wait_recv()
+            part = tokens_of(zj(j), c)
+            pb[part] = (pb[part].astype(F32) + rt[4 - j].astype(F32)).astype(BF16)
+            far_copy(which, j).start()
+
+    def pair_add(which, j):
+        pair_copy(which, j).wait_recv()
+        part = tokens_of(zj(j), c)
+        got = rb[pl.ds(pl.multiple_of(j * block, block), block)].astype(F32)
+        pb[part] = (pb[part].astype(F32) + got).astype(BF16)
+
+    def sum_loop(which, compute):
+        @pl.loop(0, LINES)
+        def chunk(i):
+            j = LINES - 1 - i
+            compute(chunk_of(zj(j)))
+            pair_copy(which, j).start()
+
+            @pl.when((i > 0) & (i < LINES - 1))
+            def _():
+                pair_add(which, j + 1)
+
+                @pl.when(inner == 0)
+                def _():
+                    line_copy(which, j + 1).start()
+
+            @pl.when(i == LINES - 1)
+            def _():
+                pair_add(which, 1)
+                line_copy(which, 1).start()
+
+        pair_add(which, 0)
+
+        def sent():
+            for j in range(LINES):
+                pair_copy(which, j).wait_send()
+            line_copy(which, 1).wait_send()
+            for j in (2, 3):
+                @pl.when(inner == 0)
+                def _():
+                    line_copy(which, j).wait_send()
+
+                @pl.when(inner == 1)
+                def _():
+                    far_copy(which, j).wait_send()
+
+        pending["sum", which, "leave"] = sent
+        pending["sum", which, 1, "arrive"] = lambda: line_copy(which, 1).wait_recv()
+        pending["sum", which, 2, "arrive"] = lambda: far_copy(which, 2).wait_recv()
+
+    def rope(v, b):
+        return v * cos[b] + pltpu.roll(v, HD // 2, 1) * sin[b]
+
+    def rope_back(v, b):
+        return v * cos[b] + pltpu.roll(v * sin[b], HD // 2, 1)
+
+    row_id = lax.broadcasted_iota(jnp.int32, (block, block), 0)
+    lane_id = lax.broadcasted_iota(jnp.int32, (block, block), 1)
+
+    def column(row):
+        return jnp.sum(jnp.where(row_id == lane_id, row, 0.0), axis=1, keepdims=True)
+
+    tile = 3 * HD
+    last = lax.div(f, GROUP - 1)
+    keep = jnp.where(lax.broadcasted_iota(jnp.int32, (1, tile), 1) < last * short, 0.0, 1.0)
+
+    def enter():
+        begin_local(("aux",), local(0, aux_in, aux.at[c]))
+        begin_local(("x",), local(1, x_in, xs.at[c]))
+        for side in range(2):
+            begin_local(("wq", side), local(2 + side, wq_in.at[:, pl.ds(side * half, half)], sa.at[side, :, pl.ds(0, half)]))
+            begin_local(("wk", side), local(4 + side, wk_in.at[:, pl.ds(side * HD, HD)], sa.at[side, :, pl.ds(half, HD)]))
+            begin_local(("wv", side), local(6 + side, wv_in.at[:, pl.ds(side * HD, HD)], sa.at[side, :, pl.ds(half + HD, HD)]))
+        begin_local(("wg",), local(8, wg_in, wgs))
+        begin_local(("wu",), local(9, wu_in, wus))
+        begin_local(("cot",), local(10, cot_in, gb.at[tokens_of(z, c)]))
+        barrier = pltpu.get_barrier_semaphore()
+        friends = [dev(zj(j // 2), p, flip(c, j % 2)) for j in range(1, GROUP)] + [xnb, ynb, dev(z, pd, c)]
+        for friend in friends:
+            signal(barrier, friend)
+        settle(("aux",), ("x",), *[(name, side) for side in range(2) for name in ("wq", "wk", "wv")])
+        gain_one = column(aux[c][2:3])[:rows]
+        for side in range(2):
+            sa[side] = (sa[side].astype(F32) * gain_one).astype(BF16)
+        pl.semaphore_wait(barrier, len(friends))
+
+    def exchange_inputs():
+        begin(("e", 0), e_copy(0, aux.at[c], aux.at[c]))
+        begin(("e", 1), e_copy(1, xs.at[c], xs.at[c]))
+
+    def bias_first():
+        begin_local(("bias_own",), local(16, bias_in.at[c], ba.at[f]))
+        for s in range(1, GROUP):
+            begin(("bias_in", s), bias_in_copy(s))
+
+    def bias_second():
+        settle(("bias_own",), *[("bias_in", s, "arrive") for s in range(1, GROUP)])
+        total = ba[0]
+        for s in range(1, GROUP):
+            total = total + ba[s]
+        bp[p] = total
+        for n in range(3):
+            begin(("bias_plane", n), bias_plane_copy(8, n, bp))
+
+    def scale_feed():
+        gain_two = column(aux[c][3:4])[:rows]
+        for name, ref in (("wg", wgs), ("wu", wus)):
+            settle((name,))
+            for n in range(0, hidden, 1792):
+                cols = pl.ds(n, min(1792, hidden - n))
+                ref[:, cols] = (ref[:, cols].astype(F32) * gain_two).astype(BF16)
+
+    def mask_upstream():
+        settle(("cot",))
+        live = jnp.where(column(aux[c][1:2]) >= 0.0, 1.0, 0.0)
+        gb[tokens_of(z, c)] = (gb[tokens_of(z, c)].astype(F32) * live).astype(BF16)
+
+    def norm_tokens():
+        settle(("e", 0, "arrive"), ("e", 1, "arrive"))
+        lanes = lax.broadcasted_iota(jnp.int32, (1, HD), 1)
+        freq_index = jnp.where(lanes < HD // 2, lanes, lanes - HD // 2).astype(F32)
+        frequency = jnp.exp(freq_index * (-2.0 * math.log(ROPE_BASE) / HD))
+        for b in range(2):
+            values = xs[b].astype(F32)
+            scale = lax.rsqrt(jnp.mean(values * values, axis=1, keepdims=True) + EPSILON)
+            xh[pl.ds(b * block, block)] = (values * scale).astype(BF16)
+            info = aux[b]
+            angles = column(info[0:1]) * frequency
+            cos[b] = jnp.cos(angles)
+            sine = jnp.sin(angles)
+            sin[b] = jnp.where(lane_id < HD // 2, -sine, sine)
+            same = column(info[1:2]) == info[1:2]
+            msk[b] = jnp.where(same & (lane_id <= row_id), 1.0, 0.0)
+
+    def project():
+        settle(*[("bias_plane", n, "arrive") for n in range(3)])
+        bias_row = (bp[0] + bp[1]) + (bp[2] + bp[3])
+        for n in range(heads // 2 + 1):
+            cols = pl.ds(n * 2 * HD, 2 * HD)
+            out = dot_nn(xh[...], w1[:, cols]) + bias_row[:, n * 2 * HD : (n + 1) * 2 * HD]
+            for b in range(2):
+                part = out[b * block : (b + 1) * block]
+                if n < heads // 2:
+                    for i in range(2):
+                        qr[b, pl.ds((2 * n + i) * block, block)] = rope(part[:, i * HD : (i + 1) * HD], b).astype(BF16)
+                else:
+                    kr[b] = rope(part[:, :HD], b).astype(BF16)
+                    vr[b] = part[:, HD:].astype(BF16)
+
+    def attend():
+        for b in range(2):
+            scores = dot_nt(qr[b], kr[b]) * factor
+            scores = jnp.where(msk[b][None] > 0.0, scores.reshape(heads, block, block), -jnp.inf)
+            weight = jnp.exp(scores - jnp.max(scores, axis=-1, keepdims=True))
+            weight = weight / jnp.sum(weight, axis=-1, keepdims=True)
+            weight = weight.reshape(heads * block, block)
+            pr[b] = weight
+            mixed = dot_nn(weight.astype(BF16), vr[b]).astype(BF16)
+            for i in range(heads):
+                ob[pl.ds(b * block, block), pl.ds(i * HD, HD)] = mixed[i * block : (i + 1) * block]
+
+    def attend_out():
+        for n in range(0, width, 512):
+            part = dot_nt(ob[...], w2[pl.ds(n, 512), :])
+            zb[0, :, pl.ds(n, 512)] = part[:block]
+            zb[1, :, pl.ds(n, 512)] = part[block:]
+        begin(("e", 2), e_copy(2, zb.at[1 - c], zr))
+
+    def hidden_state():
+        settle(("e", 2, "arrive"))
+        state = xs[c].astype(F32) + zb[c] + zr[...]
+        h_out[...] = state
+        scale_two = lax.rsqrt(jnp.mean(state * state, axis=1, keepdims=True) + EPSILON)
+        hn[tokens_of(z, c)] = (state * scale_two).astype(BF16)
+
+    def feed_forward():
+        @pl.loop(0, LINES)
+        def chunk(i):
+            rows_here = chunk_of(i)
+            left = hn[rows_here]
+            for n in range(0, shard, tile):
+                cols = pl.ds(n, tile)
+                gate = dot_nn(left, w3[:, cols])
+                lift = dot_nn(left, w4[:, cols])
+                if n == 0:
+                    gate = gate * keep
+                    lift = lift * keep
+                gt[rows_here, cols] = gate.astype(BF16)
+                up[rows_here, cols] = lift.astype(BF16)
+                act[rows_here, cols] = (gate * jax.nn.sigmoid(gate) * lift).astype(BF16)
+
+    def feed_backward():
+        def compute(rows_here):
+            left = gb[rows_here]
+            for n in range(0, shard, tile):
+                cols = pl.ds(n, tile)
+                d_act = dot_nn(left, w5[:, cols])
+                gate = gt[rows_here, cols].astype(F32)
+                lift = up[rows_here, cols].astype(F32)
+                sig = jax.nn.sigmoid(gate)
+                gt[rows_here, cols] = (d_act * lift * sig * (1.0 + gate * (1.0 - sig))).astype(BF16)
+                up[rows_here, cols] = (d_act * gate * sig).astype(BF16)
+            for n in range(0, width, 512):
+                part = pl.ds(n, 512)
+                back = dot_nt(gt[rows_here], w3[part, :]) + dot_nt(up[rows_here], w4[part, :])
+                pb[rows_here, part] = back.astype(BF16)
+
+        sum_loop(0, compute)
+        signal(pair_credit, sib)
+
+    def line_ready():
+        @pl.when(inner == 1)
+        def _():
+            signal(line_credit, dev(zj(1), p, c))
+
+    def feed_output():
+        settle(("sum", 0, "leave"))
+        pl.semaphore_wait(pair_credit, 1)
+
+        @pl.when(inner == 0)
+        def _():
+            pl.semaphore_wait(line_credit, 1)
+
+        def compute(rows_here):
+            for n in range(0, width, 512):
+                part = pl.ds(n, 512)
+                pb[rows_here, part] = dot_nt(act[rows_here], w5[part, :]).astype(BF16)
+
+        sum_loop(1, compute)
+        begin_local(("fo_own",), local(22, pb.at[tokens_of(z, c)], fo_out.at[0]))
+
+    def landing_free():
+        for target in (xnb, ynb):
+            signal(credit, target)
+
+    def landing_wait():
+        pl.semaphore_wait(credit, 2)
+
+    def hidden_gradient():
+        settle(("sum", 0, 1, "arrive"), ("sum", 0, 2, "arrive"))
+        weighted = pb[tokens_of(z, c)].astype(F32) + rt[0].astype(F32) + rt[3].astype(F32)
+        state = h_out[...]
+        scale_two = lax.rsqrt(jnp.mean(state * state, axis=1, keepdims=True) + EPSILON)
+        spread = jnp.mean(weighted * state, axis=1, keepdims=True)
+        grad = (
+            gb[tokens_of(z, c)].astype(F32)
+            + scale_two * weighted
+            - state * (scale_two * scale_two * scale_two) * spread
+        )
+        dh[...] = grad
+        dz[own_rows] = grad.astype(BF16)
+        begin(("e", 3), e_copy(3, dz.at[own_rows], dz.at[own_rows]))
+
+    def attend_out_back():
+        settle(("e", 3, "arrive"))
+        for n in range(0, heads, 2):
+            part = dot_nn(dz[...], w2[:, pl.ds(n * HD, 2 * HD)]).astype(BF16)
+            for b in range(2):
+                for i in range(2):
+                    dob[b, pl.ds((n + i) * block, block)] = part[b * block : (b + 1) * block, i * HD : (i + 1) * HD]
+
+    def attend_back():
+        for b in range(2):
+            weight = pr[b]
+            d_weight = dot_nt(dob[b], vr[b])
+            d_score = weight * (d_weight - jnp.sum(weight * d_weight, axis=-1, keepdims=True))
+            d_score = d_score.astype(BF16)
+            d_query = dot_nn(d_score, kr[b]) * factor
+            here = pl.ds(b * block, block)
+            for i in range(heads):
+                dq[here, pl.ds(i * HD, HD)] = rope_back(d_query[i * block : (i + 1) * block], b).astype(BF16)
+            dq[here, pl.ds(half, HD)] = rope_back(dot_tn(d_score, qr[b]) * factor, b).astype(BF16)
+            dq[here, pl.ds(half + HD, HD)] = dot_tn(weight.astype(BF16), dob[b]).astype(BF16)
+
+    def project_back():
+        settle(("e", 2, "leave"))
+        for n in range(0, width, 512):
+            part = dot_nt(dq[...], w1[pl.ds(n, 512), :])
+            zb[0, :, pl.ds(n, 512)] = part[:block]
+            zb[1, :, pl.ds(n, 512)] = part[block:]
+        begin(("e", 4), e_copy(4, zb.at[1 - c], zr))
+
+    def bias_back():
+        bgp[p] = jnp.sum(dq[...].astype(F32), axis=0, keepdims=True)
+        for n in range(3):
+            begin(("bias_back", n), bias_plane_copy(11, n, bgp))
+
+    def bias_last():
+        settle(*[("bias_back", n, "arrive") for n in range(3)])
+        bsum[...] = (bgp[0] + bgp[1]) + (bgp[2] + bgp[3])
+        begin_local(("bias_sum",), local(23, bsum, bg_out.at[f]))
+        for s in range(1, GROUP):
+            begin(("bias_out", s), bias_out_copy(s))
+
+    def token_gradient():
+        settle(("e", 4, "arrive"))
+        weighted = zb[c] + zr[...]
+        values = xs[c].astype(F32)
+        scale = lax.rsqrt(jnp.mean(values * values, axis=1, keepdims=True) + EPSILON)
+        spread = jnp.mean(weighted * values, axis=1, keepdims=True)
+        tg_out[...] = (dh[...] + scale * weighted - values * (scale * scale * scale) * spread).astype(BF16)
+
+    enter()
+    exchange_inputs()
+    a_send(0)
+    bias_first()
+    a_send(1)
+    scale_feed()
+    mask_upstream()
+    ag_send(0)
+    a_send(2)
+    norm_tokens()
+    ag_relay(0)
+    bias_second()
+    ag_send(1)
+    a_send(3)
+    ag_finish(0)
+    project()
+    ag_relay(1)
+    ag_send(2)
+    attend()
+    ag_finish(1)
+    attend_out()
+    hidden_state()
+    tok_send(0)
+    ag_send(3)
+    a_send(4)
+    tok_send(1)
+    ag_relay(2)
+    ag_relay(3)
+    tok_forward(0)
+    ag_send(4)
+    tok_finish(0)
+    ag_finish(2)
+    ag_finish(3)
+    feed_forward()
+    ag_relay(4)
+    tok_forward(1)
+    ag_finish(4)
+    tok_finish(1)
+    rs_start(4, gb, act)
+    feed_backward()
+    far_add(0, 2)
+    rs_middle(4)
+    ag_sent(2)
+    rs_start(2, hn, gt)
+    far_add(0, 3)
+    line_ready()
+    rs_finish(4)
+    landing_free()
+    ag_sent(3)
+    landing_wait()
+    rs_start(3, hn, up)
+    hidden_gradient()
+    rs_middle(2)
+    feed_output()
+    far_add(1, 2)
+    attend_out_back()
+    ag_sent(1)
+    rs_start(1, dz, ob)
+    far_add(1, 3)
+    rs_finish(2)
+    rs_middle(3)
+    attend_back()
+    project_back()
+    ag_sent(0)
+    rs_start(0, xh, dq)
+    rs_middle(1)
+    rs_finish(3)
+    bias_back()
+    token_gradient()
+    rs_finish(1)
+    bias_last()
+    rs_middle(0)
+    rs_finish(0)
+    settle(*list(pending))
+
+
+def kernel_call(rows, plane, block, width, hidden, aux, bias, tokens, cotangent, *weights):
+    half = width // 2
+    blocks = hidden // 128
+    shard = -(-blocks // GROUP) * 128
+    inner = half + 2 * HD
+    heads = half // HD
+    columns = (inner, half, shard, shard, shard)
+    dma = pltpu.SemaphoreType.DMA
+    vm = pltpu.VMEM
+    group_tokens = GROUP * block
+    any_space = pl.BlockSpec(memory_space=pl.ANY)
+    vmem_space = pl.BlockSpec(memory_space=pltpu.VMEM)
+    out_shape = [jax.ShapeDtypeStruct((GROUP, rows, n), BF16) for n in columns]
+    out_shape += [
+        jax.ShapeDtypeStruct((3, block, width), BF16),
+        jax.ShapeDtypeStruct((GROUP, 1, inner), F32),
+        jax.ShapeDtypeStruct((block, width), BF16),
+        jax.ShapeDtypeStruct((block, width), F32),
+    ]
+    scratch = [
+        vm((2, block, width), BF16), vm((2 * block, width), BF16), vm((2, 8, 128), F32), vm((2, rows, inner), BF16),
+        vm((rows, hidden), BF16), vm((rows, hidden), BF16),
+    ]
+    scratch += [vm((width, n), BF16) for n in columns] + [vm((width, shard), BF16)]
+    scratch += [vm((12 * 2 * rows, n), BF16) for n in columns[:4]]
+    scratch += [vm((group_tokens, width), BF16)] * 2 + [vm((group_tokens, shard), BF16)] * 3
+    scratch += [
+        vm((group_tokens, width), BF16), vm((LINES * block, width), BF16), vm((LINES, block, width), BF16),
+        vm((2, block, width), F32), vm((block, width), F32), vm((block, width), F32), vm((2 * block, width), BF16),
+        vm((2 * block, half), BF16), vm((2, heads * block, HD), BF16), vm((2, block, HD), BF16), vm((2, block, HD), BF16),
+        vm((2, heads * block, block), F32), vm((2, heads * block, HD), BF16), vm((2 * block, inner), BF16),
+        vm((2, block, HD), F32), vm((2, block, HD), F32), vm((2, block, block), F32),
+        vm((GROUP, 1, inner), F32), vm((4, 1, inner), F32), vm((4, 1, inner), F32), vm((1, inner), F32),
+    ]
+    scratch += [dma((24,))]
+    scratch += [dma((5, 8))] * 2 + [dma((5, 12))] * 4 + [dma((5, 8))] * 2 + [dma((2, 12))] * 4 + [dma((24,))] * 2 + [dma((8,))] * 2
+    scratch += [pltpu.SemaphoreType.REGULAR] * 3
+    return pl.pallas_call(
+        functools.partial(mega, rows, plane),
+        out_shape=out_shape,
+        in_specs=[any_space] * 11,
+        out_specs=[any_space] * 7 + [vmem_space] * 2,
+        scratch_shapes=scratch,
+        compiler_params=pltpu.CompilerParams(
+            collective_id=0, has_side_effects=True, vmem_limit_bytes=64 * 2**20 - 2**17
+        ),
+        name="layer",
+    )(tokens, cotangent, aux, bias, *weights)
+
+
+def kernel_body(
+    tokens, segment, position, first_gain, query_weight, query_bias, key_weight, key_bias, value_weight, value_bias,
+    out_weight, second_gain, gate_weight, up_weight, down_weight, cotangent,
+):
+    count = lax.axis_size(AXIS)
+    me = lax.axis_index(AXIS)
+    plane = count // GROUP
+    rows, width = query_weight.shape
+    block = tokens.shape[0]
+    hidden = gate_weight.shape[1]
+    key_width = key_weight.shape[1]
+    half = width // 2
+
+    def wide(v):
+        return jnp.pad(v.astype(F32), (0, 128 - v.shape[0]))
+
+    aux = jnp.stack([wide(position), wide(segment), wide(first_gain), wide(second_gain)] + [jnp.zeros((128,), F32)] * 4)
+
+    def placed(v):
+        full = jnp.zeros((v.shape[0] * count,), F32)
+        return lax.dynamic_update_slice(full, v.astype(F32), (me * v.shape[0],)).reshape(2, -1)
+
+    bias = jnp.concatenate([placed(query_bias), placed(key_bias), placed(value_bias)], axis=1)[:, None, :]
+    pieces_in, pieces_out, gate_raw, up_raw, down_raw, feed, bias_sum, token_grad, state = kernel_call(
+        rows, plane, block, width, hidden, aux, bias, tokens, cotangent,
+        query_weight, key_weight, value_weight, out_weight, gate_weight, up_weight, down_weight,
+    )
+    live_rows = (segment >= 0).astype(F32)[:, None]
+    gain_one = first_gain.astype(F32)[:, None]
+    gain_two = second_gain.astype(F32)[:, None]
+    block_output = (live_rows * (state + jnp.sum(feed.astype(F32), axis=0))).astype(BF16)
+
+    def sides(pieces):
+        total = jnp.sum(pieces.astype(F32).reshape(LINES, 2, rows, -1), axis=0)
+        return total[0], total[1]
+
+    def join(pieces):
+        shard = pieces.shape[2]
+        short = GROUP * shard - hidden
+        parts = [pieces[i] for i in range(GROUP - 1)] + [pieces[GROUP - 1][:, short:]]
+        return jnp.concatenate(parts, axis=1).astype(F32)
+
+    left, right = sides(pieces_in)
+    query_raw = jnp.concatenate([left[:, :half], right[:, :half]], axis=1)
+    key_raw = jnp.concatenate([left[:, half : half + HD], right[:, half : half + HD]], axis=1)
+    value_raw = jnp.concatenate([left[:, half + HD :], right[:, half + HD :]], axis=1)
+    gain_one_sum = (
+        jnp.sum(query_raw * query_weight.astype(F32), axis=1)
+        + jnp.sum(key_raw * key_weight.astype(F32), axis=1)
+        + jnp.sum(value_raw * value_weight.astype(F32), axis=1)
+    )
+    gate_raw, up_raw, down_raw = join(gate_raw), join(up_raw), join(down_raw)
+    gain_two_sum = jnp.sum(gate_raw * gate_weight.astype(F32) + up_raw * up_weight.astype(F32), axis=1)
+    bias_total = jnp.sum(bias_sum.reshape(LINES, 2, -1), axis=0)
+    query_bias_all = bias_total[:, :half].reshape(-1)
+    key_bias_all = bias_total[:, half : half + HD].reshape(-1)
+    value_bias_all = bias_total[:, half + HD :].reshape(-1)
+    return (
+        block_output,
+        token_grad,
+        gain_one_sum,
+        query_raw * gain_one,
+        lax.dynamic_slice(query_bias_all, (me * rows,), (rows,)),
+        key_raw * gain_one,
+        key_bias_all,
+        value_raw * gain_one,
+        lax.dynamic_slice(value_bias_all, (me * value_bias.shape[0],), (value_bias.shape[0],)),
+        jnp.concatenate(sides(pieces_out), axis=1),
+        gain_two_sum,
+        gate_raw * gain_two,
+        up_raw * gain_two,
+        down_raw,
+    )
+
+
+def layer(*args):
+    tokens, query_weight, key_weight, gate_weight = args[0], args[4], args[6], args[12]
+    rows, width = query_weight.shape
+    fits = (
+        lax.axis_size(AXIS) == 4 * GROUP
+        and rows % 16 == 0
+        and rows * lax.axis_size(AXIS) == width
+        and width == H * HD
+        and key_weight.shape[1] == KV * HD
+        and KV == 2
+        and tokens.shape[0] == 128
+        and gate_weight.shape[1] % 128 == 0
+    )
+    return kernel_body(*args) if fits else array_body(*args)
+
+
 def solution(mesh):
     split = P(AXIS)
     split_rows = P(AXIS, None)
     return jax.shard_map(
-        array_body,
+        layer,
         mesh=mesh,
         in_specs=(
             split_rows, split, split, split, split_rows, split, split_rows, split,

time: 832 us -> 338 us (0.41); the launches traced: 821 us -> 337 us
  waiting for transfers between devices: 366 us -> 0 us
  Pallas kernels: 0 us -> 317 us
  blocking collectives: 192 us -> 0 us
  matrix products: 90 us -> 0 us
  local copies, waits for them, and re-layouts: 76.3 us -> 5.45 us
  starting transfers between devices: 40.6 us -> 0 us
  other arithmetic: 41.3 us -> 14.3 us
  between operations: 15.1 us -> 1.02 us
    pallas_call x0 -> x1, Pallas kernels: none -> 317 us  [kernel_call(): pl.pallas_call(functools.partial(mega, rows, plane), out_shape=out_shape,...]
    all_to_all x6 -> x0, waiting for transfers between devices: 159 us -> none  [the longest x3 97.7 us: fold_feed(): lax.all_to_all(pieces.reshape(plane, GROUP * rows, shard), AXIS, split_ax...]
    all_gather x6 -> x0, waiting for transfers between devices: 146 us -> none  [the longest x3 85.4 us: spread(): lax.all_gather(got, AXIS, axis=0, tiled=False, axis_index_groups=plane_gr...]
    all_to_all x3 -> x0, blocking collectives: 116 us -> none  [spread(): lax.all_to_all(pieces, AXIS, split_axis=0, concat_axis=0, tiled=True, axi...]
    dot_general x20 -> x0, matrix products: 89.5 us -> none  [the longest x15 87.5 us: dot(): lax.dot_general(left, right, ((dims[:1], dims[1:]), ((), ())), preferred_...]
    reduce_scatter x3 -> x0, waiting for transfers between devices: 61.1 us -> none  [the longest x2 61.1 us: fold_tokens(): lax.psum_scatter(term.astype(BF16), AXIS, scatter_dimension=0, tiled=True...]
    unnamed x1 -> x0, blocking collectives: 38.5 us -> none
    psum x1 -> x0, blocking collectives: 37 us -> none  [array_body(): bias_sum = lax.psum(jnp.sum(input_low, axis=0, dtype=F32), AXIS)]
  transfers between devices with their start and end apart: 15 -> 0, of which waited for: 12 -> 0; matrix products, arithmetic and copies ran while one was open for 19% -> 0% of each run, Pallas kernels for 0% -> 0%
where the time goes in v3:
time: 338 us; the launch traced here: 337 us
  Pallas kernels  317 us (94%)
  other arithmetic  14.3 us (4%)
  local copies, waits for them, and re-layouts  5.45 us (2%)
    pallas_call x1, Pallas kernels, kernel_call(): pl.pallas_call(functools.partial(mega, rows, plane), out_shape=out_shape,...  317 us

profile of v3, /device:TPU:0, one launch (start us, length us, event | category | flops | bytes accessed | tf_op | source)
XLA Modules:
  0.0 337.3 jit_solution(13002552618900096941)
XLA Ops:
  0.6 0.7 convert_bitcast_fusion
  1.3 0.7 convert_element_type.65
  2.0 0.7 convert_element_type.64
  2.6 0.6 stack.23.refs_2_
  3.3 0.7 convert_dynamic-update-slice_fusion
  4.0 0.7 convert_dynamic-update-slice_fusion.1
  4.7 0.7 convert_dynamic-update-slice_fusion.2
  5.5 0.6 broadcast_in_dim.10.refs_3_
  6.1 316.5 %layer.1 = (bf16[8,48,1024]{2,1,0:T(8,128)(2,1)}, bf16[8,48,768]{2,1,0:T(8,128)(2,1)}, bf16[8,48,1152]{2,1,0:T(8,128)(2,1)}, bf16[8,48,1152]{2,1,0:T(8,128)(2,1)...) custom-call(bf16[128,1536]{1,0:T(8,128)(2,1)} %refs_0_.1, ...), custom_call_target="tpu_custom_call" | custom-call | tf_op jit(solution)/shard_map/layer/pallas_call | solution.py:946
  322.7 0.0 copy-start.13
  322.7 1.6 convert_reduce_fusion
  324.3 0.0 copy-start.10
  324.4 0.0 copy-start.11
  324.4 0.9 multiply_convert_fusion
  325.2 0.1 convert_reduce_fusion.1
  325.5 0.8 fusion.3
  326.3 0.9 fusion.2
  327.3 0.5 add_add_fusion
  327.8 0.1 reduce
  327.9 0.6 dynamic_slice.6
  328.5 0.6 slice_bitcast_fusion.7
  329.1 0.6 dynamic_slice.7
  329.7 0.1 convert_reduce_fusion.2
  329.8 0.7 pad_maximum_fusion.1
  330.6 0.0 copy-start
  330.6 0.0 copy-start.1
  330.7 0.3 copy-done.3
  331.2 0.6 copy-done
  331.8 0.3 copy-done.1
  332.1 3.0 convert_multiply_fusion
  335.2 1.3 convert_element_type.78
  336.5 0.7 copy.57
  (65 shorter events, 0.6 us)
Async XLA Ops:
  322.7 1.7 copy-start.13
  322.7 1.7 copy-start.6
  322.7 2.6 copy-start.5
  324.3 1.1 copy-start.10
  324.4 1.1 copy-start.11
  325.2 1.1 copy-start.7
  325.2 2.5 copy-start.12
  325.2 4.4 %copy-start.8 = (bf16[8,48,768]{2,1,0:T(8,128)(2,1)S(1)}, bf16[8,48,768]{2,1,0:T(8,128)(2,1)}, u32[]{:S(2)}) copy-start(bf16[8,48,768]{2,1,0:T(8,128)(2,1)} %get-tuple-element.28) | copy-start | bytes 1769476
  326.3 4.2 %copy-start.4 = (bf16[8,48,1152]{2,1,0:T(8,128)(2,1)S(1)}, bf16[8,48,1152]{2,1,0:T(8,128)(2,1)}, u32[]{:S(2)}) copy-start(bf16[8,48,1152]{2,1,0:T(8,128)(2,1)} %get-tuple-element.30) | copy-start | bytes 2654212
  329.8 1.3 copy-start.3
  330.6 1.2 copy-start
  330.6 1.5 copy-start.1
  332.1 3.0 copy-start.2
  335.1 1.4 copy-start.9

commit v4 on v3

--- a/solution.py
+++ b/solution.py
@@ -13,6 +13,7 @@
 HD = 128
 GROUP = 8
 LINES = GROUP // 2
+KEYS = H // KV
 
 EPSILON = 1e-06
 ROPE_BASE = 1000000.0
@@ -233,21 +234,23 @@
 
 def mega(rows, plane, *refs):
     (
-        x_in, cot_in, aux_in, bias_in, wq_in, wk_in, wv_in, wo_in, wg_in, wu_in, wd_in,
-        o1, o2, o3, o4, o5, fo_out, bg_out, tg_out, h_out,
-        xs, xh, aux, sa, wgs, wus, w1, w2, w3, w4, w5, g5,
+        x_in, cot_in, pos_in, seg_in, aux_in, wq_in, wk_in, wv_in, wo_in, wg_in, wu_in, wd_in,
+        o1, o2, o3, o4, o5, fo_out, bg_out, tg_out, bo_out,
+        xs, xh, aux, ids, sa, wgs, wus, w1, w2, w3, w4, w5, g5,
         r1, r2, r3, r4, hn, gb, gt, up, act, pb, rb, rt,
-        zb, zr, dh, dz, ob, qr, kr, vr, pr, dob, dq, cos, sin, msk, ba, bp, bgp, bsum,
+        zb, zr, dh, hs, dz, ob, qr, kr, vr, pr, dob, dq, cos, sin, msk, bias_in, ba, bp, bgp, bsum,
         lsem, a_s, a_r, p_s, p_r, r_s, r_r, o_s, o_r, t_s, t_r, d_s, d_r, b_s, b_r, e_s, e_r, credit, pair_credit, line_credit,
     ) = refs
     weights = (w1, w2, w3, w4, w5)
-    grads = (w1, w2, w3, w4, g5)
-    landing = (r1, r2, r3, r4, r4)
-    outs = (o1, o2, o3, o4, o5)
     block, width = x_in.shape
     shard = w3.shape[1]
     half = w2.shape[1]
     heads = half // HD
+    every = pl.ds(0, shard)
+    parts = (
+        (w1, pl.ds(0, 512), r1, o1), (w2, pl.ds(0, half), r2, o2), (w3, every, r3, o3), (w4, every, r4, o4),
+        (g5, every, r4, o5), (w1, pl.ds(512, half - 512), r1, o1), (w1, pl.ds(half, 2 * HD), r1, o1),
+    )
     strip = width // LINES
     hidden = wg_in.shape[1]
     short = GROUP * shard - hidden
@@ -320,6 +323,12 @@
         if arrive:
             pending[key + ("arrive",)] = copy.wait_recv
 
+    def left(ref, send):
+        remote(ref, ref, send, send, sib).wait_send()
+
+    def landed(ref, recv):
+        remote(ref, ref, recv, recv, sib).wait_recv()
+
     def begin_local(key, copy):
         copy.start()
         pending[key] = copy.wait
@@ -346,88 +355,133 @@
         return (wgs, wus, wd_in)[k - 2].at[:, pl.ds(start, shard)]
 
     def a_copy(k, j):
-        zz, cc = zj(j // 2), flip(c, j % 2)
+        zz, cc = zj(j // 2 if isinstance(j, int) else lax.div(j, 2)), flip(c, j % 2 if isinstance(j, int) else lax.rem(j, 2))
         return remote(
-            source(k, zz * 2 + cc, cc), weights[k].at[piece(z, p, c)], a_s.at[k, j], a_r.at[k, j], dev(zz, p, cc)
+            source(k, zz * 2 + cc, cc), weights[k].at[piece(z, p, c)], a_s.at[k],
+            a_r.at[k, j // 2 if isinstance(j, int) else lax.div(j, 2)], dev(zz, p, cc),
         )
 
-    def a_send(k):
+    def a_unit(k, j):
+        return weights[k].at[unit(zj(j), p)]
+
+    def a_pass(k, j):
+        return remote(a_unit(k, j), a_unit(k, j), a_s.at[5 + k], a_r.at[k, 5 - j], dev(zj(1), p, c))
+
+    def a_pair(k):
         begin_local(("a_own", k), local(11 + k, source(k, f, c), weights[k].at[piece(z, p, c)]))
-        for j in range(1, GROUP):
-            begin(("a", k, j), a_copy(k, j))
-
-    def a_wait(k, jz):
-        settle(("a_own", k) if jz == 0 else ("a", k, 2 * jz, "arrive"), ("a", k, 2 * jz + 1, "arrive"))
-
-    def ag_copy(k, s):
-        j = s % 4
+        a_copy(k, 1).start()
+
+    def a_line(k):
+        through = k < 2
+        for j in (2, 3):
+            a_copy(k, j).start()
+        if through:
+            for j in (0, 1):
+                a_copy(k, 4 + 2 * inner + j).start()
+        else:
+            for j in (4, 5, 6, 7):
+                a_copy(k, j).start()
+        pending["a", k, "leave"] = lambda: left(weights[k].at[pl.ds(0, (5 if through else 7) * rows)], a_s.at[k])
+        if through:
+
+            def passed():
+                @pl.when(inner == 1)
+                def _():
+                    left(weights[k].at[pl.ds(0, 4 * rows)], a_s.at[5 + k])
+
+            pending["a_pass", k, "leave"] = passed
+
+    def a_wait(k, n):
+        if n == 0:
+            settle(("a_own", k))
+            landed(weights[k].at[piece(z, p, 1 - c)], a_r.at[k, 0])
+            return 0
+        j = n if k >= 2 or n == 1 else (2 + inner if n == 2 else 3 - inner)
+        landed(a_unit(k, j), a_r.at[k, j])
+        if k < 2 and n > 1:
+
+            @pl.when(inner == 1)
+            def _():
+                a_pass(k, j).start()
+
+        return j
+
+    def ag_copy(k, s, j):
         if s < 4:
             part, target = unit(zj(j), p), xnb
         elif s < 8:
             part, target = unit(zj(j), p), ynb
-        elif j < 2:
+        elif s < 10:
             part, target = unit(zj(j), px), ynb
         else:
             part, target = unit(zj(j), py), xnb
-        return remote(weights[k].at[part], weights[k].at[part], p_s.at[k, s], p_r.at[k, s], target)
-
-    def ag_send(k):
-        for j in range(LINES):
-            a_wait(k, j)
-            begin(("ag", k, j), ag_copy(k, j))
-            begin(("ag", k, 4 + j), ag_copy(k, 4 + j))
+        index = s // 4 * 4 + j
+        return remote(weights[k].at[part], weights[k].at[part], p_s.at[k], p_r.at[k, index], target)
+
+    def ag_unit(k, n):
+        j = a_wait(k, n)
+        ag_copy(k, 0, j).start()
+        ag_copy(k, 4, j).start()
+
+    def ag_send(k, first=0):
+        for n in range(first, LINES):
+            ag_unit(k, n)
+        pending["ag", k, "leave"] = lambda: left(weights[k].at[pl.ds(0, 24 * rows)], p_s.at[k])
 
     def ag_relay(k):
         for j in range(4):
-            settle(("ag", k, j if j < 2 else 4 + j, "arrive"))
-            begin(("ag", k, 8 + j), ag_copy(k, 8 + j))
+            ag_copy(k, 0 if j < 2 else 4, j).wait_recv()
+            ag_copy(k, 8 + j, j).start()
 
     def ag_finish(k):
-        for s in (2, 3, 4, 5, 8, 9, 10, 11):
-            settle(("ag", k, s, "arrive"))
+        for s, j in ((0, 2), (0, 3), (4, 0), (4, 1), (8, 0), (8, 1), (10, 2), (10, 3)):
+            ag_copy(k, s, j).wait_recv()
 
     def ag_sent(k):
-        settle_all(lambda key: key[:2] == ("ag", k) and key[-1] == "leave")
+        settle(("ag", k, "leave"))
+        if k < 2:
+            settle(("a_pass", k, "leave"))
 
     def tok_copy(which, kind, j):
         buf = (hn, gb)[which]
         part = tokens_of(zj(0 if kind == "own" else j), c)
         if kind == "own":
-            send, recv, target = j, j, dev(zj(j), p, c)
+            send, recv, target = t_s.at[which, 0], j, dev(zj(j), p, c)
         elif kind == "pair":
-            send, recv, target = 4 + j, 4 + j, sib
+            send, recv, target = t_s.at[which, 0], 4 + j, sib
         else:
-            send, recv, target = 6 + j, 5 - j, dev(zj(1), p, c)
-        return remote(buf.at[part], buf.at[part], t_s.at[which, send], t_r.at[which, recv], target)
+            send, recv, target = t_s.at[which, 1], 5 - j, dev(zj(1), p, c)
+        return remote(buf.at[part], buf.at[part], send, t_r.at[which, recv], target)
 
     def tok_send(which):
-        begin(("tok", which, 1), tok_copy(which, "own", 1))
-        begin(("tok", which, 2), tok_copy(which, "own", 2 + inner))
-        pending["tok", which, 3, "arrive"] = lambda: tok_copy(which, "own", 3 - inner).wait_recv()
-        begin(("pair", which, 0), tok_copy(which, "pair", 0))
-
-    def tok_forward(which):
-        for n, j in ((1, 1), (2, 2 + inner), (3, 3 - inner)):
-            settle(("tok", which, n, "arrive"))
-            if n > 1:
-
-                @pl.when(inner == 1)
-                def _(j=j):
-                    tok_copy(which, "pass", j).start()
-
-            begin(("pair", which, n), tok_copy(which, "pair", j))
-
-        def passed():
+        tok_copy(which, "own", 1).start()
+        tok_copy(which, "own", 2 + inner).start()
+        tok_copy(which, "pair", 0).start()
+
+        def sent():
+            buf = (hn, gb)[which]
+            left(buf.at[pl.ds(0, 6 * block)], t_s.at[which, 0])
+
             @pl.when(inner == 1)
             def _():
-                for j in (2, 3):
-                    tok_copy(which, "pass", j).wait_send()
-
-        pending["pass", which, "leave"] = passed
+                left(buf.at[pl.ds(0, 2 * block)], t_s.at[which, 1])
+
+        pending["tok", which, "leave"] = sent
+
+    def tok_forward(which):
+        for j in (1, 2 + inner, 3 - inner):
+            tok_copy(which, "own", j).wait_recv()
+            if not isinstance(j, int):
+
+                @pl.when(inner == 1)
+                def _():
+                    tok_copy(which, "pass", j).start()
+
+            tok_copy(which, "pair", j).start()
 
     def tok_finish(which):
-        for n in range(4):
-            settle(("pair", which, n, "arrive"))
+        for j in range(4):
+            tok_copy(which, "pair", j).wait_recv()
 
     def e_copy(n, src, dst):
         return remote(src, dst, e_s.at[n], e_r.at[n], sib)
@@ -436,94 +490,93 @@
 
     def bias_in_copy(s):
         zz, cc = zj(s // 2), flip(c, s % 2)
-        return remote(bias_in.at[cc], ba.at[f], b_s.at[s], b_r.at[s], dev(zz, p, cc))
-
-    def bias_plane_copy(base, n, buf):
+        return remote(bias_in.at[cc], ba.at[f], b_s.at[0], b_r.at[0], dev(zz, p, cc))
+
+    def bias_plane_copy(group, n, buf):
         target = dev(z, (px, py, pd)[n], c)
-        return remote(buf.at[p], buf.at[p], b_s.at[base + n], b_r.at[base + n], target)
+        return remote(buf.at[p], buf.at[p], b_s.at[group], b_r.at[group], target)
 
     def bias_out_copy(s):
         zz, cc = zj(s // 2), flip(c, s % 2)
-        return remote(bsum, bg_out.at[f], b_s.at[16 + s], b_r.at[16 + s], dev(zz, p, cc))
+        return remote(bsum, bg_out.at[f], b_s.at[3], b_r.at[3], dev(zz, p, cc))
+
+    def bias_note(group, buf, count):
+        pending["bias", group, "leave"] = lambda: left(buf.at[pl.ds(0, count)], b_s.at[group])
+        pending["bias", group, "arrive"] = lambda: landed(buf.at[pl.ds(0, count)], b_r.at[group])
 
     def rs_copy(k, s, h):
-        ref = grads[k]
+        ref, cols, land = parts[k][:3]
         zz = zf((0, 1, 1, 0, 0, 1)[s], h)
         part = unit(zz, (pd, pd, px, py, px, py)[s])
         place = (0, 2, 6, 8, 4, 10)[s] + h
         target = (ynb, xnb, xnb, ynb, xnb, ynb)[s]
-        return remote(ref.at[part], landing[k].at[slot(place)], r_s.at[k, place], r_r.at[k, place], target)
-
-    def rs_note(k, kinds):
-        for s in kinds:
-            for h in range(2):
-                pending["rs", k, s, h, "leave"] = lambda s=s, h=h: rs_copy(k, s, h).wait_send()
-                pending["rs", k, s, h, "arrive"] = lambda s=s, h=h: rs_copy(k, s, h).wait_recv()
+        return remote(ref.at[part, cols], land.at[slot(place), cols], r_s.at[k], r_r.at[k, place], target)
 
     def rs_start(k, left_ref, right_ref):
+        ref, cols = parts[k][:2]
+
         @pl.loop(0, 2)
         def both(i):
             h = 1 - i
             for high in (1, 0):
                 zz = zf(high, h)
                 at = pl.multiple_of(zz * strip, 128)
-                left = left_ref[:, pl.ds(at, strip)]
-                grads[k][pl.ds(at, strip), :] = dot_tn(left, right_ref[...]).astype(BF16)
+                ref[pl.ds(at, strip), cols] = dot_tn(left_ref[:, pl.ds(at, strip)], right_ref[:, cols]).astype(BF16)
                 for s in ((0, 3), (1, 2))[high]:
                     rs_copy(k, s, h).start()
 
-        rs_note(k, (0, 1, 2, 3))
+        pending["rs", k, "leave"] = lambda: left(ref.at[pl.ds(0, 24 * rows), cols], r_s.at[k])
 
     def rs_middle(k):
+        ref, cols, land = parts[k][:3]
+
         @pl.loop(0, 2)
         def both(i):
             h = 1 - i
             for high in (1, 0):
                 rs_copy(k, high, h).wait_recv()
                 part = unit(zf(high, h), (px, py)[high])
-                got = landing[k][slot(2 * high + h)]
-                grads[k][part] = (grads[k][part].astype(F32) + got.astype(F32)).astype(BF16)
+                got = land[slot(2 * high + h), cols]
+                ref[part, cols] = (ref[part, cols].astype(F32) + got.astype(F32)).astype(BF16)
                 rs_copy(k, 4 + high, h).start()
 
-        for s in (0, 1):
-            for h in range(2):
-                pending.pop(("rs", k, s, h, "arrive"))
-        rs_note(k, (4, 5))
-
     def out_copy(k, j, other):
+        ref, cols, _, out = parts[k]
         zz, cc = zj(j), flip(c, other)
-        return remote(
-            grads[k].at[piece(zz, p, cc)], outs[k].at[f], o_s.at[k, 2 * j + other], o_r.at[k, 2 * j + other], dev(zz, p, cc)
-        )
+        return remote(ref.at[piece(zz, p, cc), cols], out.at[f, :, cols], o_s.at[k], o_r.at[k], dev(zz, p, cc))
 
     def rs_finish(k):
+        ref, cols, land, out = parts[k]
         for j in (3, 1, 2, 0):
             h, high = j % 2, j // 2
-            settle(("rs", k, (4, 2)[high], h, "arrive"), ("rs", k, (3, 5)[high], h, "arrive"))
+            rs_copy(k, (4, 2)[high], h).wait_recv()
+            rs_copy(k, (3, 5)[high], h).wait_recv()
             part = unit(zj(j), p)
-            got = landing[k][slot(4 + j)].astype(F32) + landing[k][slot(8 + j)].astype(F32)
-            grads[k][part] = (grads[k][part].astype(F32) + got).astype(BF16)
-            begin(("out", k, j, 1), out_copy(k, j, 1))
+            got = land[slot(4 + j), cols].astype(F32) + land[slot(8 + j), cols].astype(F32)
+            ref[part, cols] = (ref[part, cols].astype(F32) + got).astype(BF16)
+            out_copy(k, j, 1).start()
             if j == 0:
-                begin_local(("out_own", k), local(17 + k, grads[k].at[piece(z, p, c)], outs[k].at[f]))
+                begin_local(("out_own", k), local(17 + k, ref.at[piece(z, p, c), cols], out.at[f, :, cols]))
             else:
-                begin(("out", k, j, 0), out_copy(k, j, 0))
+                out_copy(k, j, 0).start()
+        pending["out", k, "leave"] = lambda: left(ref.at[pl.ds(0, 7 * rows), cols], o_s.at[k])
+        pending["out", k, "arrive"] = lambda: landed(ref.at[pl.ds(0, 7 * rows), cols], o_r.at[k])
 
     def pair_copy(which, j):
         return remote(
             pb.at[tokens_of(zj(j), 1 - c)], rb.at[pl.ds(pl.multiple_of(j * block, block), block)],
-            d_s.at[which, j], d_r.at[which, j], sib,
+            d_s.at[which, 0], d_r.at[which, j], sib,
         )
 
     def line_copy(which, j):
         dst = fo_out.at[1] if which == 1 and isinstance(j, int) and j == 1 else rt.at[j - 1]
         return remote(
-            pb.at[tokens_of(zj(j), c)], dst, d_s.at[which, 4 + j], d_r.at[which, 4 + j], dev(zj(1), p, c)
+            pb.at[tokens_of(zj(j), c)], dst, d_s.at[which, 1], d_r.at[which, 4 + j], dev(zj(1), p, c)
         )
 
     def far_copy(which, j):
         dst = fo_out.at[2] if which == 1 else rt.at[3]
-        return remote(pb.at[tokens_of(zj(j), c)], dst, d_s.at[which, 6 + j], d_r.at[which, 4], dev(zj(j), p, c))
+        return remote(pb.at[tokens_of(zj(j), c)], dst, d_s.at[which, 1], d_r.at[which, 4], dev(zj(j), p, c))
 
     def far_add(which, j):
         @pl.when(inner == 1)
@@ -562,17 +615,8 @@
         pair_add(which, 0)
 
         def sent():
-            for j in range(LINES):
-                pair_copy(which, j).wait_send()
-            line_copy(which, 1).wait_send()
-            for j in (2, 3):
-                @pl.when(inner == 0)
-                def _():
-                    line_copy(which, j).wait_send()
-
-                @pl.when(inner == 1)
-                def _():
-                    far_copy(which, j).wait_send()
+            left(pb.at[pl.ds(0, LINES * block)], d_s.at[which, 0])
+            left(pb.at[pl.ds(0, 3 * block)], d_s.at[which, 1])
 
         pending["sum", which, "leave"] = sent
         pending["sum", which, 1, "arrive"] = lambda: line_copy(which, 1).wait_recv()
@@ -596,6 +640,8 @@
 
     def enter():
         begin_local(("aux",), local(0, aux_in, aux.at[c]))
+        begin_local(("pos",), local(25, pos_in, ids.at[0]))
+        begin_local(("seg",), local(22, seg_in, ids.at[1]))
         begin_local(("x",), local(1, x_in, xs.at[c]))
         for side in range(2):
             begin_local(("wq", side), local(2 + side, wq_in.at[:, pl.ds(side * half, half)], sa.at[side, :, pl.ds(0, half)]))
@@ -608,7 +654,9 @@
         friends = [dev(zj(j // 2), p, flip(c, j % 2)) for j in range(1, GROUP)] + [xnb, ynb, dev(z, pd, c)]
         for friend in friends:
             signal(barrier, friend)
-        settle(("aux",), ("x",), *[(name, side) for side in range(2) for name in ("wq", "wk", "wv")])
+        settle(("aux",), ("pos",), ("seg",), ("x",), *[(name, side) for side in range(2) for name in ("wq", "wk", "wv")])
+        aux[c, 0:1] = ids[0].astype(F32)
+        aux[c, 1:2] = ids[1].astype(F32)
         gain_one = column(aux[c][2:3])[:rows]
         for side in range(2):
             sa[side] = (sa[side].astype(F32) * gain_one).astype(BF16)
@@ -619,18 +667,34 @@
         begin(("e", 1), e_copy(1, xs.at[c], xs.at[c]))
 
     def bias_first():
+        step = lax.rem(me, 2 * plane * LINES // 2)
+        info = aux[c]
+
+        def placed(row, count, size):
+            wide = jnp.concatenate([row] + [jnp.zeros_like(row)] * (size // HD - 1), axis=1) if size > HD else row
+            wide = jnp.broadcast_to(wide, (8, size))
+            return pltpu.roll(wide, step * count, 1)[0:1]
+
+        own = jnp.concatenate(
+            [placed(info[4:5], rows, half), placed(info[5:6], rows // KEYS, HD), placed(info[6:7], rows // KEYS, HD)], axis=1
+        )
+        side = lax.div(me, plane * LINES)
+        bias_in[side] = own
+        bias_in[1 - side] = jnp.zeros_like(own)
         begin_local(("bias_own",), local(16, bias_in.at[c], ba.at[f]))
         for s in range(1, GROUP):
-            begin(("bias_in", s), bias_in_copy(s))
+            bias_in_copy(s).start()
+        bias_note(0, ba, GROUP - 1)
 
     def bias_second():
-        settle(("bias_own",), *[("bias_in", s, "arrive") for s in range(1, GROUP)])
+        settle(("bias_own",), ("bias", 0, "arrive"))
         total = ba[0]
         for s in range(1, GROUP):
             total = total + ba[s]
         bp[p] = total
         for n in range(3):
-            begin(("bias_plane", n), bias_plane_copy(8, n, bp))
+            bias_plane_copy(1, n, bp).start()
+        bias_note(1, bp, 3)
 
     def scale_feed():
         gain_two = column(aux[c][3:4])[:rows]
@@ -663,7 +727,7 @@
             msk[b] = jnp.where(same & (lane_id <= row_id), 1.0, 0.0)
 
     def project():
-        settle(*[("bias_plane", n, "arrive") for n in range(3)])
+        settle(("bias", 1, "arrive"))
         bias_row = (bp[0] + bp[1]) + (bp[2] + bp[3])
         for n in range(heads // 2 + 1):
             cols = pl.ds(n * 2 * HD, 2 * HD)
@@ -699,14 +763,14 @@
     def hidden_state():
         settle(("e", 2, "arrive"))
         state = xs[c].astype(F32) + zb[c] + zr[...]
-        h_out[...] = state
+        hs[...] = state
         scale_two = lax.rsqrt(jnp.mean(state * state, axis=1, keepdims=True) + EPSILON)
         hn[tokens_of(z, c)] = (state * scale_two).astype(BF16)
 
-    def feed_forward():
-        @pl.loop(0, LINES)
+    def feed_forward(first, end):
+        @pl.loop(first, end)
         def chunk(i):
-            rows_here = chunk_of(i)
+            rows_here = chunk_of(zj(i))
             left = hn[rows_here]
             for n in range(0, shard, tile):
                 cols = pl.ds(n, tile)
@@ -757,7 +821,16 @@
                 pb[rows_here, part] = dot_nt(act[rows_here], w5[part, :]).astype(BF16)
 
         sum_loop(1, compute)
-        begin_local(("fo_own",), local(22, pb.at[tokens_of(z, c)], fo_out.at[0]))
+
+    def block_result():
+        settle(("sum", 1, 1, "arrive"), ("sum", 1, 2, "arrive"))
+        for n in range(2):
+            begin_local(("fetch", n), local(2 + n, fo_out.at[1 + n], rb.at[pl.ds(n * block, block)]))
+        settle(("fetch", 0), ("fetch", 1))
+        live = jnp.where(column(aux[c][1:2]) >= 0.0, 1.0, 0.0)
+        total = hs[...] + pb[tokens_of(z, c)].astype(F32)
+        total = total + rb[pl.ds(0, block)].astype(F32) + rb[pl.ds(block, block)].astype(F32)
+        bo_out[...] = (live * total).astype(BF16)
 
     def landing_free():
         for target in (xnb, ynb):
@@ -769,7 +842,7 @@
     def hidden_gradient():
         settle(("sum", 0, 1, "arrive"), ("sum", 0, 2, "arrive"))
         weighted = pb[tokens_of(z, c)].astype(F32) + rt[0].astype(F32) + rt[3].astype(F32)
-        state = h_out[...]
+        state = hs[...]
         scale_two = lax.rsqrt(jnp.mean(state * state, axis=1, keepdims=True) + EPSILON)
         spread = jnp.mean(weighted * state, axis=1, keepdims=True)
         grad = (
@@ -813,14 +886,16 @@
     def bias_back():
         bgp[p] = jnp.sum(dq[...].astype(F32), axis=0, keepdims=True)
         for n in range(3):
-            begin(("bias_back", n), bias_plane_copy(11, n, bgp))
+            bias_plane_copy(2, n, bgp).start()
+        bias_note(2, bgp, 3)
 
     def bias_last():
-        settle(*[("bias_back", n, "arrive") for n in range(3)])
+        settle(("bias", 2, "arrive"))
         bsum[...] = (bgp[0] + bgp[1]) + (bgp[2] + bgp[3])
-        begin_local(("bias_sum",), local(23, bsum, bg_out.at[f]))
+        begin_local(("bias_sum",), local(24, bsum, bg_out.at[f]))
         for s in range(1, GROUP):
-            begin(("bias_out", s), bias_out_copy(s))
+            bias_out_copy(s).start()
+        bias_note(3, ba, GROUP - 1)
 
     def token_gradient():
         settle(("e", 4, "arrive"))
@@ -832,38 +907,48 @@
 
     enter()
     exchange_inputs()
-    a_send(0)
+    a_pair(0)
+    a_line(0)
     bias_first()
-    a_send(1)
+    a_pair(1)
+    a_line(1)
+    ag_unit(0,0)
+    a_pair(4)
     scale_feed()
+    a_pair(2)
+    a_pair(3)
+    ag_unit(0,1)
+    ag_unit(1,0)
     mask_upstream()
-    ag_send(0)
-    a_send(2)
+    ag_unit(2,0)
+    ag_unit(3,0)
+    ag_send(0,2)
+    a_line(2)
     norm_tokens()
     ag_relay(0)
     bias_second()
-    ag_send(1)
-    a_send(3)
+    ag_send(1,1)
+    a_line(3)
     ag_finish(0)
     project()
     ag_relay(1)
-    ag_send(2)
+    ag_send(2,1)
     attend()
     ag_finish(1)
     attend_out()
     hidden_state()
     tok_send(0)
-    ag_send(3)
-    a_send(4)
+    ag_send(3,1)
+    a_line(4)
     tok_send(1)
     ag_relay(2)
     ag_relay(3)
     tok_forward(0)
-    ag_send(4)
+    ag_send(4, 0)
     tok_finish(0)
     ag_finish(2)
     ag_finish(3)
-    feed_forward()
+    feed_forward(0, LINES)
     ag_relay(4)
     tok_forward(1)
     ag_finish(4)
@@ -895,18 +980,25 @@
     project_back()
     ag_sent(0)
     rs_start(0, xh, dq)
+    rs_start(5, xh, dq)
+    rs_start(6, xh, dq)
+    rs_finish(3)
     rs_middle(1)
-    rs_finish(3)
     bias_back()
     token_gradient()
+    rs_middle(0)
     rs_finish(1)
+    rs_middle(5)
+    rs_middle(6)
     bias_last()
-    rs_middle(0)
+    block_result()
     rs_finish(0)
+    rs_finish(5)
+    rs_finish(6)
     settle(*list(pending))
 
 
-def kernel_call(rows, plane, block, width, hidden, aux, bias, tokens, cotangent, *weights):
+def kernel_call(rows, plane, block, width, hidden, aux, tokens, cotangent, position, segment, *weights):
     half = width // 2
     blocks = hidden // 128
     shard = -(-blocks // GROUP) * 128
@@ -923,37 +1015,155 @@
         jax.ShapeDtypeStruct((3, block, width), BF16),
         jax.ShapeDtypeStruct((GROUP, 1, inner), F32),
         jax.ShapeDtypeStruct((block, width), BF16),
-        jax.ShapeDtypeStruct((block, width), F32),
+        jax.ShapeDtypeStruct((block, width), BF16),
     ]
     scratch = [
-        vm((2, block, width), BF16), vm((2 * block, width), BF16), vm((2, 8, 128), F32), vm((2, rows, inner), BF16),
+        vm((2, block, width), BF16), vm((2 * block, width), BF16), vm((2, 8, 128), F32), vm((2, 1, 128), jnp.int32),
+        vm((2, rows, inner), BF16),
         vm((rows, hidden), BF16), vm((rows, hidden), BF16),
     ]
     scratch += [vm((width, n), BF16) for n in columns] + [vm((width, shard), BF16)]
     scratch += [vm((12 * 2 * rows, n), BF16) for n in columns[:4]]
     scratch += [vm((group_tokens, width), BF16)] * 2 + [vm((group_tokens, shard), BF16)] * 3
+    scratch += [vm((group_tokens, width), BF16), vm((LINES * block, width), BF16), vm((LINES, block, width), BF16)]
     scratch += [
-        vm((group_tokens, width), BF16), vm((LINES * block, width), BF16), vm((LINES, block, width), BF16),
-        vm((2, block, width), F32), vm((block, width), F32), vm((block, width), F32), vm((2 * block, width), BF16),
+        vm((2, block, width), F32), vm((block, width), F32), vm((block, width), F32), vm((block, width), F32),
+        vm((2 * block, width), BF16),
         vm((2 * block, half), BF16), vm((2, heads * block, HD), BF16), vm((2, block, HD), BF16), vm((2, block, HD), BF16),
         vm((2, heads * block, block), F32), vm((2, heads * block, HD), BF16), vm((2 * block, inner), BF16),
         vm((2, block, HD), F32), vm((2, block, HD), F32), vm((2, block, block), F32),
-        vm((GROUP, 1, inner), F32), vm((4, 1, inner), F32), vm((4, 1, inner), F32), vm((1, inner), F32),
+        vm((2, 1, inner), F32), vm((GROUP, 1, inner), F32), vm((4, 1, inner), F32), vm((4, 1, inner), F32), vm((1, inner), F32),
     ]
-    scratch += [dma((24,))]
-    scratch += [dma((5, 8))] * 2 + [dma((5, 12))] * 4 + [dma((5, 8))] * 2 + [dma((2, 12))] * 4 + [dma((24,))] * 2 + [dma((8,))] * 2
+    scratch += [dma((26,))]
+    scratch += [dma((7,)), dma((5, 4)), dma((5,)), dma((5, 12)), dma((7,)), dma((7, 12)), dma((7,)), dma((7,))]
+    scratch += [dma((2, 2)), dma((2, 8)), dma((2, 2)), dma((2, 8)), dma((4,)), dma((4,)), dma((5,)), dma((5,))]
     scratch += [pltpu.SemaphoreType.REGULAR] * 3
     return pl.pallas_call(
         functools.partial(mega, rows, plane),
         out_shape=out_shape,
-        in_specs=[any_space] * 11,
+        in_specs=[any_space] * 12,
         out_specs=[any_space] * 7 + [vmem_space] * 2,
         scratch_shapes=scratch,
         compiler_params=pltpu.CompilerParams(
             collective_id=0, has_side_effects=True, vmem_limit_bytes=64 * 2**20 - 2**17
         ),
         name="layer",
-    )(tokens, cotangent, aux, bias, *weights)
+    )(tokens, cotangent, position, segment, aux, *weights)
+
+
+def gather_outputs(rows, plane, hidden, *refs):
+    (
+        o1, o2, o3, o4, o5, bg, tg, bo, aux, wq, wk, wv, wg, wu,
+        bo_out, tg_out, gain_one_out, wq_out, bq_out, wk_out, bk_out, wv_out, bv_out, wo_out, gain_two_out,
+        wg_out, wu_out, wd_out, total,
+    ) = refs
+    step = pl.program_id(0)
+    steps = pl.num_programs(0)
+    half = wo_out.shape[1] // 2
+    shard = o3.shape[2]
+    per = o3.shape[0]
+    short = GROUP * shard - hidden
+    me = lax.axis_index(AXIS)
+    row_id = lax.broadcasted_iota(jnp.int32, (128, 128), 0)
+    lane_id = lax.broadcasted_iota(jnp.int32, (128, 128), 1)
+
+    def column(row):
+        return jnp.sum(jnp.where(row_id == lane_id, row, 0.0), axis=1, keepdims=True)[:rows]
+
+    def as_row(col):
+        return jnp.sum(jnp.where(row_id[:rows, :rows] == lane_id[:rows, :rows], col, 0.0), axis=0, keepdims=True)
+
+    gain_one = column(aux[2:3])
+    gain_two = column(aux[3:4])
+
+    @pl.when(step == 0)
+    def _():
+        bo_out[...] = bo[...]
+        tg_out[...] = tg[...]
+        sums = jnp.zeros((rows, 1), F32)
+        for side in range(2):
+            part = o1[side].astype(F32)
+            for zz in range(1, LINES):
+                part = part + o1[2 * zz + side].astype(F32)
+            q_part, k_part, v_part = part[:, :half], part[:, half : half + HD], part[:, half + HD :]
+            here, keys = pl.ds(side * half, half), pl.ds(side * HD, HD)
+            sums = sums + jnp.sum(q_part * wq[:, here].astype(F32), axis=1, keepdims=True)
+            sums = sums + jnp.sum(k_part * wk[:, keys].astype(F32), axis=1, keepdims=True)
+            sums = sums + jnp.sum(v_part * wv[:, keys].astype(F32), axis=1, keepdims=True)
+            wq_out[:, here] = q_part * gain_one
+            wk_out[:, keys] = k_part * gain_one
+            wv_out[:, keys] = v_part * gain_one
+            part = o2[side].astype(F32)
+            for zz in range(1, LINES):
+                part = part + o2[2 * zz + side].astype(F32)
+            wo_out[:, here] = part
+        gain_one_out[...] = as_row(sums)
+        sides = [(bg[side] + bg[2 + side]) + (bg[4 + side] + bg[6 + side]) for side in range(2)]
+        bk_out[:, 0:HD] = sides[0][:, half : half + HD]
+        bk_out[:, HD : 2 * HD] = sides[1][:, half : half + HD]
+        mine = jnp.where(lax.div(me, plane * LINES) == 0, sides[0], sides[1])
+        place = lax.rem(me, plane * LINES)
+
+        def taken(row, count):
+            size = row.shape[1]
+            wide = jnp.broadcast_to(row, (8, size))
+            return pltpu.roll(wide, lax.rem(size - place * count, size), 1)[0:1, :count]
+
+        bq_out[...] = taken(mine[:, :half], rows)
+        bv_out[...] = taken(mine[:, half + HD :], rows // KEYS)
+        total[...] = jnp.zeros_like(total)
+
+    def put(first):
+        sums = jnp.zeros((rows, 1), F32)
+        for i in range(per):
+            skip = first if i == per - 1 else 0
+            cols = pl.ds(i * shard, shard - skip)
+            gate = o3[i][:, skip:].astype(F32)
+            lift = o4[i][:, skip:].astype(F32)
+            sums = sums + jnp.sum(gate * wg[:, cols].astype(F32) + lift * wu[:, cols].astype(F32), axis=1, keepdims=True)
+            wg_out[:, cols] = gate * gain_two
+            wu_out[:, cols] = lift * gain_two
+            wd_out[:, cols] = o5[i][:, skip:].astype(F32)
+        total[...] = total[...] + sums
+
+    @pl.when(step < steps - 1)
+    def _():
+        put(0)
+
+    @pl.when(step == steps - 1)
+    def _():
+        put(short)
+        gain_two_out[...] = as_row(total[...])
+
+
+def output_call(rows, plane, block, width, hidden, pieces, bias_sum, token_grad, block_output, aux, weights):
+    per = 2
+    shard = pieces[2].shape[2]
+    key_width = weights[1].shape[1]
+
+    def whole(shape):
+        return pl.BlockSpec(shape, lambda i: (0,) * len(shape))
+
+    feed = pl.BlockSpec((per, rows, shard), lambda i: (i, 0, 0))
+    wide = pl.BlockSpec((rows, per * shard), lambda i: (0, i))
+    shapes = [
+        ((block, width), BF16), ((block, width), BF16), ((1, rows), F32), ((rows, width), F32), ((1, rows), F32),
+        ((rows, key_width), F32), ((1, key_width), F32), ((rows, key_width), F32), ((1, rows // KEYS), F32),
+        ((rows, width), F32), ((1, rows), F32),
+        ((rows, hidden), F32), ((rows, hidden), F32), ((rows, hidden), F32),
+    ]
+    return pl.pallas_call(
+        functools.partial(gather_outputs, rows, plane, hidden),
+        grid=(GROUP // per,),
+        out_shape=[jax.ShapeDtypeStruct(*shape) for shape in shapes],
+        in_specs=[whole(pieces[0].shape), whole(pieces[1].shape), feed, feed, feed, whole(bias_sum.shape)]
+        + [whole((block, width))] * 2 + [whole(aux.shape)]
+        + [whole((rows, width)), whole((rows, key_width)), whole((rows, key_width)), wide, wide],
+        out_specs=[whole(shape) for shape, _ in shapes[:11]] + [wide] * 3,
+        scratch_shapes=[pltpu.VMEM((rows, 1), F32)],
+        compiler_params=pltpu.CompilerParams(vmem_limit_bytes=64 * 2**20 - 2**17),
+        name="outputs",
+    )(*pieces, bias_sum, token_grad, block_output, aux, *weights)
 
 
 def kernel_body(
@@ -961,74 +1171,24 @@
     out_weight, second_gain, gate_weight, up_weight, down_weight, cotangent,
 ):
     count = lax.axis_size(AXIS)
-    me = lax.axis_index(AXIS)
     plane = count // GROUP
     rows, width = query_weight.shape
     block = tokens.shape[0]
     hidden = gate_weight.shape[1]
-    key_width = key_weight.shape[1]
-    half = width // 2
-
-    def wide(v):
-        return jnp.pad(v.astype(F32), (0, 128 - v.shape[0]))
-
-    aux = jnp.stack([wide(position), wide(segment), wide(first_gain), wide(second_gain)] + [jnp.zeros((128,), F32)] * 4)
-
-    def placed(v):
-        full = jnp.zeros((v.shape[0] * count,), F32)
-        return lax.dynamic_update_slice(full, v.astype(F32), (me * v.shape[0],)).reshape(2, -1)
-
-    bias = jnp.concatenate([placed(query_bias), placed(key_bias), placed(value_bias)], axis=1)[:, None, :]
-    pieces_in, pieces_out, gate_raw, up_raw, down_raw, feed, bias_sum, token_grad, state = kernel_call(
-        rows, plane, block, width, hidden, aux, bias, tokens, cotangent,
+
+    aux = jnp.zeros((1024,), F32)
+    for n, vector in enumerate((first_gain, second_gain, query_bias, key_bias, value_bias), 2):
+        aux = aux + jnp.pad(vector.astype(F32), (128 * n, 1024 - 128 * n - vector.shape[0]))
+    aux = aux.reshape(8, 128)
+    *pieces, _, bias_sum, token_grad, block_output = kernel_call(
+        rows, plane, block, width, hidden, aux, tokens, cotangent, position[None], segment[None],
         query_weight, key_weight, value_weight, out_weight, gate_weight, up_weight, down_weight,
     )
-    live_rows = (segment >= 0).astype(F32)[:, None]
-    gain_one = first_gain.astype(F32)[:, None]
-    gain_two = second_gain.astype(F32)[:, None]
-    block_output = (live_rows * (state + jnp.sum(feed.astype(F32), axis=0))).astype(BF16)
-
-    def sides(pieces):
-        total = jnp.sum(pieces.astype(F32).reshape(LINES, 2, rows, -1), axis=0)
-        return total[0], total[1]
-
-    def join(pieces):
-        shard = pieces.shape[2]
-        short = GROUP * shard - hidden
-        parts = [pieces[i] for i in range(GROUP - 1)] + [pieces[GROUP - 1][:, short:]]
-        return jnp.concatenate(parts, axis=1).astype(F32)
-
-    left, right = sides(pieces_in)
-    query_raw = jnp.concatenate([left[:, :half], right[:, :half]], axis=1)
-    key_raw = jnp.concatenate([left[:, half : half + HD], right[:, half : half + HD]], axis=1)
-    value_raw = jnp.concatenate([left[:, half + HD :], right[:, half + HD :]], axis=1)
-    gain_one_sum = (
-        jnp.sum(query_raw * query_weight.astype(F32), axis=1)
-        + jnp.sum(key_raw * key_weight.astype(F32), axis=1)
-        + jnp.sum(value_raw * value_weight.astype(F32), axis=1)
+    outs = output_call(
+        rows, plane, block, width, hidden, pieces, bias_sum, token_grad, block_output, aux,
+        (query_weight, key_weight, value_weight, gate_weight, up_weight),
     )
-    gate_raw, up_raw, down_raw = join(gate_raw), join(up_raw), join(down_raw)
-    gain_two_sum = jnp.sum(gate_raw * gate_weight.astype(F32) + up_raw * up_weight.astype(F32), axis=1)
-    bias_total = jnp.sum(bias_sum.reshape(LINES, 2, -1), axis=0)
-    query_bias_all = bias_total[:, :half].reshape(-1)
-    key_bias_all = bias_total[:, half : half + HD].reshape(-1)
-    value_bias_all = bias_total[:, half + HD :].reshape(-1)
-    return (
-        block_output,
-        token_grad,
-        gain_one_sum,
-        query_raw * gain_one,
-        lax.dynamic_slice(query_bias_all, (me * rows,), (rows,)),
-        key_raw * gain_one,
-        key_bias_all,
-        value_raw * gain_one,
-        lax.dynamic_slice(value_bias_all, (me * value_bias.shape[0],), (value_bias.shape[0],)),
-        jnp.concatenate(sides(pieces_out), axis=1),
-        gain_two_sum,
-        gate_raw * gain_two,
-        up_raw * gain_two,
-        down_raw,
-    )
+    return tuple(out.reshape(-1) if out.shape[0] == 1 else out for out in outs)
 
 
 def layer(*args):

time: 338 us -> 316 us (0.935)
  other arithmetic: 14.3 us -> 1.32 us
  local copies, waits for them, and re-layouts: 5.45 us -> 0 us
  Pallas kernels: 317 us -> 313 us
    pallas_call x1, Pallas kernels: 317 us -> 305 us  [kernel_call(): pl.pallas_call(functools.partial(mega, rows, plane), out_shape=out_shape,...]
    pallas_call x0 -> x1, Pallas kernels: none -> 7.32 us  [output_call(): pl.pallas_call(functools.partial(gather_outputs, rows, plane, hidden), gr...]
    mul x3 -> x0, other arithmetic: 4.7 us -> none  [the longest x1 2.98 us: kernel_body(): up_raw * gain_two]
    convert_element_type x5 -> x0, other arithmetic: 3.48 us -> none  [the longest x2 1.31 us: wide(): return jnp.pad(v.astype(F32), (0, 128 - v.shape[0]))]
where the time goes in v4:
time: 316 us; the launch traced here: 315 us
  Pallas kernels  313 us (99%)
    pallas_call x1, Pallas kernels, kernel_call(): pl.pallas_call(functools.partial(mega, rows, plane), out_shape=out_shape,...  305 us
    pallas_call x1, Pallas kernels, output_call(): pl.pallas_call(functools.partial(gather_outputs, rows, plane, hidden), gr...  7.32 us

profile of v4, /device:TPU:0, one launch (start us, length us, event | category | flops | bytes accessed | tf_op | source)
XLA Modules:
  0.0 314.8 jit_solution(6076240099419375904)
XLA Ops:
  0.6 1.3 add_bitcast_fusion.refs_4_.refs_8_
  2.0 305.4 %layer.1 = (bf16[8,48,1024]{2,1,0:T(8,128)(2,1)}, bf16[8,48,768]{2,1,0:T(8,128)(2,1)}, bf16[8,48,1152]{2,1,0:T(8,128)(2,1)}, bf16[8,48,1152]{2,1,0:T(8,128)(2,1)...) custom-call(bf16[128,1536]{1,0:T(8,128)(2,1)} %refs_0_.1, ...), custom_call_target="tpu_custom_call" | custom-call | tf_op jit(solution)/shard_map/layer/pallas_call | solution.py:1041
  307.3 7.3 %outputs.1 = (bf16[128,1536]{1,0:T(8,128)(2,1)}, bf16[128,1536]{1,0:T(8,128)(2,1)}, f32[1,48]{1,0:T(1,128)}, f32[48,1536]{1,0:T(8,128)}, f32[1,48]{1,0:T(1,128)}...) custom-call(bf16[8,48,1024]{2,1,0:T(8,128)(2,1)} %get-tuple-element., ...), custom_call_target="tpu_custom_call" | custom-call | tf_op jit(solution)/shard_map/outputs/pallas_call | solution.py:1155

commit v5 on v4

--- a/solution.py
+++ b/solution.py
@@ -238,7 +238,7 @@
         o1, o2, o3, o4, o5, fo_out, bg_out, tg_out, bo_out,
         xs, xh, aux, ids, sa, wgs, wus, w1, w2, w3, w4, w5, g5,
         r1, r2, r3, r4, hn, gb, gt, up, act, pb, rb, rt,
-        zb, zr, dh, hs, dz, ob, qr, kr, vr, pr, dob, dq, cos, sin, msk, bias_in, ba, bp, bgp, bsum,
+        zb, zr, hs, dz, ob, qr, kr, vr, pr, dob, dq, cos, sin, msk, bias_in, ba, bp, bgp, bsum,
         lsem, a_s, a_r, p_s, p_r, r_s, r_r, o_s, o_r, t_s, t_r, d_s, d_r, b_s, b_r, e_s, e_r, credit, pair_credit, line_credit,
     ) = refs
     weights = (w1, w2, w3, w4, w5)
@@ -512,20 +512,19 @@
         target = (ynb, xnb, xnb, ynb, xnb, ynb)[s]
         return remote(ref.at[part, cols], land.at[slot(place), cols], r_s.at[k], r_r.at[k, place], target)
 
-    def rs_start(k, left_ref, right_ref):
+    def rs_step(k, left_ref, right_ref, h):
         ref, cols = parts[k][:2]
-
-        @pl.loop(0, 2)
+        for high in (1, 0):
+            at = pl.multiple_of(zf(high, h) * strip, 128)
+            ref[pl.ds(at, strip), cols] = dot_tn(left_ref[:, pl.ds(at, strip)], right_ref[:, cols]).astype(BF16)
+            for s in ((0, 3), (1, 2))[high]:
+                rs_copy(k, s, h).start()
+        pending["rs", k, "leave"] = lambda: left(ref.at[pl.ds(0, 24 * rows), cols], r_s.at[k])
+
+    def rs_start(k, left_ref, right_ref, steps=(0, 1)):
+        @pl.loop(steps[0], steps[-1] + 1)
         def both(i):
-            h = 1 - i
-            for high in (1, 0):
-                zz = zf(high, h)
-                at = pl.multiple_of(zz * strip, 128)
-                ref[pl.ds(at, strip), cols] = dot_tn(left_ref[:, pl.ds(at, strip)], right_ref[:, cols]).astype(BF16)
-                for s in ((0, 3), (1, 2))[high]:
-                    rs_copy(k, s, h).start()
-
-        pending["rs", k, "leave"] = lambda: left(ref.at[pl.ds(0, 24 * rows), cols], r_s.at[k])
+            rs_step(k, left_ref, right_ref, 1 - i)
 
     def rs_middle(k):
         ref, cols, land = parts[k][:3]
@@ -592,10 +591,12 @@
         got = rb[pl.ds(pl.multiple_of(j * block, block), block)].astype(F32)
         pb[part] = (pb[part].astype(F32) + got).astype(BF16)
 
-    def sum_loop(which, compute):
+    def sum_loop(which, compute, beside=None):
         @pl.loop(0, LINES)
         def chunk(i):
             j = LINES - 1 - i
+            if beside is not None:
+                beside(i)
             compute(chunk_of(zj(j)))
             pair_copy(which, j).start()
 
@@ -783,7 +784,12 @@
                 up[rows_here, cols] = lift.astype(BF16)
                 act[rows_here, cols] = (gate * jax.nn.sigmoid(gate) * lift).astype(BF16)
 
-    def feed_backward():
+    def feed_backward(together=False):
+        def beside(i):
+            @pl.when(lax.rem(i, 2) == 0)
+            def _():
+                rs_step(4, gb, act, 1 - lax.div(i, 2))
+
         def compute(rows_here):
             left = gb[rows_here]
             for n in range(0, shard, tile):
@@ -799,7 +805,7 @@
                 back = dot_nt(gt[rows_here], w3[part, :]) + dot_nt(up[rows_here], w4[part, :])
                 pb[rows_here, part] = back.astype(BF16)
 
-        sum_loop(0, compute)
+        sum_loop(0, compute, beside if together else None)
         signal(pair_credit, sib)
 
     def line_ready():
@@ -830,7 +836,8 @@
         live = jnp.where(column(aux[c][1:2]) >= 0.0, 1.0, 0.0)
         total = hs[...] + pb[tokens_of(z, c)].astype(F32)
         total = total + rb[pl.ds(0, block)].astype(F32) + rb[pl.ds(block, block)].astype(F32)
-        bo_out[...] = (live * total).astype(BF16)
+        xs[1 - c] = (live * total).astype(BF16)
+        begin_local(("bo",), local(1, xs.at[1 - c], bo_out))
 
     def landing_free():
         for target in (xnb, ynb):
@@ -850,7 +857,6 @@
             + scale_two * weighted
             - state * (scale_two * scale_two * scale_two) * spread
         )
-        dh[...] = grad
         dz[own_rows] = grad.astype(BF16)
         begin(("e", 3), e_copy(3, dz.at[own_rows], dz.at[own_rows]))
 
@@ -903,7 +909,10 @@
         values = xs[c].astype(F32)
         scale = lax.rsqrt(jnp.mean(values * values, axis=1, keepdims=True) + EPSILON)
         spread = jnp.mean(weighted * values, axis=1, keepdims=True)
-        tg_out[...] = (dh[...] + scale * weighted - values * (scale * scale * scale) * spread).astype(BF16)
+        grad = dz[own_rows].astype(F32) + scale * weighted - values * (scale * scale * scale) * spread
+        settle(("e", 1, "leave"))
+        xs[c] = grad.astype(BF16)
+        begin_local(("tg",), local(0, xs.at[c], tg_out))
 
     enter()
     exchange_inputs()
@@ -953,8 +962,7 @@
     tok_forward(1)
     ag_finish(4)
     tok_finish(1)
-    rs_start(4, gb, act)
-    feed_backward()
+    feed_backward(True)
     far_add(0, 2)
     rs_middle(4)
     ag_sent(2)
@@ -980,19 +988,19 @@
     project_back()
     ag_sent(0)
     rs_start(0, xh, dq)
+    rs_finish(3)
+    rs_middle(1)
     rs_start(5, xh, dq)
     rs_start(6, xh, dq)
-    rs_finish(3)
-    rs_middle(1)
+    rs_middle(0)
+    rs_finish(1)
     bias_back()
     token_gradient()
-    rs_middle(0)
-    rs_finish(1)
     rs_middle(5)
     rs_middle(6)
+    rs_finish(0)
     bias_last()
     block_result()
-    rs_finish(0)
     rs_finish(5)
     rs_finish(6)
     settle(*list(pending))
@@ -1009,7 +1017,6 @@
     vm = pltpu.VMEM
     group_tokens = GROUP * block
     any_space = pl.BlockSpec(memory_space=pl.ANY)
-    vmem_space = pl.BlockSpec(memory_space=pltpu.VMEM)
     out_shape = [jax.ShapeDtypeStruct((GROUP, rows, n), BF16) for n in columns]
     out_shape += [
         jax.ShapeDtypeStruct((3, block, width), BF16),
@@ -1027,7 +1034,7 @@
     scratch += [vm((group_tokens, width), BF16)] * 2 + [vm((group_tokens, shard), BF16)] * 3
     scratch += [vm((group_tokens, width), BF16), vm((LINES * block, width), BF16), vm((LINES, block, width), BF16)]
     scratch += [
-        vm((2, block, width), F32), vm((block, width), F32), vm((block, width), F32), vm((block, width), F32),
+        vm((2, block, width), F32), vm((block, width), F32), vm((block, width), F32),
         vm((2 * block, width), BF16),
         vm((2 * block, half), BF16), vm((2, heads * block, HD), BF16), vm((2, block, HD), BF16), vm((2, block, HD), BF16),
         vm((2, heads * block, block), F32), vm((2, heads * block, HD), BF16), vm((2 * block, inner), BF16),
@@ -1042,7 +1049,7 @@
         functools.partial(mega, rows, plane),
         out_shape=out_shape,
         in_specs=[any_space] * 12,
-        out_specs=[any_space] * 7 + [vmem_space] * 2,
+        out_specs=[any_space] * 9,
         scratch_shapes=scratch,
         compiler_params=pltpu.CompilerParams(
             collective_id=0, has_side_effects=True, vmem_limit_bytes=64 * 2**20 - 2**17
@@ -1137,7 +1144,7 @@
 
 
 def output_call(rows, plane, block, width, hidden, pieces, bias_sum, token_grad, block_output, aux, weights):
-    per = 2
+    per = 4
     shard = pieces[2].shape[2]
     key_width = weights[1].shape[1]
 

time: 316 us -> 308 us (0.975)
  Pallas kernels: 313 us -> 306 us
    pallas_call x1, Pallas kernels: 305 us -> 300 us  [kernel_call(): pl.pallas_call(functools.partial(mega, rows, plane), out_shape=out_shape,...]
where the time goes in v5:
time: 308 us
  Pallas kernels  306 us (99%)
    pallas_call x1, Pallas kernels, kernel_call(): pl.pallas_call(functools.partial(mega, rows, plane), out_shape=out_shape,...  300 us

profile of v5, /device:TPU:0, one launch (start us, length us, event | category | flops | bytes accessed | tf_op | source)
XLA Modules:
  0.0 307.9 jit_solution(11033418302357997377)
XLA Ops:
  0.6 1.3 add_bitcast_fusion.refs_4_.refs_8_
  2.0 299.8 %layer.1 = (bf16[8,48,1024]{2,1,0:T(8,128)(2,1)}, bf16[8,48,768]{2,1,0:T(8,128)(2,1)}, bf16[8,48,1152]{2,1,0:T(8,128)(2,1)}, bf16[8,48,1152]{2,1,0:T(8,128)(2,1)...) custom-call(bf16[128,1536]{1,0:T(8,128)(2,1)} %refs_0_.1, ...), custom_call_target="tpu_custom_call" | custom-call | tf_op jit(solution)/shard_map/layer/pallas_call | solution.py:1048
  301.8 5.9 %outputs.1 = (bf16[128,1536]{1,0:T(8,128)(2,1)}, bf16[128,1536]{1,0:T(8,128)(2,1)}, f32[1,48]{1,0:T(1,128)}, f32[48,1536]{1,0:T(8,128)}, f32[1,48]{1,0:T(1,128)}...) custom-call(bf16[8,48,1024]{2,1,0:T(8,128)(2,1)} %get-tuple-element., ...), custom_call_target="tpu_custom_call" | custom-call | tf_op jit(solution)/shard_map/outputs/pallas_call | solution.py:1162

commit v6 on v5

--- a/solution.py
+++ b/solution.py
@@ -415,7 +415,8 @@
             part, target = unit(zj(j), px), ynb
         else:
             part, target = unit(zj(j), py), xnb
-        index = s // 4 * 4 + j
+        low = isinstance(j, int) and j < 2
+        index = j if (s < 4 and low) or (4 <= s < 8 and not low) else 4
         return remote(weights[k].at[part], weights[k].at[part], p_s.at[k], p_r.at[k, index], target)
 
     def ag_unit(k, n):
@@ -434,8 +435,7 @@
             ag_copy(k, 8 + j, j).start()
 
     def ag_finish(k):
-        for s, j in ((0, 2), (0, 3), (4, 0), (4, 1), (8, 0), (8, 1), (10, 2), (10, 3)):
-            ag_copy(k, s, j).wait_recv()
+        landed(weights[k].at[pl.ds(0, 16 * rows)], p_r.at[k, 4])
 
     def ag_sent(k):
         settle(("ag", k, "leave"))
@@ -510,7 +510,7 @@
         part = unit(zz, (pd, pd, px, py, px, py)[s])
         place = (0, 2, 6, 8, 4, 10)[s] + h
         target = (ynb, xnb, xnb, ynb, xnb, ynb)[s]
-        return remote(ref.at[part, cols], land.at[slot(place), cols], r_s.at[k], r_r.at[k, place], target)
+        return remote(ref.at[part, cols], land.at[slot(place), cols], r_s.at[k], r_r.at[k, (0, 2, 6, 4, 4, 6)[s] + h], target)
 
     def rs_step(k, left_ref, right_ref, h):
         ref, cols = parts[k][:2]
@@ -548,8 +548,7 @@
         ref, cols, land, out = parts[k]
         for j in (3, 1, 2, 0):
             h, high = j % 2, j // 2
-            rs_copy(k, (4, 2)[high], h).wait_recv()
-            rs_copy(k, (3, 5)[high], h).wait_recv()
+            landed(land.at[pl.ds(0, 4 * rows), cols], r_r.at[k, 4 + j])
             part = unit(zj(j), p)
             got = land[slot(4 + j), cols].astype(F32) + land[slot(8 + j), cols].astype(F32)
             ref[part, cols] = (ref[part, cols].astype(F32) + got).astype(BF16)
@@ -971,10 +970,10 @@
     line_ready()
     rs_finish(4)
     landing_free()
+    hidden_gradient()
     ag_sent(3)
     landing_wait()
     rs_start(3, hn, up)
-    hidden_gradient()
     rs_middle(2)
     feed_output()
     far_add(1, 2)
@@ -1042,7 +1041,7 @@
         vm((2, 1, inner), F32), vm((GROUP, 1, inner), F32), vm((4, 1, inner), F32), vm((4, 1, inner), F32), vm((1, inner), F32),
     ]
     scratch += [dma((26,))]
-    scratch += [dma((7,)), dma((5, 4)), dma((5,)), dma((5, 12)), dma((7,)), dma((7, 12)), dma((7,)), dma((7,))]
+    scratch += [dma((7,)), dma((5, 4)), dma((5,)), dma((5, 5)), dma((7,)), dma((7, 8)), dma((7,)), dma((7,))]
     scratch += [dma((2, 2)), dma((2, 8)), dma((2, 2)), dma((2, 8)), dma((4,)), dma((4,)), dma((5,)), dma((5,))]
     scratch += [pltpu.SemaphoreType.REGULAR] * 3
     return pl.pallas_call(

time: 308 us -> 308 us (level)
  no operation moved by 1% of the time
where the time goes in v6:
time: 308 us; the launch traced here: 307 us
  Pallas kernels  305 us (99%)
    pallas_call x1, Pallas kernels, kernel_call(): pl.pallas_call(functools.partial(mega, rows, plane), out_shape=out_shape,...  299 us

profile of v6, /device:TPU:0, one launch (start us, length us, event | category | flops | bytes accessed | tf_op | source)
XLA Modules:
  0.0 307.3 jit_solution(8788477804033701828)
XLA Ops:
  0.6 1.3 add_bitcast_fusion.refs_4_.refs_8_
  2.0 299.2 %layer.1 = (bf16[8,48,1024]{2,1,0:T(8,128)(2,1)}, bf16[8,48,768]{2,1,0:T(8,128)(2,1)}, bf16[8,48,1152]{2,1,0:T(8,128)(2,1)}, bf16[8,48,1152]{2,1,0:T(8,128)(2,1)...) custom-call(bf16[128,1536]{1,0:T(8,128)(2,1)} %refs_0_.1, ...), custom_call_target="tpu_custom_call" | custom-call | tf_op jit(solution)/shard_map/layer/pallas_call | solution.py:1047
  301.2 5.9 %outputs.1 = (bf16[128,1536]{1,0:T(8,128)(2,1)}, bf16[128,1536]{1,0:T(8,128)(2,1)}, f32[1,48]{1,0:T(1,128)}, f32[48,1536]{1,0:T(8,128)}, f32[1,48]{1,0:T(1,128)}...) custom-call(bf16[8,48,1024]{2,1,0:T(8,128)(2,1)} %get-tuple-element., ...), custom_call_target="tpu_custom_call" | custom-call | tf_op jit(solution)/shard_map/outputs/pallas_call | solution.py:1161
